TPU v7x, 128 devices: a whole 4x4x4 slice. The times are simulated.
128 devices in a mesh: dp: 2 (over x_lo), context: 16 (over z, y), tensor: 4 (over x_hi, core).
Axes of the slice: x: 4 (x_hi: 2, x_lo: 2; x = x_hi * 2 + x_lo), y: 4, z: 4, core: 2. Of those that a mesh axis runs over, the one named last changes fastest.
Arguments:
- latents: bfloat16 [4, 1024, 1024], P('dp', 'context'), may hold values from -6 to 6
- cond: bfloat16 [4, 1024], P('dp'), may hold values from -6 to 6
- ada_weight: bfloat16 [1, 1024, 6144], P(None, 'tensor', ('dp', 'context')), may hold values from -0.1875 to 0.1875
- ada_bias: bfloat16 [1, 6144], replicated, may hold values from -3 to 3
- query_key_value_weight: bfloat16 [1, 1024, 3, 1024], P(None, ('dp', 'context'), None, 'tensor'), may hold values from -0.1875 to 0.1875
- qv_bias: bfloat16 [1, 2, 1024], P(None, None, 'tensor'), may hold values from -3 to 3
- attention_output_weight: bfloat16 [1, 1024, 1024], P(None, 'tensor', ('dp', 'context')), may hold values from -3 to 3
- attention_output_bias: bfloat16 [1, 1024], replicated, may hold values from -3 to 3
- first_dense_weight: bfloat16 [1, 1024, 4096], P(None, ('dp', 'context'), 'tensor'), may hold values from -0.1875 to 0.1875
- first_dense_bias: bfloat16 [1, 4096], P(None, 'tensor'), may hold values from -3 to 3
- second_dense_weight: bfloat16 [1, 4096, 1024], P(None, 'tensor', ('dp', 'context')), may hold values from -0.09375 to 0.09375
- second_dense_bias: bfloat16 [1, 1024], replicated, may hold values from -3 to 3
- cotangent: bfloat16 [4, 1024, 1024], P('dp', 'context'), may hold values from -6 to 6
Outputs:
- block_out: bfloat16 [4, 1024, 1024], P('dp', 'context')
- latents_grad: float32 [4, 1024, 1024], P('dp', 'context')
- cond_grad: float32 [4, 1024], P('dp', 'tensor')
- ada_weight_grad: float32 [1, 1024, 6144], P(None, 'tensor', ('dp', 'context'))
- ada_bias_grad: float32 [1, 6144], replicated
- qkv_weight_grad: float32 [1, 1024, 3, 1024], P(None, ('dp', 'context'), None, 'tensor')
- qv_bias_grad: float32 [1, 2, 1024], P(None, None, 'tensor')
- out_weight_grad: float32 [1, 1024, 1024], P(None, 'tensor', ('dp', 'context'))
- out_bias_grad: float32 [1, 1024], replicated
- fc1_weight_grad: float32 [1, 1024, 4096], P(None, ('dp', 'context'), 'tensor')
- fc1_bias_grad: float32 [1, 4096], P(None, 'tensor')
- fc2_weight_grad: float32 [1, 4096, 1024], P(None, 'tensor', ('dp', 'context'))
- fc2_bias_grad: float32 [1, 1024], replicated
All inputs are finite; a program needn't handle non-finite values.
Results may differ from a plain program's by a relative error of at most 0.009.
The roundings to bfloat16 on the way count: a program that leaves them out, or rounds other values in their place, can miss the bound.
Values may be sent and summed in bfloat16 or wider, within the bound.
A program may use at most 128 MiB of HBM per device.

v0:
```python
import math

import jax
import jax.numpy as jnp
from jax import lax
from jax.sharding import PartitionSpec as P

HEAD_DIM = 64


EPSILON = 1e-06


def normalize(values):
    center = values - jnp.mean(values, axis=-1, keepdims=True)
    inverse = lax.rsqrt(jnp.mean(center * center, axis=-1, keepdims=True) + EPSILON)
    return (center * inverse, inverse)


def norm_back(grad_hat, normed, inverse):
    first = jnp.mean(grad_hat, axis=-1, keepdims=True)
    second = jnp.mean(grad_hat * normed, axis=-1, keepdims=True)
    return inverse * (grad_hat - first - normed * second)


def gelu_tanh(values):
    return jax.nn.gelu(values, approximate=True)


def tensor_total(values):
    return lax.psum(values, "tensor")


def input_total(values):
    return lax.psum(values, "tensor")


def fetch_layer(pieces):
    return (
        lax.all_gather(pieces[0], ("dp", "context"), axis=1, tiled=True),
        lax.all_gather(pieces[1], ("dp", "context"), axis=0, tiled=True),
        lax.all_gather(pieces[2], ("dp", "context"), axis=1, tiled=True),
        lax.all_gather(pieces[3], ("dp", "context"), axis=0, tiled=True),
        lax.all_gather(pieces[4], ("dp", "context"), axis=1, tiled=True),
    )


def fetch_layer_back(pieces):
    return (
        lax.all_gather(pieces[0], ("dp", "context"), axis=1, tiled=True),
        lax.all_gather(pieces[1], ("dp", "context"), axis=0, tiled=True),
        lax.all_gather(pieces[2], ("dp", "context"), axis=1, tiled=True),
        lax.all_gather(pieces[3], ("dp", "context"), axis=0, tiled=True),
        lax.all_gather(pieces[4], ("dp", "context"), axis=1, tiled=True),
    )


def on_device(
    latents,
    cond,
    ada_weight,
    ada_bias,
    query_key_value_weight,
    qv_bias,
    attention_output_weight,
    attention_output_bias,
    first_dense_weight,
    first_dense_bias,
    second_dense_weight,
    second_dense_bias,
    cotangent,
):
    single_float = jnp.float32
    bf16 = jnp.bfloat16
    highest = lax.Precision.HIGHEST
    seqs, local_len, width = latents.shape
    layers = ada_weight.shape[0]
    part_width = query_key_value_weight.shape[3]
    head_dim = HEAD_DIM
    heads_here = part_width // head_dim
    scale = 1.0 / math.sqrt(head_dim)
    cond_width = ada_weight.shape[1]
    cond_slice = lax.dynamic_slice_in_dim(
        cond.astype(single_float), lax.axis_index("tensor") * cond_width, cond_width, 1
    )
    cond_part = jax.nn.silu(cond_slice).astype(bf16)
    stream = latents.astype(single_float)
    layer_index = 0
    weights = fetch_layer(
        (
            ada_weight[layer_index],
            query_key_value_weight[layer_index],
            attention_output_weight[layer_index],
            first_dense_weight[layer_index],
            second_dense_weight[layer_index],
        )
    )
    w_ada, query_key_value_matrix, output_weight, up_weight, down_weight = weights
    mod_part = jnp.dot(cond_part, w_ada, preferred_element_type=single_float)
    modulation = lax.psum(mod_part, "tensor") + ada_bias[layer_index].astype(single_float)
    modulation = modulation.reshape(seqs, 6, 1, width)
    normed, inverse = normalize(stream)
    hidden_state = (normed * (1.0 + modulation[:, 1]) + modulation[:, 0]).astype(bf16)
    mixed_tokens = jnp.einsum(
        "nvi,itw->nvtw", hidden_state, query_key_value_matrix, preferred_element_type=single_float
    )
    biases = qv_bias[layer_index].astype(single_float)
    query = (mixed_tokens[:, :, 0] + biases[0]).astype(bf16)
    keys = mixed_tokens[:, :, 1].astype(bf16)
    values = (mixed_tokens[:, :, 2] + biases[1]).astype(bf16)
    keys_all = lax.all_gather(keys, "context", axis=1, tiled=True)
    values_all = lax.all_gather(values, "context", axis=1, tiled=True)
    full_len = keys_all.shape[1]
    query_heads = query.reshape(seqs, local_len, heads_here, head_dim)
    key_heads = keys_all.reshape(seqs, full_len, heads_here, head_dim)
    value_heads = values_all.reshape(seqs, full_len, heads_here, head_dim)
    scores = (
        jnp.einsum("sqhd,skhd->shqk", query_heads, key_heads, preferred_element_type=single_float)
        * scale
    )
    top = jnp.max(scores, axis=-1, keepdims=True)
    expo = jnp.exp(scores - top)
    total = jnp.sum(expo, axis=-1, keepdims=True)
    log_total = top + jnp.log(total)
    prob = (expo / total).astype(bf16)
    attended_tokens = jnp.einsum(
        "shqk,skhd->sqhd", prob, value_heads, preferred_element_type=single_float
    )
    attended_tokens = attended_tokens.astype(bf16).reshape(seqs, local_len, part_width)
    branch_output = tensor_total(
        jnp.einsum(
            "pub,bo->puo", attended_tokens, output_weight, preferred_element_type=single_float
        )
    )
    branch_output = branch_output + attention_output_bias[layer_index].astype(single_float)
    middle = stream + modulation[:, 2] * branch_output
    normed_two, inverse_two = normalize(middle)
    second_hidden_state = (normed_two * (1.0 + modulation[:, 4]) + modulation[:, 3]).astype(bf16)
    before_block = jnp.einsum(
        "pxo,og->pxg", second_hidden_state, up_weight, preferred_element_type=single_float
    )
    before_block = before_block + first_dense_bias[layer_index].astype(single_float)
    activated_hidden = gelu_tanh(before_block).astype(bf16)
    feed_forward = tensor_total(
        jnp.einsum(
            "pub,bo->puo", activated_hidden, down_weight, preferred_element_type=single_float
        )
    )
    feed_forward = feed_forward + second_dense_bias[layer_index].astype(single_float)
    saved = [
        (
            modulation,
            normed,
            inverse,
            hidden_state,
            query_heads,
            key_heads,
            value_heads,
            log_total,
            attended_tokens,
            branch_output,
            normed_two,
            inverse_two,
            second_hidden_state,
            before_block,
            activated_hidden,
            feed_forward,
        )
    ]
    stream = middle + modulation[:, 5] * feed_forward
    block_out = stream.astype(bf16)
    grad = cotangent.astype(single_float)
    cond_grad_part = jnp.zeros((seqs, cond_width), single_float)
    weight_lists = [[None] * layers for item in range(5)]
    bias_lists = [[None] * layers for item in range(5)]
    for layer_index in reversed(range(layers)):
        (
            modulation,
            normed,
            inverse,
            hidden_state,
            query_heads,
            key_heads,
            value_heads,
            log_total,
            attended_tokens,
            branch_output,
            normed_two,
            inverse_two,
            second_hidden_state,
            before_block,
            activated_hidden,
            feed_forward,
        ) = saved[layer_index]
        weights = fetch_layer_back(
            (
                ada_weight[layer_index],
                query_key_value_weight[layer_index],
                attention_output_weight[layer_index],
                first_dense_weight[layer_index],
                second_dense_weight[layer_index],
            )
        )
        w_ada, query_key_value_matrix, output_weight, up_weight, down_weight = weights
        full_len = key_heads.shape[1]
        feed_gradient = (grad * modulation[:, 5]).astype(bf16)
        gate_two = jnp.sum(grad * feed_forward, axis=1)
        down_bias_grad = jnp.sum(feed_gradient.astype(single_float), axis=(0, 1))
        down_gradient = jnp.einsum(
            "ipk,ipz->kz", activated_hidden, feed_gradient, preferred_element_type=single_float
        )
        activation_gradient = jnp.einsum(
            "cjy,hy->cjh", feed_gradient, down_weight, preferred_element_type=single_float
        )
        unused, gelu_pull = jax.vjp(gelu_tanh, before_block)
        before_gradient = gelu_pull(activation_gradient)[0].astype(bf16)
        up_bias_grad = jnp.sum(before_gradient.astype(single_float), axis=(0, 1))
        up_gradient = jnp.einsum(
            "uek,ueg->kg", second_hidden_state, before_gradient, preferred_element_type=single_float
        )
        d_hidden_two = input_total(
            jnp.einsum(
                "zjr,ur->zju", before_gradient, up_weight, preferred_element_type=single_float
            )
        )
        shift_two = jnp.sum(d_hidden_two, axis=1)
        scale_two = jnp.sum(d_hidden_two * normed_two, axis=1)
        d_middle = grad + norm_back(
            d_hidden_two * (1.0 + modulation[:, 4]), normed_two, inverse_two
        )
        gate_one = jnp.sum(d_middle * branch_output, axis=1)
        branch_gradient = (d_middle * modulation[:, 2]).astype(bf16)
        out_bias_grad = jnp.sum(branch_gradient.astype(single_float), axis=(0, 1))
        output_gradient = jnp.einsum(
            "ipk,ipz->kz", attended_tokens, branch_gradient, preferred_element_type=single_float
        )
        attended_gradient = jnp.einsum(
            "cjy,hy->cjh", branch_gradient, output_weight, preferred_element_type=single_float
        )
        attended_gradient = attended_gradient.astype(bf16).reshape(
            seqs, local_len, heads_here, head_dim
        )
        scores = (
            jnp.einsum(
                "sqhd,skhd->shqk", query_heads, key_heads, preferred_element_type=single_float
            )
            * scale
        )
        prob_full = jnp.exp(scores - log_total)
        d_prob = jnp.einsum(
            "sqhd,skhd->shqk", attended_gradient, value_heads, preferred_element_type=single_float
        )
        row_sums = jnp.sum(prob_full * d_prob, axis=-1, keepdims=True)
        d_scores = (prob_full * (d_prob - row_sums)).astype(bf16)
        d_query = (
            jnp.einsum("shqk,skhd->sqhd", d_scores, key_heads, preferred_element_type=single_float)
            * scale
        )
        d_query = d_query.astype(bf16).reshape(seqs, local_len, part_width)
        prob = prob_full.astype(bf16)
        d_values_part = jnp.einsum(
            "shqk,sqhd->skhd", prob, attended_gradient, preferred_element_type=single_float
        )
        d_keys_part = (
            jnp.einsum(
                "shqk,sqhd->skhd", d_scores, query_heads, preferred_element_type=single_float
            )
            * scale
        )
        d_keys, d_values = (
            lax.psum_scatter(
                d_keys_part.reshape(seqs, full_len, part_width),
                "context",
                scatter_dimension=1,
                tiled=True,
            ),
            lax.psum_scatter(
                d_values_part.reshape(seqs, full_len, part_width),
                "context",
                scatter_dimension=1,
                tiled=True,
            ),
        )
        d_keys = d_keys.astype(bf16)
        d_values = d_values.astype(bf16)
        qv_grad = jnp.stack(
            [
                jnp.sum(d_query.astype(single_float), axis=(0, 1)),
                jnp.sum(d_values.astype(single_float), axis=(0, 1)),
            ]
        )
        mixed_gradient = jnp.stack([d_query, d_keys, d_values], axis=2)
        mixed_tokens_gradient = jnp.einsum(
            "tmi,tmyq->iyq", hidden_state, mixed_gradient, preferred_element_type=single_float
        )
        d_hidden = input_total(
            jnp.einsum(
                "tweu,ieu->twi",
                mixed_gradient,
                query_key_value_matrix,
                preferred_element_type=single_float,
            )
        )
        shift_one = jnp.sum(d_hidden, axis=1)
        scale_one = jnp.sum(d_hidden * normed, axis=1)
        grad = d_middle + norm_back(d_hidden * (1.0 + modulation[:, 1]), normed, inverse)
        d_mod = jnp.stack([shift_one, scale_one, gate_one, shift_two, scale_two, gate_two], axis=1)
        d_mod = d_mod.reshape(seqs, 6 * width)
        ada_bias_grad = jnp.sum(d_mod, axis=0)
        ada_grad = jnp.dot(cond_part.astype(single_float).T, d_mod, precision=highest)
        cond_grad_part = jnp.dot(d_mod, w_ada.astype(single_float).T, precision=highest)
        shards = (
            lax.psum_scatter(ada_grad, ("dp", "context"), scatter_dimension=1, tiled=True),
            lax.psum_scatter(
                mixed_tokens_gradient, ("dp", "context"), scatter_dimension=0, tiled=True
            ),
            lax.psum_scatter(output_gradient, ("dp", "context"), scatter_dimension=1, tiled=True),
            lax.psum_scatter(up_gradient, ("dp", "context"), scatter_dimension=0, tiled=True),
            lax.psum_scatter(down_gradient, ("dp", "context"), scatter_dimension=1, tiled=True),
        )
        for slot in range(5):
            weight_lists[slot][layer_index] = shards[slot]
        bias_lists[0][layer_index] = ada_bias_grad
        bias_lists[1][layer_index] = qv_grad
        bias_lists[2][layer_index] = out_bias_grad
        bias_lists[3][layer_index] = up_bias_grad
        bias_lists[4][layer_index] = down_bias_grad
    bias_totals = lax.psum(
        tuple((jnp.stack(bias_lists[slot]) for slot in range(5))), ("dp", "context")
    )
    cond_total = lax.psum(cond_grad_part, "context")
    sigmoid = jax.nn.sigmoid(cond_slice)
    cond_grad = cond_total * sigmoid * (1.0 + cond_slice * (1.0 - sigmoid))
    stacked = [jnp.stack(weight_lists[slot]) for slot in range(5)]
    return (
        block_out,
        grad,
        cond_grad,
        stacked[0],
        bias_totals[0],
        stacked[1],
        bias_totals[1],
        stacked[2],
        bias_totals[2],
        stacked[3],
        bias_totals[3],
        stacked[4],
        bias_totals[4],
    )


def solution(mesh):
    return jax.shard_map(
        on_device,
        mesh=mesh,
        in_specs=(
            P("dp", "context", None),
            P("dp", None),
            P(None, "tensor", ("dp", "context")),
            P(),
            P(None, ("dp", "context"), None, "tensor"),
            P(None, None, "tensor"),
            P(None, "tensor", ("dp", "context")),
            P(),
            P(None, ("dp", "context"), "tensor"),
            P(None, "tensor"),
            P(None, "tensor", ("dp", "context")),
            P(),
            P("dp", "context", None),
        ),
        out_specs=(
            P("dp", "context", None),
            P("dp", "context", None),
            P("dp", "tensor"),
            P(None, "tensor", ("dp", "context")),
            P(),
            P(None, ("dp", "context"), None, "tensor"),
            P(None, None, "tensor"),
            P(None, "tensor", ("dp", "context")),
            P(),
            P(None, ("dp", "context"), "tensor"),
            P(None, "tensor"),
            P(None, "tensor", ("dp", "context")),
            P(),
        ),
        check_vma=False,
    )
```

profile of v0, /device:TPU:0, one launch (start us, length us, event | category | flops | bytes accessed | tf_op | source)
XLA Modules:
  0.0 1873.2 jit_solution(5427272009000141617)
XLA Ops:
  7.2 0.7 all-gather.15.cloned.1.call-update
  8.0 0.7 all-gather.17.cloned.1.call-update
  8.7 0.8 add.232
  9.5 1.1 convert_reduce_fusion
  10.6 1.2 fusion.43
  11.8 155.5 %all-gather.15.cloned.1.call-done = bf16[1,256,6144]{1,2,0:T(8,128)(2,1)} async-done(((bf16[1,256,192]{1,2,0:T(8,128)(2,1)}), bf16[1,256,6144]{1,2,0:T(8,128)(2,1)}) %all-gather.15.cloned.1.call-update) | async-done | bytes 3145744 | tf_op jit(solution)/shard_map/all_gather | solution.py:40
  167.3 2.8 fusion.2
  170.1 13.7 psum.77
  184.0 138.1 %all-gather.17.cloned.1.call-done = bf16[1,1024,3,256]{3,1,2,0:T(8,128)(2,1)} async-done(((bf16[1,32,3,256]{3,1,2,0:T(8,128)(2,1)}), bf16[1,1024,3,256]{3,1,2,0:T(8,128)(2,1)}) %all-gather.17.cloned.1.call-update) | async-done | bytes 1572880 | tf_op jit(solution)/shard_map/all_gather | solution.py:41
  322.1 1.8 fusion.15
  323.9 0.6 slice.71
  324.7 0.6 fusion.62
  325.5 83.9 %all-gather.3 = bf16[1,256,1024]{1,2,0:T(8,128)(2,1)S(1)} all-gather(bf16[1,256,32]{1,2,0:T(8,128)(2,1)S(1)} %copy-done.44), channel_id=5, replica_groups=mesh['dp'=2,'context'=16,'tensor'=4] {'dp','context'}, dimensions={2}, use_global_device_ids=true | all-gather | bytes 540672 | tf_op jit(solution)/shard_map/all_gather | solution.py:42
  409.6 2.5 copy.73
  412.0 1.9 multiply_reduce_fusion.1
  414.4 2.3 copy.71
  416.7 2.0 convolution_convert_fusion
  418.7 1.1 fusion.54
  420.5 0.7 all-gather.23.cloned.1.call-update
  421.4 38.0 %all-reduce.6.cloned.1.call-done = f32[2,64,1024]{2,1,0:T(8,128)} async-done(((f32[2,64,1024]{2,1,0:T(8,128)}), f32[2,64,1024]{2,1,0:T(8,128)}) %all-reduce.6.cloned.1.call-update) | async-done | bytes 524304 | tf_op jit(solution)/shard_map/psum | solution.py:31
  459.4 1.2 fusion.79
  460.9 152.9 %all-gather.21.cloned.1.call-done = bf16[1,1024,1024]{2,1,0:T(8,128)(2,1)} async-done(((bf16[1,32,1024]{2,1,0:T(8,128)(2,1)}), bf16[1,1024,1024]{2,1,0:T(8,128)(2,1)}) %all-gather.21.cloned.1.call-update) | async-done | bytes 2097168 | tf_op jit(solution)/shard_map/all_gather | solution.py:43
  613.8 2.1 fusion.21
  615.9 152.9 %all-gather.23.cloned.1.call-done = bf16[1,1024,1024]{1,2,0:T(8,128)(2,1)} async-done(((bf16[1,1024,32]{1,2,0:T(8,128)(2,1)}), bf16[1,1024,1024]{1,2,0:T(8,128)(2,1)}) %all-gather.23.cloned.1.call-update) | async-done | bytes 2097168 | tf_op jit(solution)/shard_map/all_gather | solution.py:44
  768.8 3.1 convert_reduce_fusion.2
  771.9 0.7 copy-done.17
  772.6 1.6 fusion.8
  774.9 41.6 %all-reduce.8.cloned.1.call-done = f32[2,64,1024]{2,1,0:T(8,128)} async-done(((f32[2,64,1024]{2,1,0:T(8,128)}), f32[2,64,1024]{2,1,0:T(8,128)}) %all-reduce.8.cloned.1.call-update) | async-done | bytes 524304 | tf_op jit(solution)/shard_map/psum | solution.py:35
  816.5 2.0 multiply_reduce_fusion.2
  818.5 2.8 convert_reduce_fusion.3
  821.3 0.7 copy-done.12
  822.0 0.9 convolution_convert_fusion.1
  822.8 1.0 copy.99
  823.8 2.6 fusion.26
  826.4 2.9 copy.82
  829.3 2.0 multiply_reduce_fusion
  831.9 1.0 copy-done.6
  833.4 1.9 copy.80
  835.4 1.5 copy-done.14
  836.9 1.6 fusion.6
  839.2 64.3 %reduce-scatter.10.cloned.1.call-done = f32[2,64,256]{2,1,0:T(8,128)} async-done(((f32[2,1024,256]{2,1,0:T(8,128)}), f32[2,64,256]{2,1,0:T(8,128)}) %reduce-scatter.10.cloned.1.call-update) | async-done | bytes 131088 | tf_op jit(solution)/shard_map/reduce_scatter | solution.py:277
  903.5 0.9 convert_reduce_fusion.5
  904.4 76.1 %reduce-scatter.8.cloned.1.call-done = f32[2,64,256]{2,1,0:T(8,128)} async-done(((f32[2,1024,256]{2,1,0:T(8,128)}), f32[2,64,256]{2,1,0:T(8,128)}) %reduce-scatter.8.cloned.1.call-update) | async-done | bytes 131088 | tf_op jit(solution)/shard_map/reduce_scatter | solution.py:271
  980.6 0.9 convert_bitcast_fusion
  981.5 1.5 fusion.18
  983.2 1.3 convolution_bitcast_fusion.3
  984.7 2.8 convolution_bitcast_fusion.1
  987.6 0.9 copy-done.11
  988.5 2.8 convolution_bitcast_fusion
  991.4 0.6 copy-done.23
  992.0 2.3 convolution_bitcast_fusion.2
  995.0 33.0 %all-reduce.10.cloned.1.call-done = (f32[2,64,1024]{2,1,0:T(8,128)}, f32[2,64,1024]{2,1,0:T(8,128)}) async-done(((f32[2,64,1024]{2,1,0:T(8,128)}, f32[2,64,1024]{2,1,0:T(8,128)}), (f32[2,64,1024]{2,1,0:T(8,128)}, f32[2,64,1024]{2,1,0:T(8,128)})) %all-reduce.10.cloned.1.call-update) | async-done | bytes 1048592 | tf_op jit(solution)/shard_map/psum | solution.py:31
  1028.0 1.4 fusion.42
  1029.5 2.1 multiply_reduce_fusion.3
  1031.7 0.9 convert_reduce_fusion.1
  1032.6 4.6 fusion.76
  1037.4 1.7 copy-done.1
  1039.1 1.3 fusion
  1040.4 40.6 %psum.82 = f32[2,256]{1,0:T(2,128)S(1)} all-reduce(f32[2,256]{1,0:T(2,128)S(1)} %fusion), channel_id=1, replica_groups=mesh['dp'=2,'context'=16,'tensor'=4] {'context'}, use_global_device_ids=true, to_apply=%region_24.25 | all-reduce | flops 512 | bytes 4096 | tf_op jit(solution)/shard_map/psum | solution.py:331
  1081.0 152.2 %all-reduce = (f32[1,6144]{1,0:T(1,128)}, f32[1,2,256]{2,1,0:T(2,128)}, f32[1,1024]{1,0:T(1,128)}, f32[1,1024]{1,0:T(1,128)}, f32[1,1024]{1,0:T(1,128)}) all-reduce(f32[1,6144]{1,0:T(1,128)S(1)} %bitcast.179, f32[1,2,256]{2,1,0:T(2,128)S(1)} %maximum_bitcast_fusion, ...), channel_id=1, replica_groups=mesh['dp'=2,'context'=16,'tensor'=4] {'dp','context'}, use_global_device_ids=true, to_apply=%region_27.28 | all-reduce | flops 9728 | bytes 77824 | tf_op jit(solution)/shard_map/psum | solution.py:328
  1233.8 125.9 %reduce-scatter.18.cloned.1.call-done = f32[32,1024]{1,0:T(8,128)} async-done(((f32[1024,1024]{1,0:T(8,128)}), f32[32,1024]{1,0:T(8,128)}) %reduce-scatter.18.cloned.1.call-update) | async-done | bytes 131088 | tf_op jit(solution)/shard_map/reduce_scatter | solution.py:318
  1359.7 168.0 %reduce-scatter.20.cloned.1.call-done = f32[1024,32]{0,1:T(8,128)} async-done(((f32[1024,1024]{0,1:T(8,128)}), f32[1024,32]{0,1:T(8,128)}) %reduce-scatter.20.cloned.1.call-update) | async-done | bytes 131088 | tf_op jit(solution)/shard_map/reduce_scatter | solution.py:319
  1527.6 165.1 %reduce-scatter.14.cloned.1.call-done = f32[32,3,256]{2,0,1:T(8,128)} async-done(((f32[1024,3,256]{2,0,1:T(8,128)}), f32[32,3,256]{2,0,1:T(8,128)}) %reduce-scatter.14.cloned.1.call-update) | async-done | bytes 98320 | tf_op jit(solution)/shard_map/reduce_scatter | solution.py:314
  1692.8 173.9 %reduce-scatter.12.cloned.1.call-done = f32[256,192]{0,1:T(8,128)} async-done(((f32[256,6144]{0,1:T(8,128)}), f32[256,192]{0,1:T(8,128)}) %reduce-scatter.12.cloned.1.call-update) | async-done | bytes 196624 | tf_op jit(solution)/shard_map/reduce_scatter | solution.py:313
  (171 shorter events, 6.7 us)
Async XLA Ops:
  7.2 160.1 %all-gather.15.cloned.1.call-start = ((), (), s32[]{:S(2)}) async-start(), calls=%async_computation.17 | async-start | bytes 3244032 | tf_op jit(solution)/shard_map/all_gather | solution.py:40
  7.9 314.1 %all-gather.17.cloned.1.call-start = ((), (), s32[]{:S(2)}) async-start(), calls=%async_computation.18 | async-start | bytes 1622016 | tf_op jit(solution)/shard_map/all_gather | solution.py:41
  8.7 400.9 %all-gather.19.cloned.1.call-start = ((), (), s32[]{:S(2)}) async-start(), calls=%async_computation.19 | async-start | bytes 1114112 | tf_op jit(solution)/shard_map/all_gather | solution.py:111
  9.5 312.6 %copy-start = (bf16[2,64,1024]{2,1,0:T(8,128)(2,1)S(1)}, bf16[2,64,1024]{2,1,0:T(8,128)(2,1)}, u32[]{:S(2)}) copy-start(bf16[2,64,1024]{2,1,0:T(8,128)(2,1)} %param.13) | copy-start | bytes 786436
  10.6 313.3 %copy-start.29 = (f32[2,64]{1,0:T(2,128)}, f32[2,64]{1,0:T(2,128)S(1)}, u32[]{:S(2)}) copy-start(f32[2,64]{1,0:T(2,128)S(1)} %broadcast_multiply_fusion.5) | copy-start | bytes 1540
  11.8 312.1 %copy-start.35 = (f32[2,64]{1,0:T(2,128)}, f32[2,64]{1,0:T(2,128)S(1)}, u32[]{:S(2)}) copy-start(f32[2,64]{1,0:T(2,128)S(1)} %add_rsqrt_fusion.1) | copy-start | bytes 1540
  170.1 154.5 %copy-start.46 = (bf16[1,2,256]{2,1,0:T(2,128)(2,1)S(1)}, bf16[1,2,256]{2,1,0:T(2,128)(2,1)}, u32[]{:S(2)}) copy-start(bf16[1,2,256]{2,1,0:T(2,128)(2,1)} %param.18) | copy-start | bytes 3076
  170.1 155.4 %copy-start.44 = (bf16[1,256,32]{1,2,0:T(8,128)(2,1)S(1)}, bf16[1,256,32]{1,2,0:T(8,128)(2,1)}, u32[]{:S(2)}) copy-start(bf16[1,256,32]{1,2,0:T(8,128)(2,1)} %param.19) | copy-start | bytes 49156
  184.0 141.4 %copy-start.22 = (f32[2,1,1,1024]{3,0,1,2:T(2,128)}, f32[2,1,1,1024]{3,0,1,2:T(2,128)S(1)}, u32[]{:S(2)}) copy-start(f32[2,1,1,1024]{3,0,1,2:T(2,128)S(1)} %copy.108) | copy-start | bytes 24580
  324.6 89.9 %all-gather.13.cloned.1.call-start = ((), (), s32[]{:S(2)}) async-start(), calls=%async_computation.7 | async-start | bytes 1114112 | tf_op jit(solution)/shard_map/all_gather | solution.py:112
  325.3 134.1 %all-reduce.6.cloned.1.call-start = ((), (), s32[]{:S(2)}) async-start(), calls=%async_computation.8 | async-start | bytes 1048576 | tf_op jit(solution)/shard_map/psum | solution.py:31
  325.5 88.4 %copy-start.41 = (f32[4,64]{1,0:T(4,128)}, f32[4,64]{1,0:T(4,128)S(1)}, u32[]{:S(2)}) copy-start(f32[4,64]{1,0:T(4,128)S(1)} %add.209) | copy-start | bytes 3076
  409.4 9.4 copy-start.4
  409.5 4.4 copy-start.9
  416.7 4.5 copy-start.47
  416.7 4.6 copy-start.48
  418.7 195.1 %copy-start.20 = (bf16[2,4,64,64]{3,2,1,0:T(8,128)(2,1)}, bf16[2,4,64,64]{3,2,1,0:T(8,128)(2,1)S(1)}, u32[]{:S(2)}) copy-start(bf16[2,4,64,64]{3,2,1,0:T(8,128)(2,1)S(1)} %convolution_convert_fusion) | copy-start | bytes 196612
  419.9 193.9 %all-gather.21.cloned.1.call-start = ((), (), s32[]{:S(2)}) async-start(), calls=%async_computation.20 | async-start | bytes 2162688 | tf_op jit(solution)/shard_map/all_gather | solution.py:43
  420.4 348.3 %all-gather.23.cloned.1.call-start = ((), (), s32[]{:S(2)}) async-start(), calls=%async_computation.21 | async-start | bytes 2162688 | tf_op jit(solution)/shard_map/all_gather | solution.py:44
  421.2 395.3 %all-reduce.8.cloned.1.call-start = ((), (), s32[]{:S(2)}) async-start(), calls=%async_computation.9 | async-start | bytes 1048576 | tf_op jit(solution)/shard_map/psum | solution.py:35
  421.3 194.6 %copy-start.31 = (f32[1,1024]{1,0:T(1,128)}, f32[1,1024]{1,0:T(1,128)S(1)}, u32[]{:S(2)}) copy-start(f32[1,1024]{1,0:T(1,128)S(1)} %convert_element_type.164) | copy-start | bytes 12292
  421.3 347.4 %copy-start.24 = (f32[2,1,1,1024]{3,0,1,2:T(2,128)}, f32[2,1,1,1024]{3,0,1,2:T(2,128)S(1)}, u32[]{:S(2)}) copy-start(f32[2,1,1,1024]{3,0,1,2:T(2,128)S(1)} %copy.107) | copy-start | bytes 24580
  421.4 194.5 %copy-start.26 = (f32[2,1024]{1,0:T(2,128)}, f32[2,1024]{1,0:T(2,128)S(1)}, u32[]{:S(2)}) copy-start(f32[2,1024]{1,0:T(2,128)S(1)} %get-tuple-element.54) | copy-start | bytes 24580
  460.6 357.8 %copy-start.33 = (f32[2,64]{1,0:T(2,128)}, f32[2,64]{1,0:T(2,128)S(1)}, u32[]{:S(2)}) copy-start(f32[2,64]{1,0:T(2,128)S(1)} %broadcast_multiply_fusion.4) | copy-start | bytes 1540
  460.9 357.6 %copy-start.39 = (f32[2,64]{1,0:T(2,128)}, f32[2,64]{1,0:T(2,128)S(1)}, u32[]{:S(2)}) copy-start(f32[2,64]{1,0:T(2,128)S(1)} %add_rsqrt_fusion) | copy-start | bytes 1540
  768.8 3.8 copy-start.2
  771.9 0.7 copy-start.17
  774.2 129.3 %reduce-scatter.10.cloned.1.call-start = ((), (), s32[]{:S(2)}) async-start(), calls=%async_computation.11 | async-start | bytes 2228224 | tf_op jit(solution)/shard_map/reduce_scatter | solution.py:277
  816.5 5.5 copy-start.5
  821.2 0.7 copy-start.12
  829.3 151.3 %reduce-scatter.8.cloned.1.call-start = ((), (), s32[]{:S(2)}) async-start(), calls=%async_computation.10 | async-start | bytes 2228224 | tf_op jit(solution)/shard_map/reduce_scatter | solution.py:271
  829.3 2.0 copy-start.28
  831.3 1.6 copy-start.10
  831.4 1.6 copy-start.42
  831.9 1.0 copy-start.6
  835.3 1.6 copy-start.14
  835.3 192.7 %all-reduce.10.cloned.1.call-start = ((), (), s32[]{:S(2)}) async-start(), calls=%async_computation.22 | async-start | bytes 2097152 | tf_op jit(solution)/shard_map/psum | solution.py:31
  836.9 1.6 copy-start.7
  836.9 1.6 copy-start.8
  838.5 143.0 %copy-start.3 = (bf16[1,1024,3,256]{3,1,2,0:T(8,128)(2,1)S(1)}, bf16[1,1024,3,256]{3,1,2,0:T(8,128)(2,1)}, u32[]{:S(2)}) copy-start(bf16[1,1024,3,256]{3,1,2,0:T(8,128)(2,1)} %all-gather.17.cloned.1.call-done) | copy-start | bytes 4718596
  838.9 144.3 %copy-start.13 = (bf16[2,64,1024]{2,1,0:T(8,128)(2,1)S(1)}, bf16[2,64,1024]{2,1,0:T(8,128)(2,1)}, u32[]{:S(2)}) copy-start(bf16[2,64,1024]{2,1,0:T(8,128)(2,1)} %copy-done.12) | copy-start | bytes 786436
  839.0 144.3 %copy-start.21 = (bf16[2,4,64,64]{3,2,1,0:T(8,128)(2,1)S(1)}, bf16[2,4,64,64]{3,2,1,0:T(8,128)(2,1)}, u32[]{:S(2)}) copy-start(bf16[2,4,64,64]{3,2,1,0:T(8,128)(2,1)} %copy-done.20) | copy-start | bytes 196612
  982.9 1.7 copy-start.18
  982.9 1.7 copy-start.27
  982.9 1.7 copy-start.34
  982.9 1.7 copy-start.40
  983.0 250.9 %reduce-scatter.16.cloned.1.call-start = ((), (), s32[]{:S(2)}) async-start(), calls=%async_computation.14 | async-start | bytes 1081344 | tf_op jit(solution)/shard_map/reduce_scatter | solution.py:317
  984.6 375.1 %reduce-scatter.18.cloned.1.call-start = ((), (), s32[]{:S(2)}) async-start(), calls=%async_computation.15 | async-start | bytes 4325376 | tf_op jit(solution)/shard_map/reduce_scatter | solution.py:318
  987.5 0.9 copy-start.11
  987.5 1.0 copy-start.25
  987.5 540.1 %reduce-scatter.20.cloned.1.call-start = ((), (), s32[]{:S(2)}) async-start(), calls=%async_computation.16 | async-start | bytes 4325376 | tf_op jit(solution)/shard_map/reduce_scatter | solution.py:319
  991.3 0.7 copy-start.36
  991.3 701.4 %reduce-scatter.14.cloned.1.call-start = ((), (), s32[]{:S(2)}) async-start(), calls=%async_computation.13 | async-start | bytes 3244032 | tf_op jit(solution)/shard_map/reduce_scatter | solution.py:314
  994.3 35.1 %copy-start.15 = (f32[2,64,1024]{2,1,0:T(8,128)S(1)}, f32[2,64,1024]{2,1,0:T(8,128)}, u32[]{:S(2)}) copy-start(f32[2,64,1024]{2,1,0:T(8,128)} %all-reduce.6.cloned.1.call-done) | copy-start | bytes 1572868
  994.3 35.1 %copy-start.16 = (f32[2,64,1024]{2,1,0:T(8,128)S(1)}, f32[2,64,1024]{2,1,0:T(8,128)}, u32[]{:S(2)}) copy-start(f32[2,64,1024]{2,1,0:T(8,128)} %get-tuple-element.32) | copy-start | bytes 1572868
  994.3 35.2 %copy-start.32 = (f32[1,1024]{1,0:T(1,128)S(1)}, f32[1,1024]{1,0:T(1,128)}, u32[]{:S(2)}) copy-start(f32[1,1024]{1,0:T(1,128)} %copy-done.31) | copy-start | bytes 12292
  994.4 37.3 %copy-start.38 = (f32[2,1024]{1,0:T(2,128)S(1)}, f32[2,1024]{1,0:T(2,128)}, u32[]{:S(2)}) copy-start(f32[2,1024]{1,0:T(2,128)} %get-tuple-element.19) | copy-start | bytes 24580
  994.4 37.3 %copy-start.37 = (f32[2,1024]{1,0:T(2,128)S(1)}, f32[2,1024]{1,0:T(2,128)}, u32[]{:S(2)}) copy-start(f32[2,1024]{1,0:T(2,128)} %get-tuple-element.13) | copy-start | bytes 24580
  994.4 872.3 %reduce-scatter.12.cloned.1.call-start = ((), (), s32[]{:S(2)}) async-start(), calls=%async_computation.12 | async-start | bytes 6488064 | tf_op jit(solution)/shard_map/reduce_scatter | solution.py:313
  1028.0 3.7 copy-start.19
  1029.4 3.1 copy-start.50
  1037.2 1.9 copy-start.1
  1037.2 43.8 %copy-start.43 = (f32[1024]{0:T(1024)S(1)}, f32[1024]{0:T(1024)}, u32[]{:S(2)}) copy-start(f32[1024]{0:T(1024)} %get-tuple-element.30) | copy-start | bytes 12292
  1037.2 43.8 %copy-start.45 = (f32[1024]{0:T(1024)S(1)}, f32[1024]{0:T(1024)}, u32[]{:S(2)}) copy-start(f32[1024]{0:T(1024)} %get-tuple-element.52) | copy-start | bytes 12292
  (3 other events, 2.1 us)
Sparse Core Ops, SparseCore 0:
  9.7 157.5 all-gather.14
  168.9 153.0 all-gather.16
  324.8 43.0 all-gather.18
  370.5 42.0 all-gather.12
  420.0 39.3 all-reduce.5
  460.9 152.7 all-gather.20
  615.4 153.3 all-gather.22
  774.4 42.0 all-reduce.7
  829.4 74.0 reduce-scatter.9
  907.0 73.5 reduce-scatter.7
  983.7 44.2 all-reduce.9
  1030.9 161.2 reduce-scatter.15
  1195.2 164.4 reduce-scatter.17
  1362.5 165.0 reduce-scatter.19
  1530.5 162.2 reduce-scatter.13
  1695.7 170.8 reduce-scatter.11
where the time goes:
time: 1870 us
  waiting for transfers between devices  1490 us (80%)
  blocking collectives  290 us (16%)
  matrix products  41.2 us (2%)
  local copies, waits for them, and re-layouts  19.7 us (1%)
    reduce_scatter x1, waiting for transfers between devices, on_device(): lax.psum_scatter(ada_grad, ('dp', 'context'), scatter_dimension=1, tiled=...  174 us
    reduce_scatter x1, waiting for transfers between devices, on_device(): lax.psum_scatter(down_gradient, ('dp', 'context'), scatter_dimension=1, t...  168 us
    reduce_scatter x1, waiting for transfers between devices, on_device(): lax.psum_scatter(mixed_tokens_gradient, ('dp', 'context'), scatter_dimens...  165 us
    all_gather x1, waiting for transfers between devices, fetch_layer(): lax.all_gather(pieces[0], ('dp', 'context'), axis=1, tiled=True)  155 us
    all_gather x1, waiting for transfers between devices, fetch_layer(): lax.all_gather(pieces[3], ('dp', 'context'), axis=0, tiled=True)  153 us
    all_gather x1, waiting for transfers between devices, fetch_layer(): lax.all_gather(pieces[4], ('dp', 'context'), axis=1, tiled=True)  153 us
    psum x1, blocking collectives, on_device(): lax.psum(tuple((jnp.stack(bias_lists[slot]) for slot in range(5))), ('dp'...  152 us
    all_gather x1, waiting for transfers between devices, fetch_layer(): lax.all_gather(pieces[1], ('dp', 'context'), axis=0, tiled=True)  138 us
  transfers between devices with their start and end apart: 16, of which 13 were waited for; matrix products, arithmetic and copies ran while one was open for 2% of the time, Pallas kernels for 0%

commit v1 on v0

v1 whole, which is shorter than its diff:
```python
import functools
import math

import jax
import jax.numpy as jnp
from jax import lax
from jax.experimental import pallas as pl
from jax.experimental.pallas import tpu as pltpu
from jax.sharding import PartitionSpec as P

EPSILON = 1e-06
F32 = jnp.float32
BF16 = jnp.bfloat16
MESH = pl.DeviceIdType.MESH
VMEM = pl.BlockSpec(memory_space=pltpu.VMEM)
DMA = pltpu.SemaphoreType.DMA


def place():
    dp = lax.axis_index("dp")
    ctx = lax.axis_index("context")
    t = lax.axis_index("tensor")
    return dp, ctx, t, (t // 2) * 2 + dp, ctx % 4, ctx // 4, t % 2


def device(x, y, z, core):
    return (x % 2, z * 4 + y, (x // 2) * 2 + core)


def remote(src, dst, send, recv, target):
    return pltpu.make_async_remote_copy(
        src_ref=src, dst_ref=dst, send_sem=send, recv_sem=recv,
        device_id=target, device_id_type=MESH,
    )


def greet(targets):
    barrier = pltpu.get_barrier_semaphore()
    count = 0
    for first, last, target in targets:
        def one(k, carry, target=target):
            pl.semaphore_signal(barrier, inc=1, device_id=target(k), device_id_type=MESH)
            return carry
        lax.fori_loop(first, last, one, 0)
        count += last - first
    pl.semaphore_wait(barrier, count)


def z_peer(k):
    dp, ctx, t, x, y, z, core = place()
    return (dp, ((z + k) % 4) * 4 + y, t)


def y_peer(k):
    dp, ctx, t, x, y, z, core = place()
    return (dp, z * 4 + (y + k) % 4, t)


def ring_index():
    dp, ctx, t, x, y, z, core = place()
    return x * 2 + core


def ring_peer(k):
    dp, ctx, t, x, y, z, core = place()
    r = (x * 2 + core + k) % 8
    return device(r // 2, y, z, r % 2)


def plane_peer(k):
    dp, ctx, t, x, y, z, core = place()
    f = (y * 8 + x * 2 + core + k) % 32
    return device((f // 2) % 4, f // 8, z, f % 2)


def shard_peer(k):
    dp, ctx, t, x, y, z, core = place()
    f = (dp * 16 + ctx + k) % 32
    return (f // 16, f % 16, t)


def any_peer(k):
    dp, ctx, t, x, y, z, core = place()
    f = ((dp * 16 + ctx) * 4 + t + k) % 128
    return (f // 64, (f // 4) % 16, f % 4)


def gather_start(own, slots, mine, n, peer, send, recv):
    def one(k, carry):
        remote(own, slots.at[mine], send.at[k], recv.at[mine], peer(k)).start()
        return carry
    lax.fori_loop(1, n, one, 0)


def gather_wait(own, slots, mine, n, peer, send, recv):
    def one(k, carry):
        other = (mine + k) % n
        copy = remote(own, slots.at[other], send.at[k], recv.at[other], peer(k))
        copy.wait_recv()
        copy.wait_send()
        return carry
    lax.fori_loop(1, n, one, 0)


def scatter_start(parts, slots, mine, n, peer, send, recv):
    def one(k, carry):
        other = (mine + k) % n
        remote(parts.at[other], slots.at[mine], send.at[k], recv.at[mine], peer(k)).start()
        return carry
    lax.fori_loop(1, n, one, 0)


def scatter_wait(parts, slots, mine, n, peer, send, recv):
    def one(k, carry):
        other = (mine + k) % n
        copy = remote(parts.at[other], slots.at[other], send.at[k], recv.at[other], peer(k))
        copy.wait_recv()
        copy.wait_send()
        return carry
    lax.fori_loop(1, n, one, 0)


def call(kernel, collective_id, outs, scratch, args, vmem=60):
    return pl.pallas_call(
        kernel,
        out_shape=outs,
        in_specs=[VMEM] * len(args),
        out_specs=[VMEM] * len(outs),
        scratch_shapes=scratch,
        compiler_params=pltpu.CompilerParams(
            collective_id=collective_id, has_side_effects=True, vmem_limit_bytes=vmem << 20
        ),
    )(*args)


def shape(dims, dtype):
    return jax.ShapeDtypeStruct(dims, dtype)


def normalize(values):
    center = values - jnp.mean(values, axis=-1, keepdims=True)
    inverse = lax.rsqrt(jnp.mean(center * center, axis=-1, keepdims=True) + EPSILON)
    return center * inverse, inverse


def norm_back(grad_hat, normed, inverse):
    first = jnp.mean(grad_hat, axis=-1, keepdims=True)
    second = jnp.mean(grad_hat * normed, axis=-1, keepdims=True)
    return inverse * (grad_hat - first - normed * second)


def dot(left, right, contract):
    return lax.dot_general(
        left, right, ((contract[0], contract[1]), ((), ())), preferred_element_type=F32
    )


NN = ((1,), (0,))
NT = ((1,), (1,))
TN = ((0,), (0,))


def pre_kernel(lat, cot, wp, cond, ada, xg, cg, wf, modg,
               cond_b, part, parts, total,
               w_send, w_recv, w2_send, w2_recv, wx_send, wx_recv, w_local,
               x_send, x_recv, c_send, c_recv, m_send, m_recv, g_send, g_recv, k_send, k_recv):
    dp, ctx, t, x, y, z, core = place()
    x_hi = t // 2
    partner = (1 - dp, ctx, t)
    greet([(1, 128, any_peer)])
    cond_copy = remote(cond, cond_b, k_send, k_recv, partner)
    cond_copy.start()
    across = remote(wp.at[1 - dp], wf.at[dp, ctx], wx_send, wx_recv, partner)
    across.start()
    local = pltpu.make_async_copy(wp.at[dp], wf.at[dp, ctx], w_local)
    local.start()

    def tokens(src, dst, send, recv, act):
        for other in range(4):
            same = jnp.logical_and(x == y, x == other)
            target = device(other, x, z, core)
            copy = remote(src.at[x_hi], dst.at[y], send.at[other], recv.at[y], target)
            if act == "start":
                @pl.when(jnp.logical_not(same))
                def _():
                    copy.start()

                @pl.when(same)
                def _():
                    pltpu.make_async_copy(src.at[x_hi], dst.at[y], recv.at[y]).start()
            else:
                @pl.when(jnp.logical_not(same))
                def _():
                    copy.wait_send()

                remote(src.at[x_hi], dst.at[other], send.at[other], recv.at[other], partner).wait_recv()

    tokens(lat, xg, x_send, x_recv, "start")

    def own_rows(k, carry):
        peer = (ctx + k) % 16
        remote(wp.at[dp], wf.at[dp, ctx], w_send.at[k], w_recv.at[ctx], (dp, peer, t)).start()
        return carry
    lax.fori_loop(1, 16, own_rows, 0)
    tokens(cot, cg, c_send, c_recv, "start")

    cond_copy.wait()
    part[dp] = dot(cond[...].astype(BF16), ada[...], NN)
    part[1 - dp] = dot(cond_b[...].astype(BF16), ada[...], NN)

    def tensor_peer(k):
        return (dp, ctx, (t + k) % 4)
    gather_start(part, parts, t, 4, tensor_peer, m_send, m_recv)
    parts[t] = part[...]

    across.wait()

    def other_rows(k, carry):
        peer = (ctx + k) % 16
        mine = wf.at[1 - dp, ctx]
        remote(mine, mine, w2_send.at[k], w2_recv.at[ctx], (dp, peer, t)).start()
        return carry
    lax.fori_loop(1, 16, other_rows, 0)

    gather_wait(part, parts, t, 4, tensor_peer, m_send, m_recv)
    total[...] = (parts[0] + parts[1]) + (parts[2] + parts[3])
    mine = dp * 16 + ctx

    def mod_start(k, carry):
        f = (mine + k) % 32
        remote(total.at[f % 2], modg.at[mine], g_send.at[k], g_recv.at[mine], shard_peer(k)).start()
        return carry
    lax.fori_loop(1, 32, mod_start, 0)
    modg[mine] = total[y % 2]

    def mod_wait(k, carry):
        f = (mine + k) % 32
        copy = remote(total.at[0], modg.at[f], g_send.at[k], g_recv.at[f], shard_peer(k))
        copy.wait()
        return carry
    lax.fori_loop(1, 32, mod_wait, 0)
    tokens(lat, xg, x_send, x_recv, "wait")
    tokens(cot, cg, c_send, c_recv, "wait")
    local.wait()

    def rows_wait(k, carry):
        peer = (ctx + k) % 16
        remote(wp.at[dp], wf.at[dp, peer], w_send.at[k], w_recv.at[peer], (dp, peer, t)).wait()
        one = wf.at[1 - dp, peer]
        remote(one, one, w2_send.at[k], w2_recv.at[peer], (dp, peer, t)).wait()
        return carry
    lax.fori_loop(1, 16, rows_wait, 0)


def keys_kernel(own, slots, send, recv):
    z = place()[5]
    greet([(1, 4, z_peer)])
    gather_start(own, slots, z, 4, z_peer, send, recv)
    slots[z] = own[...]
    gather_wait(own, slots, z, 4, z_peer, send, recv)


def middle_kernel(parts, x_ref, vec, hidden, branch_ref, middle_ref, slots, own, s1, r1, s2, r2):
    r = ring_index()
    greet([(1, 8, ring_peer)])
    scatter_start(parts, slots, r, 8, ring_peer, s1, r1)
    slots[r] = parts[r]
    scatter_wait(parts, slots, r, 8, ring_peer, s1, r1)
    branch = jnp.sum(slots[...].astype(F32), axis=0) + vec[6:7]
    middle = x_ref[...].astype(F32) + vec[2:3] * branch
    branch_ref[...] = branch
    middle_ref[...] = middle
    normed, _ = normalize(middle)
    own[...] = (normed * (1.0 + vec[4:5]) + vec[3:4]).astype(BF16)
    gather_start(own, hidden, r, 8, ring_peer, s2, r2)
    hidden[r] = own[...]
    gather_wait(own, hidden, r, 8, ring_peer, s2, r2)


def turn_kernel(feed_parts, grad_parts, cot, branch_ref, middle_ref, vec,
                d_branch, d_middle_ref, out_ref, sums, slots1, slots2, own,
                s0, r0, s1, r1, s2, r2):
    r = ring_index()
    greet([(1, 8, ring_peer)])
    scatter_start(grad_parts, slots2, r, 8, ring_peer, s1, r1)
    scatter_start(feed_parts, slots1, r, 8, ring_peer, s0, r0)
    slots2[r] = grad_parts[r]
    slots1[r] = feed_parts[r]
    scatter_wait(grad_parts, slots2, r, 8, ring_peer, s1, r1)
    grad = cot[...].astype(F32)
    middle = middle_ref[...]
    normed, inverse = normalize(middle)
    d_hidden = jnp.sum(slots2[...].astype(F32), axis=0)
    d_middle = grad + norm_back(d_hidden * (1.0 + vec[4:5]), normed, inverse)
    own[...] = (d_middle * vec[2:3]).astype(BF16)
    gather_start(own, d_branch, r, 8, ring_peer, s2, r2)
    d_branch[r] = own[...]
    d_middle_ref[...] = d_middle
    scatter_wait(feed_parts, slots1, r, 8, ring_peer, s0, r0)
    feed = jnp.sum(slots1[...].astype(F32), axis=0) + vec[7:8]
    out_ref[...] = (middle + vec[5:6] * feed).astype(BF16)
    sums[...] = jnp.zeros_like(sums)
    sums[2:3] = jnp.sum(d_middle * branch_ref[...], axis=0, keepdims=True)
    sums[3:4] = jnp.sum(d_hidden, axis=0, keepdims=True)
    sums[4:5] = jnp.sum(d_hidden * normed, axis=0, keepdims=True)
    sums[5:6] = jnp.sum(grad * feed, axis=0, keepdims=True)
    gather_wait(own, d_branch, r, 8, ring_peer, s2, r2)


def d_keys_kernel(parts, out, slots, send, recv):
    z = place()[5]
    greet([(1, 4, z_peer)])
    scatter_start(parts, slots, z, 4, z_peer, send, recv)
    slots[z] = parts[z]
    scatter_wait(parts, slots, z, 4, z_peer, send, recv)
    out[...] = jnp.sum(slots[...].astype(F32), axis=0).astype(BF16)


def last_kernel(parts, x_ref, d_middle, block, vec, sums, small,
                grad_out, block_out, small_all,
                slots, own, m_own, m_slots, z_own, z_slots, y_own,
                s1, r1, gs, gr, bs, br, ms, mr, zs, zr, ys, yr):
    dp, ctx, t, x, y, z, core = place()
    r = ring_index()
    greet([(1, 32, plane_peer), (1, 4, z_peer)])
    scatter_start(parts, slots, r, 8, ring_peer, s1, r1)

    def spread(src, dst, send, recv, act):
        for k in range(4):
            x_hi, other = k // 2, k % 2
            x_to = 2 * x_hi + y % 2
            same = jnp.logical_and(jnp.logical_and(x_to == x, x == y), core == other)
            target = device(x_to, x, z, other)
            slot = dst.at[y // 2, core]
            recv_sem = recv.at[(y // 2) * 2 + core]
            copy = remote(src, slot, send.at[k], recv_sem, target)
            if act == "start":
                @pl.when(jnp.logical_not(same))
                def _():
                    copy.start()

                @pl.when(same)
                def _():
                    pltpu.make_async_copy(src, slot, recv_sem).start()
            else:
                @pl.when(jnp.logical_not(same))
                def _():
                    copy.wait_send()

                remote(src, dst.at[k // 2, k % 2], send.at[k], recv.at[k],
                       (1 - dp, ctx, t)).wait_recv()

    spread(block, block_out, bs, br, "start")
    slots[r] = parts[r]
    scatter_wait(parts, slots, r, 8, ring_peer, s1, r1)
    normed, inverse = normalize(x_ref[...].astype(F32))
    d_hidden = jnp.sum(slots[...].astype(F32), axis=0)
    own[...] = d_middle[...] + norm_back(d_hidden * (1.0 + vec[1:2]), normed, inverse)
    spread(own, grad_out, gs, gr, "start")
    m_own[...] = sums[...]
    m_own[0:1] = jnp.sum(d_hidden, axis=0, keepdims=True)
    m_own[1:2] = jnp.sum(d_hidden * normed, axis=0, keepdims=True)
    gather_start(m_own, m_slots, r, 8, ring_peer, ms, mr)
    m_slots[r] = m_own[...]
    gather_wait(m_own, m_slots, r, 8, ring_peer, ms, mr)
    z_own[0:8] = jnp.sum(m_slots[...], axis=0)
    z_own[8:16] = small[...]
    gather_start(z_own, z_slots, z, 4, z_peer, zs, zr)
    z_slots[z] = z_own[...]
    gather_wait(z_own, z_slots, z, 4, z_peer, zs, zr)
    y_own[...] = jnp.sum(z_slots[...], axis=0)
    gather_start(y_own, small_all, y, 4, y_peer, ys, yr)
    small_all[y] = y_own[...]
    gather_wait(y_own, small_all, y, 4, y_peer, ys, yr)
    spread(block, block_out, bs, br, "wait")
    spread(own, grad_out, gs, gr, "wait")


def weights_kernel(parts, bias, cond_part, out, bias_out, cond_out, slots, rows, c_slots,
                   ws, wr, xs, xr, ks, kr, cs, cr):
    dp, ctx, t, x, y, z, core = place()
    partner = (1 - dp, ctx, t)
    mine = dp * 16 + ctx
    greet([(1, 32, shard_peer)])
    gather_start(cond_part, c_slots, mine, 32, shard_peer, cs, cr)
    bias_copy = remote(bias, bias_out.at[dp], ks, kr, partner)
    bias_copy.start()

    def start(k, carry):
        peer = (ctx + k) % 16
        remote(parts.at[:, peer], slots.at[ctx], ws.at[k], wr.at[ctx], (dp, peer, t)).start()
        return carry
    lax.fori_loop(1, 16, start, 0)
    slots[ctx] = parts[:, ctx]
    c_slots[mine] = cond_part[...]
    bias_out[dp] = bias[...]

    def wait(k, carry):
        peer = (ctx + k) % 16
        remote(parts.at[:, peer], slots.at[peer], ws.at[k], wr.at[peer], (dp, peer, t)).wait()
        return carry
    lax.fori_loop(1, 16, wait, 0)

    def add(k, carry):
        for half in range(2):
            rows[half] += slots[k, half].astype(F32)
        return carry
    rows[...] = jnp.zeros_like(rows)
    lax.fori_loop(0, 16, add, 0)
    across = remote(rows.at[1 - dp], out.at[dp], xs, xr, partner)
    across.start()
    out[dp] = rows[dp]
    gather_wait(cond_part, c_slots, mine, 32, shard_peer, cs, cr)
    cond_out[...] = jnp.sum(c_slots[...], axis=0)
    bias_back = remote(bias, bias_out.at[1 - dp], ks, kr, partner)
    bias_back.wait()
    remote(rows.at[1 - dp], out.at[1 - dp], xs, xr, partner).wait()


def on_device(
    latents, cond, ada_weight, ada_bias, qkv_weight, qv_bias, out_weight, out_bias,
    first_weight, first_bias, second_weight, second_bias, cotangent,
):
    dp, ctx, t, x, y, z, core = place()
    ring = x * 2 + core
    scale = 1.0 / math.sqrt(64)
    cond_slice = lax.dynamic_slice_in_dim(cond.astype(F32), t * 256, 256, 1)
    cond_act = jax.nn.silu(cond_slice).astype(BF16).astype(F32)
    cond_block = jnp.pad(cond_act, ((0, 6), (0, 0)))
    ada = ada_weight[0]
    ada_pad = jnp.pad(ada, ((0, 0), (0, 64)))
    qkv_half = qkv_weight[0].reshape(32, 3, 2, 128).transpose(2, 0, 1, 3).reshape(2, 32, 384)
    out_half = out_weight[0].T.reshape(32, 2, 128).transpose(1, 0, 2)
    first_half = first_weight[0].reshape(32, 2, 512).transpose(1, 0, 2)
    second_half = second_weight[0].T.reshape(32, 2, 512).transpose(1, 0, 2)
    pack = jnp.concatenate([qkv_half, out_half, first_half, second_half], axis=2)

    xg, cg, wf, modg, cond_other = call(
        pre_kernel_out, 1,
        [shape((4, 64, 1024), BF16), shape((4, 64, 1024), BF16),
         shape((2, 16, 32, 1536), BF16), shape((32, 8, 256), F32), shape((8, 256), F32)],
        [pltpu.VMEM((2, 8, 256), F32), pltpu.VMEM((4, 2, 8, 256), F32),
         pltpu.VMEM((2, 8, 256), F32),
         DMA((16,)), DMA((16,)), DMA((16,)), DMA((16,)), DMA, DMA, DMA,
         DMA((4,)), DMA((4,)), DMA((4,)), DMA((4,)), DMA((4,)), DMA((4,)),
         DMA((32,)), DMA((32,)), DMA, DMA],
        [latents, cotangent, pack, cond_block, ada_pad],
    )
    w = wf.reshape(1024, 1536)
    w_qkv, w_out, w_first, w_second = w[:, :384], w[:, 384:512], w[:, 512:1024], w[:, 1024:]
    row = lax.dynamic_slice_in_dim(modg, y // 2, 1, 1)[:, 0, :192].reshape(6144)
    modulation = (row + ada_bias[0].astype(F32)).reshape(6, 1024)
    vec = jnp.concatenate(
        [modulation, out_bias.astype(F32), second_bias.astype(F32)], axis=0
    )
    stream = xg.reshape(256, 1024)
    cot = cg.reshape(256, 1024)
    x_own = lax.dynamic_slice_in_dim(stream, ring * 32, 32, 0)
    cot_own = lax.dynamic_slice_in_dim(cot, ring * 32, 32, 0)

    normed, _ = normalize(stream.astype(F32))
    hidden = (normed * (1.0 + vec[1]) + vec[0]).astype(BF16)
    mixed = dot(hidden, w_qkv, NN)
    biases = lax.dynamic_slice_in_dim(qv_bias[0].astype(F32), dp * 128, 128, 1)
    query = (mixed[:, :128] + biases[0]).astype(BF16)
    key_value = jnp.concatenate([mixed[:, 128:256], mixed[:, 256:] + biases[1]], axis=1).astype(BF16)
    (all_kv,) = call(
        keys_kernel, 2, [shape((4, 256, 256), BF16)], [DMA((4,)), DMA((4,))], [key_value]
    )
    all_kv = all_kv.reshape(1024, 256)
    q2 = query.reshape(256, 2, 64)
    k2 = all_kv[:, :128].reshape(1024, 2, 64)
    v2 = all_kv[:, 128:].reshape(1024, 2, 64)
    scores = jnp.einsum("qhd,khd->hqk", q2, k2, preferred_element_type=F32) * scale
    top = jnp.max(scores, axis=-1, keepdims=True)
    expo = jnp.exp(scores - top)
    prob = expo / jnp.sum(expo, axis=-1, keepdims=True)
    prob_low = prob.astype(BF16)
    attended = jnp.einsum("hqk,khd->qhd", prob_low, v2, preferred_element_type=F32)
    attended = attended.astype(BF16).reshape(256, 128)
    branch_part = dot(attended, w_out, NT).astype(BF16).reshape(8, 32, 1024)
    chunk = shape((32, 1024), F32)
    tokens = shape((8, 32, 1024), BF16)
    hidden_two, branch_own, middle_own = call(
        middle_kernel, 3, [tokens, chunk, chunk],
        [pltpu.VMEM((8, 32, 1024), BF16), pltpu.VMEM((32, 1024), BF16)] + [DMA((8,))] * 4,
        [branch_part, x_own, vec],
    )
    hidden_two = hidden_two.reshape(256, 1024)
    bias_first = lax.dynamic_slice_in_dim(first_bias[0].astype(F32), dp * 512, 512, 0)
    before = dot(hidden_two, w_first, NN) + bias_first
    activated, pull = jax.vjp(lambda v: jax.nn.gelu(v, approximate=True), before)
    activated = activated.astype(BF16)
    feed_part = dot(activated, w_second, NT).astype(BF16).reshape(8, 32, 1024)
    d_feed = (cot.astype(F32) * vec[5]).astype(BF16)
    d_before = pull(dot(d_feed, w_second, NN))[0].astype(BF16)
    grad_part = dot(d_before, w_first, NT).astype(BF16).reshape(8, 32, 1024)
    d_branch, d_middle_own, block_own, sums = call(
        turn_kernel, 4, [tokens, chunk, shape((32, 1024), BF16), shape((8, 1024), F32)],
        [pltpu.VMEM((8, 32, 1024), BF16), pltpu.VMEM((8, 32, 1024), BF16),
         pltpu.VMEM((32, 1024), BF16)] + [DMA((8,))] * 6,
        [feed_part, grad_part, cot_own, branch_own, middle_own, vec],
    )
    d_branch = d_branch.reshape(256, 1024)
    d_attended = dot(d_branch, w_out, NN).astype(BF16).reshape(256, 2, 64)
    d_prob = jnp.einsum("qhd,khd->hqk", d_attended, v2, preferred_element_type=F32)
    row_sums = jnp.sum(prob * d_prob, axis=-1, keepdims=True)
    d_scores = (prob * (d_prob - row_sums)).astype(BF16)
    d_query = jnp.einsum("hqk,khd->qhd", d_scores, k2, preferred_element_type=F32) * scale
    d_query = d_query.astype(BF16).reshape(256, 128)
    d_keys = jnp.einsum("hqk,qhd->khd", d_scores, q2, preferred_element_type=F32) * scale
    d_values = jnp.einsum("hqk,qhd->khd", prob_low, d_attended, preferred_element_type=F32)
    d_kv = jnp.concatenate([d_keys.reshape(1024, 128), d_values.reshape(1024, 128)], axis=1)
    (d_kv,) = call(
        d_keys_kernel, 5, [shape((256, 256), BF16)],
        [pltpu.VMEM((4, 256, 256), BF16), DMA((4,)), DMA((4,))],
        [d_kv.astype(BF16).reshape(4, 256, 256)],
    )
    d_qkv = jnp.concatenate([d_query, d_kv], axis=1)
    d_hidden_part = dot(d_qkv, w_qkv, NT).astype(BF16).reshape(8, 32, 1024)
    bias_row = jnp.concatenate([
        jnp.sum(d_before.astype(F32), axis=0),
        jnp.sum(d_query.astype(F32), axis=0),
        jnp.sum(d_kv[:, 128:].astype(F32), axis=0),
        jnp.zeros((256,), F32),
    ])
    small = jnp.concatenate([
        jnp.sum(d_branch.astype(F32), axis=0)[None],
        jnp.sum(d_feed.astype(F32), axis=0)[None],
        bias_row[None],
        jnp.zeros((5, 1024), F32),
    ], axis=0)
    latents_grad, block_out, small_all = call(
        last_kernel, 6,
        [shape((2, 2, 32, 1024), F32), shape((2, 2, 32, 1024), BF16), shape((4, 16, 1024), F32)],
        [pltpu.VMEM((8, 32, 1024), BF16), pltpu.VMEM((32, 1024), F32),
         pltpu.VMEM((8, 1024), F32), pltpu.VMEM((8, 8, 1024), F32),
         pltpu.VMEM((16, 1024), F32), pltpu.VMEM((4, 16, 1024), F32), pltpu.VMEM((16, 1024), F32),
         DMA((8,)), DMA((8,)), DMA((4,)), DMA((4,)), DMA((4,)), DMA((4,)),
         DMA((8,)), DMA((8,)), DMA((4,)), DMA((4,)), DMA((4,)), DMA((4,))],
        [d_hidden_part, x_own, d_middle_own, block_own, vec, sums, small],
    )
    d_mod = small_all[:, :6].reshape(2, 2, 6144).transpose(1, 0, 2).reshape(4, 6144)
    biases = jnp.sum(small_all[:, 8:11], axis=0)
    d_mod_part = lax.dynamic_slice_in_dim(d_mod, (dp * 16 + ctx) * 192, 192, 1)
    cond_pair = jnp.stack([cond_act, cond_other[:2]])
    cond_four = jnp.where(dp == 0, cond_pair, cond_pair[::-1]).reshape(4, 256)
    highest = lax.Precision.HIGHEST
    ada_grad = jnp.dot(cond_four.T, d_mod_part, precision=highest)
    cond_part = jnp.dot(d_mod_part, ada.astype(F32).T, precision=highest)
    grads = jnp.concatenate([
        dot(hidden, d_qkv, TN), dot(d_branch, attended, TN),
        dot(hidden_two, d_before, TN), dot(d_feed, activated, TN),
    ], axis=1).astype(BF16).reshape(2, 16, 32, 1536)
    w_grad, bias_pair, cond_total = call(
        weights_kernel, 7,
        [shape((2, 32, 1536), F32), shape((2, 8, 1024), F32), shape((8, 256), F32)],
        [pltpu.VMEM((16, 2, 32, 1536), BF16), pltpu.VMEM((2, 32, 1536), F32),
         pltpu.VMEM((32, 8, 256), F32),
         DMA((16,)), DMA((16,)), DMA, DMA, DMA, DMA, DMA((32,)), DMA((32,))],
        [grads, jnp.pad(biases[2:3], ((0, 7), (0, 0))), jnp.pad(cond_part, ((0, 4), (0, 0)))],
    )
    sigmoid = jax.nn.sigmoid(cond_slice)
    cond_mine = lax.dynamic_slice_in_dim(cond_total, dp * 2, 2, 0)
    cond_grad = cond_mine * sigmoid * (1.0 + cond_slice * (1.0 - sigmoid))
    pair = bias_pair[:, 0]
    qkv_grad = w_grad[:, :, :384].reshape(2, 32, 3, 128).transpose(1, 2, 0, 3).reshape(1, 32, 3, 256)
    out_grad = w_grad[:, :, 384:512].transpose(0, 2, 1).reshape(1, 256, 32)
    first_grad = w_grad[:, :, 512:1024].transpose(1, 0, 2).reshape(1, 32, 1024)
    second_grad = w_grad[:, :, 1024:].transpose(0, 2, 1).reshape(1, 1024, 32)
    return (
        block_out.reshape(2, 64, 1024),
        latents_grad.reshape(2, 64, 1024),
        cond_grad,
        ada_grad[None],
        jnp.sum(d_mod, axis=0)[None],
        qkv_grad,
        pair[:, 512:768].reshape(2, 2, 128).transpose(1, 0, 2).reshape(1, 2, 256),
        out_grad,
        biases[0:1],
        first_grad,
        pair[:, :512].reshape(1, 1024),
        second_grad,
        biases[1:2],
    )


def pre_kernel_out(lat, cot, wp, cond, ada, xg, cg, wf, modg, cond_b, part, parts, total, *sems):
    pre_kernel(lat, cot, wp, cond, ada, xg, cg, wf, modg, cond_b, part, parts, total, *sems)


def solution(mesh):
    return jax.shard_map(
        on_device,
        mesh=mesh,
        in_specs=(
            P("dp", "context", None),
            P("dp", None),
            P(None, "tensor", ("dp", "context")),
            P(),
            P(None, ("dp", "context"), None, "tensor"),
            P(None, None, "tensor"),
            P(None, "tensor", ("dp", "context")),
            P(),
            P(None, ("dp", "context"), "tensor"),
            P(None, "tensor"),
            P(None, "tensor", ("dp", "context")),
            P(),
            P("dp", "context", None),
        ),
        out_specs=(
            P("dp", "context", None),
            P("dp", "context", None),
            P("dp", "tensor"),
            P(None, "tensor", ("dp", "context")),
            P(),
            P(None, ("dp", "context"), None, "tensor"),
            P(None, None, "tensor"),
            P(None, "tensor", ("dp", "context")),
            P(),
            P(None, ("dp", "context"), "tensor"),
            P(None, "tensor"),
            P(None, "tensor", ("dp", "context")),
            P(),
        ),
        check_vma=False,
    )
```

time: 1870 us -> 327 us (0.17)
  waiting for transfers between devices: 1490 us -> 0 us
  blocking collectives: 290 us -> 0 us
  Pallas kernels: 0 us -> 249 us
    reduce_scatter x7 -> x0, waiting for transfers between devices: 773 us -> none  [the longest x1 174 us: on_device(): lax.psum_scatter(ada_grad, ('dp', 'context'), scatter_dimension=1, tiled=...]
    all_gather x6 -> x0, waiting for transfers between devices: 599 us -> none  [the longest x1 155 us: fetch_layer(): lax.all_gather(pieces[0], ('dp', 'context'), axis=1, tiled=True)]
    pallas_call x0 -> x7, Pallas kernels: none -> 249 us  [call(): pl.pallas_call(kernel, out_shape=outs, in_specs=[VMEM] * len(args), out_s...]
    psum x3 -> x0, blocking collectives: 206 us -> none  [the longest x1 152 us: on_device(): lax.psum(tuple((jnp.stack(bias_lists[slot]) for slot in range(5))), ('dp'...]
    psum x3 -> x0, waiting for transfers between devices: 113 us -> none  [the longest x2 71 us: tensor_total(): return lax.psum(values, 'tensor')]
    all_gather x1 -> x0, blocking collectives: 83.9 us -> none  [fetch_layer(): lax.all_gather(pieces[2], ('dp', 'context'), axis=1, tiled=True)]
    dot_general x21 -> x19, matrix products: 41.2 us -> 26.3 us  [the longest x12 20.1 us: dot(): lax.dot_general(left, right, ((contract[0], contract[1]), ((), ())), pref...]
  transfers between devices with their start and end apart: 16 -> 0, of which waited for: 13 -> 0; matrix products, arithmetic and copies ran while one was open for 2% -> 0% of each run, Pallas kernels for 0% -> 0%
where the time goes in v1:
time: 327 us; the launch traced here: 324 us
  Pallas kernels  249 us (76%)
  matrix products  27.2 us (8%)
  local copies, waits for them, and re-layouts  26.7 us (8%)
  other arithmetic  19.4 us (6%)
    pallas_call x7, Pallas kernels, call(): pl.pallas_call(kernel, out_shape=outs, in_specs=[VMEM] * len(args), out_s...  249 us
    dot_general x12, matrix products, dot(): lax.dot_general(left, right, ((contract[0], contract[1]), ((), ())), pref...  20.1 us

profile of v1, /device:TPU:0, one launch (start us, length us, event | category | flops | bytes accessed | tf_op | source)
XLA Modules:
  0.0 323.9 jit_solution(16314382892230406786)
XLA Ops:
  0.7 0.7 fusion.50
  2.0 0.8 reshape_squeeze.11
  2.9 0.9 reshape_squeeze.12
  3.8 0.8 copy.100
  4.7 0.7 pad_maximum_fusion.2.wp
  5.4 1.0 copy.67
  6.4 0.7 pad.17.ada
  7.0 72.7 %shard_map.228 = (bf16[4,64,1024]{2,1,0:T(8,128)(2,1)}, bf16[4,64,1024]{2,1,0:T(8,128)(2,1)}, bf16[2,16,32,1536]{3,2,1,0:T(8,128)(2,1)}, f32[32,8,256]{2,1,0:T(8,128)}, f32[8,256]{1,0:T(8,128)}) custom-call(bf16[2,64,1024]{2,1,0:T(8,128)(2,1)} %lat.1, bf16[2,64,1024]{2,1,0:T(8,128)(2,1)} %cot.1, bf16[2,32,1536]{2,1,0:T(8,128)(2,1)} %pad_maximum_fusion.2.wp, ...), custom_call_target="tpu_custom_call" | custom-call | tf_op jit(solution)/shard_map/pallas_call | solution.py:124
  79.8 1.6 constant_dynamic-slice_fusion
  81.4 1.0 dynamic-slice_reduce_fusion
  82.6 2.0 convert_reduce_fusion
  84.6 1.3 fusion.7
  86.4 1.6 fusion.15
  88.1 0.7 pad_maximum_fusion.4.own
  88.7 10.6 %shard_map.229 = bf16[4,256,256]{2,1,0:T(8,128)(2,1)} custom-call(bf16[256,256]{1,0:T(8,128)(2,1)} %pad_maximum_fusion.4.own), custom_call_target="tpu_custom_call" | custom-call | tf_op jit(solution)/shard_map/pallas_call | solution.py:124
  99.3 1.1 fusion.63
  100.7 0.9 fusion.66
  101.8 1.9 convolution_convert_fusion.9
  103.7 2.1 convolution_convert_fusion.6
  105.9 1.4 convert_reduce_fusion.6
  107.3 0.7 reshape.240
  108.1 0.7 convert_element_type.147
  108.8 0.7 convert_element_type.148
  110.1 22.6 %shard_map.230 = (bf16[8,32,1024]{2,1,0:T(8,128)(2,1)}, f32[32,1024]{1,0:T(8,128)}, f32[32,1024]{1,0:T(8,128)}) custom-call(bf16[8,32,1024]{2,1,0:T(8,128)(2,1)} %bitcast.171, bf16[32,1024]{1,0:T(8,128)(2,1)} %get-tuple-element.76.x_ref, f32[8,1024]{1,0:T(8,128)} %pad_maximum_fusion.7.vec), custom_call_target="tpu_custom_call" | custom-call | tf_op jit(solution)/shard_map/pallas_call | solution.py:124
  132.8 0.7 dynamic-slice_convert_fusion
  133.5 1.8 convolution_add_fusion
  135.3 2.7 convert_reduce_fusion.3
  138.1 0.7 copy-done.10
  138.8 1.3 convolution_convert_fusion.4
  140.0 1.3 convolution_convert_fusion.5
  141.3 24.0 %shard_map.231 = (bf16[8,32,1024]{2,1,0:T(8,128)(2,1)}, f32[32,1024]{1,0:T(8,128)}, bf16[32,1024]{1,0:T(8,128)(2,1)}, f32[8,1024]{1,0:T(8,128)}) custom-call(bf16[8,32,1024]{2,1,0:T(8,128)(2,1)} %bitcast.185, bf16[8,32,1024]{2,1,0:T(8,128)(2,1)} %bitcast.184, bf16[32,1024]{1,0:T(8,128)(2,1)} %get-tuple-element.75.cot, ...), custom_call_target="tpu_custom_call" | custom-call | tf_op jit(solution)/shard_map/pallas_call | solution.py:124
  165.3 1.4 convolution_convert_fusion.10
  167.3 2.0 multiply_convert_fusion
  169.4 1.1 convert_reduce_fusion.5
  171.3 1.0 fusion.3
  172.8 0.9 pad_maximum_fusion.1.parts
  173.6 12.3 %shard_map.232 = bf16[256,256]{1,0:T(8,128)(2,1)} custom-call(bf16[4,256,256]{2,1,0:T(8,128)(2,1)} %pad_maximum_fusion.1.parts), custom_call_target="tpu_custom_call" | custom-call | tf_op jit(solution)/shard_map/pallas_call | solution.py:124
  186.1 1.4 convolution_convert_fusion.2
  187.8 1.4 convolution_convert_fusion.1
  189.4 1.0 convolution_convert_fusion.7
  190.4 0.8 fusion.28
  191.2 1.0 copy.78
  192.2 1.8 convolution_convert_fusion
  194.0 1.9 pad_maximum_fusion.parts
  196.2 0.7 maximum_maximum_fusion.small
  196.9 2.4 convolution_convert_fusion.3
  199.3 44.2 %shard_map.233 = (f32[2,2,32,1024]{3,2,1,0:T(8,128)}, bf16[2,2,32,1024]{3,2,1,0:T(8,128)(2,1)}, f32[4,16,1024]{2,1,0:T(8,128)}) custom-call(bf16[8,32,1024]{2,1,0:T(8,128)(2,1)} %bitcast.177, bf16[32,1024]{1,0:T(8,128)(2,1)} %get-tuple-element.76.x_ref, f32[32,1024]{1,0:T(8,128)} %get-tuple-element.39.d_middle, bf16[32,1024]{1,0:T(8,128)(2,1)} %get-tuple-element.40.block, ...), custom_call_target="tpu_custom_call" | custom-call | tf_op jit(solution)/shard_map/pallas_call | solution.py:124
  243.5 0.9 slice_reduce_fusion.1
  244.9 0.7 pad.19.cond_part
  245.5 0.9 slice_reduce_fusion
  247.7 62.8 %shard_map.234 = (f32[2,32,1536]{2,1,0:T(8,128)}, f32[2,8,1024]{2,1,0:T(8,128)}, f32[8,256]{1,0:T(8,128)}) custom-call(bf16[2,16,32,1536]{3,2,1,0:T(8,128)(2,1)} %pad_maximum_fusion.parts, f32[8,1024]{1,0:T(8,128)} %pad.18.bias, f32[8,256]{1,0:T(8,128)} %pad.19.cond_part), custom_call_target="tpu_custom_call" | custom-call | tf_op jit(solution)/shard_map/pallas_call | solution.py:124
  310.5 1.1 slice_bitcast_fusion
  311.7 0.8 reshape.236
  312.6 0.8 reshape.238
  313.4 0.9 slice.113
  314.4 0.7 reshape.232
  315.1 0.8 slice_bitcast_fusion.2
  315.9 0.6 reshape.235
  316.5 0.8 slice.114
  318.6 1.3 fusion.43
  319.9 0.7 slice_bitcast_fusion.4
  320.7 1.1 convolution_bitcast_fusion
  322.4 0.7 copy.106
  323.1 0.8 copy.107
  (123 shorter events, 9.2 us)
Async XLA Ops:
  0.6 4.0 %copy-start = (bf16[1,256,32]{1,2,0:T(8,128)(2,1)S(1)}, bf16[1,256,32]{1,2,0:T(8,128)(2,1)}, u32[]{:S(2)}) copy-start(bf16[1,256,32]{1,2,0:T(8,128)(2,1)} %param.19) | copy-start | bytes 49156
  0.7 81.9 %copy-start.16 = (bf16[1,6144]{1,0:T(2,128)(2,1)S(1)}, bf16[1,6144]{1,0:T(2,128)(2,1)}, u32[]{:S(2)}) copy-start(bf16[1,6144]{1,0:T(2,128)(2,1)} %param.16) | copy-start | bytes 36868
  79.8 6.3 %copy-start.1 = (bf16[4,64,1024]{2,1,0:T(8,128)(2,1)S(1)}, bf16[4,64,1024]{2,1,0:T(8,128)(2,1)}, u32[]{:S(2)}) copy-start(bf16[4,64,1024]{2,1,0:T(8,128)(2,1)} %get-tuple-element.31) | copy-start | bytes 1572868
  82.6 3.5 %copy-start.20 = (f32[1024]{0:T(1024)}, f32[1024]{0:T(1024)S(1)}, u32[]{:S(2)}) copy-start(f32[1024]{0:T(1024)S(1)} %get-tuple-element.57) | copy-start | bytes 12292
  82.6 5.4 %copy-start.29 = (bf16[1,2,256]{2,1,0:T(2,128)(2,1)S(1)}, bf16[1,2,256]{2,1,0:T(2,128)(2,1)}, u32[]{:S(2)}) copy-start(bf16[1,2,256]{2,1,0:T(2,128)(2,1)} %param.18) | copy-start | bytes 3076
  100.7 0.9 copy-start.14
  101.6 2.1 copy-start.24
  101.6 65.1 %copy-start.4 = (f32[2,256,1024]{2,1,0:T(8,128)}, f32[2,256,1024]{2,1,0:T(8,128)S(1)}, u32[]{:S(2)}) copy-start(f32[2,256,1024]{2,1,0:T(8,128)S(1)} %get-tuple-element.66) | copy-start | bytes 6291460
  101.7 2.0 copy-start.12
  103.7 31.6 %copy-start.3 = (bf16[4,64,1024]{2,1,0:T(8,128)(2,1)S(1)}, bf16[4,64,1024]{2,1,0:T(8,128)(2,1)}, u32[]{:S(2)}) copy-start(bf16[4,64,1024]{2,1,0:T(8,128)(2,1)} %get-tuple-element.35) | copy-start | bytes 1572868
  108.1 27.2 %copy-start.21 = (f32[1024]{0:T(1024)S(1)}, f32[1024]{0:T(1024)}, u32[]{:S(2)}) copy-start(f32[1024]{0:T(1024)} %copy-done.20) | copy-start | bytes 12292
  135.3 4.7 %copy-start.30 = (f32[256,512]{1,0:T(8,128)}, f32[256,512]{1,0:T(8,128)S(1)}, u32[]{:S(2)}) copy-start(f32[256,512]{1,0:T(8,128)S(1)} %convolution_add_fusion) | copy-start | bytes 1572868
  135.3 3.4 %copy-start.17 = (bf16[2,16,32,1536]{3,2,1,0:T(8,128)(2,1)S(1)}, bf16[2,16,32,1536]{3,2,1,0:T(8,128)(2,1)}, u32[]{:S(2)}) copy-start(bf16[2,16,32,1536]{3,2,1,0:T(8,128)(2,1)} %get-tuple-element.33) | copy-start | bytes 9437188
  138.1 0.7 copy-start.10
  140.0 26.7 %copy-start.13 = (bf16[1024,128]{0,1:T(8,128)(2,1)S(1)}, bf16[1024,128]{0,1:T(8,128)(2,1)}, u32[]{:S(2)}) copy-start(bf16[1024,128]{0,1:T(8,128)(2,1)} %copy-done.12) | copy-start | bytes 786436
  140.0 26.7 %copy-start.25 = (f32[2,256]{1,0:T(2,128)S(1)}, f32[2,256]{1,0:T(2,128)}, u32[]{:S(2)}) copy-start(f32[2,256]{1,0:T(2,128)} %copy-done.24) | copy-start | bytes 6148
  166.7 0.6 copy-start.18
  167.3 3.2 copy-start.15
  169.3 2.0 copy-start.19
  169.4 2.0 copy-start.26
  172.8 14.8 %copy-start.8 = (bf16[8,32,1024]{2,1,0:T(8,128)(2,1)S(1)}, bf16[8,32,1024]{2,1,0:T(8,128)(2,1)}, u32[]{:S(2)}) copy-start(bf16[8,32,1024]{2,1,0:T(8,128)(2,1)} %get-tuple-element.34) | copy-start | bytes 1572868
  186.1 3.0 copy-start.2
  191.1 2.8 copy-start.5
  193.9 1.9 copy-start.28
  194.0 2.0 copy-start.6
  194.0 2.0 copy-start.27
  194.0 2.2 copy-start.22
  195.9 48.8 %copy-start.9 = (bf16[1,256,192]{1,2,0:T(8,128)(2,1)S(1)}, bf16[1,256,192]{1,2,0:T(8,128)(2,1)}, u32[]{:S(2)}) copy-start(bf16[1,256,192]{1,2,0:T(8,128)(2,1)} %param.15) | copy-start | bytes 294916
  310.5 8.1 %copy-start.23 = (bf16[2,1024]{1,0:T(2,128)(2,1)S(1)}, bf16[2,1024]{1,0:T(2,128)(2,1)}, u32[]{:S(2)}) copy-start(bf16[2,1024]{1,0:T(2,128)(2,1)} %param.14) | copy-start | bytes 12292
  310.5 11.9 %copy-start.11 = (bf16[2,2,32,1024]{3,2,1,0:T(8,128)(2,1)S(1)}, bf16[2,2,32,1024]{3,2,1,0:T(8,128)(2,1)}, u32[]{:S(2)}) copy-start(bf16[2,2,32,1024]{3,2,1,0:T(8,128)(2,1)} %get-tuple-element.42) | copy-start | bytes 786436
  310.5 12.6 %copy-start.7 = (f32[2,2,32,1024]{3,2,1,0:T(8,128)S(1)}, f32[2,2,32,1024]{3,2,1,0:T(8,128)}, u32[]{:S(2)}) copy-start(f32[2,2,32,1024]{3,2,1,0:T(8,128)} %get-tuple-element.43) | copy-start | bytes 1572868

commit v2 on v1

v2 whole, which is shorter than its diff:
```python
import math

import jax
import jax.numpy as jnp
from jax import lax
from jax.experimental import pallas as pl
from jax.experimental.pallas import tpu as pltpu
from jax.sharding import PartitionSpec as P

EPSILON = 1e-06
F32 = jnp.float32
BF16 = jnp.bfloat16
MESH = pl.DeviceIdType.MESH
VMEM = pl.BlockSpec(memory_space=pltpu.VMEM)
DMA = pltpu.SemaphoreType.DMA


def place():
    dp = lax.axis_index("dp")
    ctx = lax.axis_index("context")
    t = lax.axis_index("tensor")
    return dp, ctx, t, (t // 2) * 2 + dp, ctx % 4, ctx // 4, t % 2


def device(x, y, z, core):
    return (x % 2, z * 4 + y, (x // 2) * 2 + core)


def remote(src, dst, send, recv, target):
    return pltpu.make_async_remote_copy(
        src_ref=src, dst_ref=dst, send_sem=send, recv_sem=recv,
        device_id=target, device_id_type=MESH,
    )


def greet(targets):
    barrier = pltpu.get_barrier_semaphore()
    count = 0
    for first, last, target in targets:
        def one(k, carry, target=target):
            pl.semaphore_signal(barrier, inc=1, device_id=target(k), device_id_type=MESH)
            return carry
        lax.fori_loop(first, last, one, 0)
        count += last - first
    pl.semaphore_wait(barrier, count)


def z_peer(k):
    dp, ctx, t, x, y, z, core = place()
    return (dp, ((z + k) % 4) * 4 + y, t)


def y_peer(k):
    dp, ctx, t, x, y, z, core = place()
    return (dp, z * 4 + (y + k) % 4, t)


def ring_index():
    dp, ctx, t, x, y, z, core = place()
    return x * 2 + core


def ring_peer(k):
    dp, ctx, t, x, y, z, core = place()
    r = (x * 2 + core + k) % 8
    return device(r // 2, y, z, r % 2)


def gather_start(own, slots, mine, n, peer, send, recv):
    def one(k, carry):
        remote(own, slots.at[mine], send.at[k], recv.at[mine], peer(k)).start()
        return carry
    lax.fori_loop(1, n, one, 0)


def gather_wait(own, slots, mine, n, peer, send, recv):
    def one(k, carry):
        other = (mine + k) % n
        copy = remote(own, slots.at[other], send.at[k], recv.at[other], peer(k))
        copy.wait_recv()
        copy.wait_send()
        return carry
    lax.fori_loop(1, n, one, 0)


def scatter_start(parts, slots, mine, n, peer, send, recv):
    def one(k, carry):
        other = (mine + k) % n
        remote(parts.at[other], slots.at[mine], send.at[k], recv.at[mine], peer(k)).start()
        return carry
    lax.fori_loop(1, n, one, 0)


def scatter_wait(parts, slots, mine, n, peer, send, recv):
    def one(k, carry):
        other = (mine + k) % n
        copy = remote(parts.at[other], slots.at[other], send.at[k], recv.at[other], peer(k))
        copy.wait_recv()
        copy.wait_send()
        return carry
    lax.fori_loop(1, n, one, 0)


def shape(dims, dtype):
    return jax.ShapeDtypeStruct(dims, dtype)


def normalize(values):
    center = values - jnp.mean(values, axis=-1, keepdims=True)
    inverse = lax.rsqrt(jnp.mean(center * center, axis=-1, keepdims=True) + EPSILON)
    return center * inverse, inverse


def norm_back(grad_hat, normed, inverse):
    first = jnp.mean(grad_hat, axis=-1, keepdims=True)
    second = jnp.mean(grad_hat * normed, axis=-1, keepdims=True)
    return inverse * (grad_hat - first - normed * second)


def dot(left, right, contract, precision=None):
    return lax.dot_general(
        left, right, (contract, ((), ())), precision=precision, preferred_element_type=F32
    )


NN = ((1,), (0,))
NT = ((1,), (1,))
TN = ((0,), (0,))
SCALE = 1.0 / math.sqrt(64)
ROOT = math.sqrt(2.0 / math.pi)
STEPS = (1, 3, 2)


def from_back(k):
    y, z = lax.axis_index("context") % 4, lax.axis_index("context") // 4
    return (y + 4 - k) % 4, (z + 4 - k) % 4


def plane_one(full, h, send, recv, start):
    dp, ctx, t, x, y, z, core = place()
    mine = full.at[h, z, y]
    for k in STEPS:
        target = (dp, ((z + h * k) % 4) * 4 + (y + (1 - h) * k) % 4, t)
        if start:
            remote(mine, mine, send.at[h, k], recv.at[h, k], target).start()
        else:
            slot = full.at[h, (z + h * (4 - k)) % 4, (y + (1 - h) * (4 - k)) % 4]
            remote(mine, slot, send.at[h, k], recv.at[h, k], target).wait()


def plane_two(full, send, recv, start):
    dp, ctx, t, x, y, z, core = place()
    for k in STEPS:
        by, bz = from_back(k)
        row, column = full.at[0, z], full.at[1, :, y]
        if start:
            remote(row, row, send.at[0, k], recv.at[0, k], z_peer(k)).start()
            remote(column, column, send.at[1, k], recv.at[1, k], y_peer(k)).start()
        else:
            remote(row, full.at[0, bz], send.at[0, k], recv.at[0, k], z_peer(k)).wait()
            remote(column, full.at[1, :, by], send.at[1, k], recv.at[1, k], y_peer(k)).wait()


def reduce_one(parts, slots, send, recv, start):
    dp, ctx, t, x, y, z, core = place()
    for k in STEPS:
        by, bz = from_back(k)
        row, column = parts.at[0, (z + k) % 4], parts.at[1, :, (y + k) % 4]
        to_row = slots.at[0, z if start else bz]
        to_column = slots.at[1, y if start else by]
        for copy in (remote(row, to_row, send.at[0, k], recv.at[0, k], z_peer(k)),
                     remote(column, to_column, send.at[1, k], recv.at[1, k], y_peer(k))):
            copy.start() if start else copy.wait()
    if start:
        slots[0, z] = parts[0, z]
        slots[1, y] = parts[1, :, y]


def reduce_two(parts, slots, send, recv, start):
    dp, ctx, t, x, y, z, core = place()
    for k in STEPS:
        by, bz = from_back(k)
        to_y = slots.at[0, y if start else by]
        to_z = slots.at[1, z if start else bz]
        for copy in (remote(parts.at[0, (y + k) % 4], to_y, send.at[0, k], recv.at[0, k], y_peer(k)),
                     remote(parts.at[1, (z + k) % 4], to_z, send.at[1, k], recv.at[1, k], z_peer(k))):
            copy.start() if start else copy.wait()
    if start:
        slots[0, y] = parts[0, y]
        slots[1, z] = parts[1, z]


def add_slots(slots, out):
    for h in range(2):
        total = slots[h, 0].astype(F32)
        for k in range(1, 4):
            total = total + slots[h, k].astype(F32)
        out[h] = total.astype(out.dtype)


def tokens(src, dst, send, recv, start):
    dp, ctx, t, x, y, z, core = place()
    for other in range(4):
        same = jnp.logical_and(x == y, x == other)
        copy = remote(src.at[t // 2], dst.at[y], send.at[other], recv.at[y],
                      device(other, x, z, core))
        if start:
            @pl.when(jnp.logical_not(same))
            def _():
                copy.start()

            @pl.when(same)
            def _():
                pltpu.make_async_copy(src.at[t // 2], dst.at[y], recv.at[y]).start()
        else:
            @pl.when(jnp.logical_not(same))
            def _():
                copy.wait_send()

            remote(src.at[t // 2], dst.at[other], send.at[other], recv.at[other],
                   (1 - dp, ctx, t)).wait_recv()


def spread(src, dst, send, recv, start):
    dp, ctx, t, x, y, z, core = place()
    for k in range(4):
        x_hi, other = k // 2, k % 2
        x_to = 2 * x_hi + y % 2
        same = jnp.logical_and(jnp.logical_and(x_to == x, x == y), core == other)
        slot = dst.at[y // 2, core]
        recv_sem = recv.at[(y // 2) * 2 + core]
        copy = remote(src, slot, send.at[k], recv_sem, device(x_to, x, z, other))
        if start:
            @pl.when(jnp.logical_not(same))
            def _():
                copy.start()

            @pl.when(same)
            def _():
                pltpu.make_async_copy(src, slot, recv_sem).start()
        else:
            @pl.when(jnp.logical_not(same))
            def _():
                copy.wait_send()

            remote(src, dst.at[k // 2, k % 2], send.at[k], recv.at[k],
                   (1 - dp, ctx, t)).wait_recv()


def tokens_target(k):
    dp, ctx, t, x, y, z, core = place()
    return device(k, x, z, core)


def tokens_source(k):
    dp, ctx, t, x, y, z, core = place()
    return device(y, k, z, core)


def spread_target(k):
    dp, ctx, t, x, y, z, core = place()
    return device(2 * (k // 2) + y % 2, x, z, k % 2)


def spread_source(k):
    dp, ctx, t, x, y, z, core = place()
    return device(y, 2 * (k // 2) + dp, z, k % 2)


def ctx_peer(k):
    dp, ctx, t, x, y, z, core = place()
    return (dp, (ctx + k) % 16, t)


INPUTS = dict(lat=0, cot=1, packa=2, packb=3, cond=4, ada=5, ada_bias=6, qv=7, b1=8, ob=9, b2=10)
OUTPUTS = dict(
    block_out=((2, 2, 32, 1024), BF16),
    grad_out=((2, 2, 32, 1024), F32),
    cond_out=((8, 256), F32),
    ada_out=((256, 256), F32),
    ada_bias_out=((1, 6144), F32),
    ga_out=((2, 32, 512), F32),
    gb_out=((2, 32, 1024), F32),
    bias_out=((2, 8, 1024), F32),
    wide_out=((8, 1024), F32),
)
BUFFERS = dict(
    xg=((4, 64, 1024), BF16), cg=((4, 64, 1024), BF16),
    wa=((2, 4, 4, 32, 512), BF16), wb=((2, 4, 4, 32, 1024), BF16),
    cond_b=((8, 256), F32), cond8=((8, 256), F32),
    part=((8, 256), F32), parts=((8, 8, 256), F32), pair=((2, 8, 256), F32),
    modg=((16, 2, 8, 256), F32), flat=((8, 6144), F32), vec=((8, 1024), F32),
    normed=((256, 1024), F32), hidden=((256, 1024), BF16),
    kv=((256, 256), BF16), kvg=((4, 256, 256), BF16), prob=((2, 256, 1024), F32),
    branch_part=((8, 32, 1024), BF16), branch_slots=((8, 32, 1024), BF16),
    h2_own=((32, 1024), BF16), h2=((8, 32, 1024), BF16),
    d_feed=((256, 1024), BF16), d_act=((256, 512), F32),
    dh2_part=((8, 32, 1024), BF16), dh2_slots=((8, 32, 1024), BF16),
    feed_part=((8, 32, 1024), BF16), feed_slots=((8, 32, 1024), BF16),
    db_own=((32, 1024), BF16), db=((8, 32, 1024), BF16),
    block_own=((32, 1024), BF16), d_middle=((32, 1024), F32),
    dkv_part=((4, 256, 256), BF16), dkv_slots=((4, 256, 256), BF16),
    dh_part=((8, 32, 1024), BF16), dh_slots=((8, 32, 1024), BF16),
    grad_own=((32, 1024), F32),
    m_own=((8, 1024), F32), m_slots=((8, 8, 1024), F32),
    z_own=((16, 1024), F32), z_slots=((4, 16, 1024), F32),
    y_own=((16, 1024), F32), y_slots=((4, 16, 1024), F32),
    dm=((8, 6144), F32), bias_own=((8, 1024), F32),
    cond_part=((8, 256), F32), cond_slots=((16, 8, 256), F32), cond_sum=((8, 256), F32),
    cond_other=((8, 256), F32),
    ga=((2, 4, 4, 32, 512), BF16), ga1=((2, 4, 4, 32, 512), BF16),
    ga2=((2, 4, 32, 512), BF16), ga3=((2, 4, 32, 512), BF16), gas=((2, 32, 512), F32),
    gb=((2, 4, 4, 32, 1024), BF16), gb1=((2, 4, 4, 32, 1024), BF16),
    gb2=((2, 4, 32, 1024), BF16), gb3=((2, 4, 32, 1024), BF16), gbs=((2, 32, 1024), F32),
)
SEMS = dict(
    s_cond=(), s_xa=(), s_xb=(), s_xg=(4,), s_cg=(4,),
    s_wa1=(2, 4), s_wa2=(2, 4), s_wb1=(2, 4), s_wb2=(2, 4),
    s_mod=(8,), s_mod2=(16,), s_kv=(4,),
    s_branch=(8,), s_h2=(8,), s_dh2=(8,), s_feed=(8,), s_db=(8,),
    s_block=(4,), s_dkv=(4,), s_dh=(8,), s_grad=(4,),
    s_m=(8,), s_z=(4,), s_y=(4,), s_bias=(), s_c=(16,), s_cx=(),
    s_ga1=(2, 4), s_ga2=(2, 4), s_gb1=(2, 4), s_gb2=(2, 4), s_gax=(), s_gbx=(),
)


class Refs:
    pass


def block_kernel(*refs):
    g = Refs()
    names = list(INPUTS) + list(OUTPUTS) + list(BUFFERS)
    for name, ref in zip(names, refs):
        setattr(g, name, ref)
    sems = refs[len(names):]
    for i, name in enumerate(SEMS):
        setattr(g, name, (sems[2 * i], sems[2 * i + 1]))
    dp, ctx, t, x, y, z, core = place()
    r = x * 2 + core
    partner = (1 - dp, ctx, t)

    greet([(1, 8, ring_peer), (1, 16, ctx_peer)] + [(0, 4, f) for f in (
        tokens_target, tokens_source, spread_target, spread_source)])

    cond_copy = remote(g.cond, g.cond_b, *g.s_cond, partner)
    cond_copy.start()
    across_a = remote(g.packa.at[1 - dp], g.wa.at[dp, z, y], *g.s_xa, partner)
    across_a.start()
    g.wa[dp, z, y] = g.packa[dp]
    plane_one(g.wa, dp, *g.s_wa1, True)
    tokens(g.lat, g.xg, *g.s_xg, True)
    cond_copy.wait()
    g.cond8[...] = g.cond[...] + g.cond_b[...]
    g.part[...] = dot(g.cond8[...].astype(BF16), g.ada[...], NN)
    gather_start(g.part, g.parts, r, 8, ring_peer, *g.s_mod)
    g.parts[r] = g.part[...]
    across_b = remote(g.packb.at[1 - dp], g.wb.at[dp, z, y], *g.s_xb, partner)
    across_b.start()
    g.wb[dp, z, y] = g.packb[dp]
    remote(g.packa.at[1 - dp], g.wa.at[1 - dp, z, y], *g.s_xa, partner).wait()
    plane_one(g.wa, 1 - dp, *g.s_wa1, True)
    gather_wait(g.part, g.parts, r, 8, ring_peer, *g.s_mod)
    for c in range(2):
        g.pair[c] = (g.parts[2 * c] + g.parts[2 * c + 1]) + (g.parts[2 * c + 4] + g.parts[2 * c + 5])
    gather_start(g.pair, g.modg, ctx, 16, ctx_peer, *g.s_mod2)
    g.modg[ctx] = g.pair[...]
    plane_one(g.wa, dp, *g.s_wa1, False)
    plane_one(g.wa, 1 - dp, *g.s_wa1, False)
    plane_two(g.wa, *g.s_wa2, True)
    plane_one(g.wb, dp, *g.s_wb1, True)
    remote(g.packb.at[1 - dp], g.wb.at[1 - dp, z, y], *g.s_xb, partner).wait()
    plane_one(g.wb, 1 - dp, *g.s_wb1, True)
    tokens(g.cot, g.cg, *g.s_cg, True)

    tokens(g.lat, g.xg, *g.s_xg, False)
    normed, _ = normalize(g.xg[...].astype(F32).reshape(256, 1024))
    g.normed[...] = normed
    gather_wait(g.pair, g.modg, ctx, 16, ctx_peer, *g.s_mod2)
    for p in range(16):
        c, first = p // 8, (2 * p) % 16
        both = jnp.concatenate([g.modg[first, c][:, :192], g.modg[first + 1, c][:, :192]], axis=1)
        g.flat[:, 384 * p:384 * p + 384] = (
            both + g.ada_bias[0:1, 384 * p:384 * p + 384].astype(F32))
    for k in range(6):
        g.vec[k:k + 1] = g.flat[pl.ds(y, 1), k * 1024:(k + 1) * 1024]
    shift1, scale1, gate1, shift2, scale2, gate2 = [g.vec[k:k + 1] for k in range(6)]
    hidden = (g.normed[...] * (1.0 + scale1) + shift1).astype(BF16)
    g.hidden[...] = hidden
    plane_two(g.wa, *g.s_wa2, False)
    mixed = dot(hidden, g.wa[:, :, :, :, :384].reshape(1024, 384), NN)
    query = (mixed[:, :128] + g.qv[0:1]).astype(BF16)
    g.kv[:, :128] = mixed[:, 128:256].astype(BF16)
    g.kv[:, 128:] = (mixed[:, 256:] + g.qv[1:2]).astype(BF16)
    gather_start(g.kv, g.kvg, z, 4, z_peer, *g.s_kv)
    g.kvg[z] = g.kv[...]
    plane_one(g.wb, dp, *g.s_wb1, False)
    plane_one(g.wb, 1 - dp, *g.s_wb1, False)
    plane_two(g.wb, *g.s_wb2, True)
    gather_wait(g.kv, g.kvg, z, 4, z_peer, *g.s_kv)

    heads = []
    for h in range(2):
        key = g.kvg[:, :, 64 * h:64 * h + 64].reshape(1024, 64)
        value = g.kvg[:, :, 128 + 64 * h:192 + 64 * h].reshape(1024, 64)
        scores = dot(query[:, 64 * h:64 * h + 64], key, NT) * SCALE
        expo = jnp.exp(scores - jnp.max(scores, axis=-1, keepdims=True))
        prob = expo / jnp.sum(expo, axis=-1, keepdims=True)
        g.prob[h] = prob
        heads.append(dot(prob.astype(BF16), value, NN))
    attended = jnp.concatenate(heads, axis=1).astype(BF16)
    w_out = g.wa[:, :, :, :, 384:].reshape(1024, 128)
    g.branch_part[...] = dot(attended, w_out, NT).astype(BF16).reshape(8, 32, 1024)
    scatter_start(g.branch_part, g.branch_slots, r, 8, ring_peer, *g.s_branch)
    g.branch_slots[r] = g.branch_part[r]
    tokens(g.cot, g.cg, *g.s_cg, False)
    d_feed = (g.cg[...].astype(F32).reshape(256, 1024) * gate2).astype(BF16)
    g.d_feed[...] = d_feed
    plane_two(g.wb, *g.s_wb2, False)
    w_second = g.wb[:, :, :, :, 512:].reshape(1024, 512)
    g.d_act[...] = dot(d_feed, w_second, NN)
    g.z_own[...] = jnp.zeros_like(g.z_own)
    g.z_own[9:10] = jnp.sum(d_feed.astype(F32), axis=0, keepdims=True)
    scatter_wait(g.branch_part, g.branch_slots, r, 8, ring_peer, *g.s_branch)

    own_rows = pl.ds(pl.multiple_of(core * 32, 32), 32)
    x_own = g.xg[x, own_rows].astype(F32)
    branch = jnp.sum(g.branch_slots[...].astype(F32), axis=0) + g.ob[...].astype(F32)
    middle = x_own + gate1 * branch
    normed_two, inverse_two = normalize(middle)
    g.h2_own[...] = (normed_two * (1.0 + scale2) + shift2).astype(BF16)
    gather_start(g.h2_own, g.h2, r, 8, ring_peer, *g.s_h2)
    g.h2[r] = g.h2_own[...]
    gather_wait(g.h2_own, g.h2, r, 8, ring_peer, *g.s_h2)

    hidden_two = g.h2[...].reshape(256, 1024)
    w_first = g.wb[:, :, :, :, :512].reshape(1024, 512)
    before = dot(hidden_two, w_first, NN) + g.b1[...]
    square = before * before
    tanh = jnp.tanh(ROOT * before * (1.0 + 0.044715 * square))
    activated = (0.5 * before * (1.0 + tanh)).astype(BF16)
    slope = 0.5 * (1.0 + tanh) + (0.5 * ROOT) * before * (1.0 - tanh * tanh) * (
        1.0 + (3.0 * 0.044715) * square)
    d_before = (g.d_act[...] * slope).astype(BF16)
    g.dh2_part[...] = dot(d_before, w_first, NT).astype(BF16).reshape(8, 32, 1024)
    scatter_start(g.dh2_part, g.dh2_slots, r, 8, ring_peer, *g.s_dh2)
    g.dh2_slots[r] = g.dh2_part[r]
    g.feed_part[...] = dot(activated, w_second, NT).astype(BF16).reshape(8, 32, 1024)
    g.gb[:, :, :, :, :512] = dot(hidden_two, d_before, TN).astype(BF16).reshape(2, 4, 4, 32, 512)
    g.gb[:, :, :, :, 512:] = dot(d_feed, activated, TN).astype(BF16).reshape(2, 4, 4, 32, 512)
    reduce_one(g.gb, g.gb1, *g.s_gb1, True)
    g.z_own[10:11, :512] = jnp.sum(d_before.astype(F32), axis=0, keepdims=True)
    scatter_wait(g.dh2_part, g.dh2_slots, r, 8, ring_peer, *g.s_dh2)

    cot_own = g.cg[x, own_rows].astype(F32)
    d_hidden = jnp.sum(g.dh2_slots[...].astype(F32), axis=0)
    d_middle = cot_own + norm_back(d_hidden * (1.0 + scale2), normed_two, inverse_two)
    g.d_middle[...] = d_middle
    g.db_own[...] = (d_middle * gate1).astype(BF16)
    gather_start(g.db_own, g.db, r, 8, ring_peer, *g.s_db)
    scatter_start(g.feed_part, g.feed_slots, r, 8, ring_peer, *g.s_feed)
    g.db[r] = g.db_own[...]
    g.feed_slots[r] = g.feed_part[r]
    g.m_own[...] = jnp.zeros_like(g.m_own)
    g.m_own[2:3] = jnp.sum(d_middle * branch, axis=0, keepdims=True)
    g.m_own[3:4] = jnp.sum(d_hidden, axis=0, keepdims=True)
    g.m_own[4:5] = jnp.sum(d_hidden * normed_two, axis=0, keepdims=True)
    gather_wait(g.db_own, g.db, r, 8, ring_peer, *g.s_db)

    d_branch = g.db[...].reshape(256, 1024)
    d_attended = dot(d_branch, w_out, NN).astype(BF16)
    d_query, d_key, d_value = [], [], []
    for h in range(2):
        key = g.kvg[:, :, 64 * h:64 * h + 64].reshape(1024, 64)
        value = g.kvg[:, :, 128 + 64 * h:192 + 64 * h].reshape(1024, 64)
        d_one = d_attended[:, 64 * h:64 * h + 64]
        prob = g.prob[h]
        d_prob = dot(d_one, value, NT)
        d_scores = (prob * (d_prob - jnp.sum(prob * d_prob, axis=-1, keepdims=True))).astype(BF16)
        d_key.append(dot(d_scores, query[:, 64 * h:64 * h + 64], TN) * SCALE)
        d_value.append(dot(prob.astype(BF16), d_one, TN))
        d_query.append(dot(d_scores, key, NN) * SCALE)
    d_kv = jnp.concatenate(d_key + d_value, axis=1).astype(BF16)
    g.dkv_part[...] = d_kv.reshape(4, 256, 256)
    scatter_start(g.dkv_part, g.dkv_slots, z, 4, z_peer, *g.s_dkv)
    g.dkv_slots[z] = g.dkv_part[z]
    d_query = jnp.concatenate(d_query, axis=1).astype(BF16)
    g.ga[:, :, :, :, 384:] = dot(d_branch, attended, TN).astype(BF16).reshape(2, 4, 4, 32, 128)
    g.z_own[8:9] = jnp.sum(d_branch.astype(F32), axis=0, keepdims=True)
    g.z_own[10:11, 512:640] = jnp.sum(d_query.astype(F32), axis=0, keepdims=True)
    scatter_wait(g.feed_part, g.feed_slots, r, 8, ring_peer, *g.s_feed)
    feed = jnp.sum(g.feed_slots[...].astype(F32), axis=0) + g.b2[...].astype(F32)
    g.block_own[...] = (middle + gate2 * feed).astype(BF16)
    spread(g.block_own, g.block_out, *g.s_block, True)
    g.m_own[5:6] = jnp.sum(cot_own * feed, axis=0, keepdims=True)
    reduce_one(g.gb, g.gb1, *g.s_gb1, False)
    add_slots(g.gb1, g.gb2)
    reduce_two(g.gb2, g.gb3, *g.s_gb2, True)
    scatter_wait(g.dkv_part, g.dkv_slots, z, 4, z_peer, *g.s_dkv)

    d_kv = jnp.sum(g.dkv_slots[...].astype(F32), axis=0).astype(BF16)
    g.z_own[10:11, 640:768] = jnp.sum(d_kv[:, 128:].astype(F32), axis=0, keepdims=True)
    d_qkv = jnp.concatenate([d_query, d_kv], axis=1)
    d_part = dot(d_qkv, g.wa[:, :, :, :, :384].reshape(1024, 384), NT)
    g.dh_part[...] = d_part.astype(BF16).reshape(8, 32, 1024)
    scatter_start(g.dh_part, g.dh_slots, r, 8, ring_peer, *g.s_dh)
    g.m_own[0:1] = jnp.sum(d_part, axis=0, keepdims=True)
    g.m_own[1:2] = jnp.sum(d_part * g.normed[...], axis=0, keepdims=True)
    gather_start(g.m_own, g.m_slots, r, 8, ring_peer, *g.s_m)
    g.dh_slots[r] = g.dh_part[r]
    g.m_slots[r] = g.m_own[...]
    g.ga[:, :, :, :, :384] = dot(g.hidden[...], d_qkv, TN).astype(BF16).reshape(2, 4, 4, 32, 384)
    reduce_one(g.ga, g.ga1, *g.s_ga1, True)
    gather_wait(g.m_own, g.m_slots, r, 8, ring_peer, *g.s_m)
    g.z_own[0:8] = jnp.sum(g.m_slots[...], axis=0)
    gather_start(g.z_own, g.z_slots, z, 4, z_peer, *g.s_z)
    g.z_slots[z] = g.z_own[...]
    scatter_wait(g.dh_part, g.dh_slots, r, 8, ring_peer, *g.s_dh)

    x_normed, x_inverse = normalize(x_own)
    d_hidden = jnp.sum(g.dh_slots[...].astype(F32), axis=0)
    g.grad_own[...] = g.d_middle[...] + norm_back(d_hidden * (1.0 + scale1), x_normed, x_inverse)
    spread(g.grad_own, g.grad_out, *g.s_grad, True)
    gather_wait(g.z_own, g.z_slots, z, 4, z_peer, *g.s_z)
    g.y_own[...] = jnp.sum(g.z_slots[...], axis=0)
    gather_start(g.y_own, g.y_slots, y, 4, y_peer, *g.s_y)
    g.y_slots[y] = g.y_own[...]
    reduce_two(g.gb2, g.gb3, *g.s_gb2, False)
    add_slots(g.gb3, g.gbs)
    remote(g.gbs.at[1 - dp], g.gb_out.at[dp], *g.s_gbx, partner).start()
    g.gb_out[dp] = g.gbs[dp]
    reduce_one(g.ga, g.ga1, *g.s_ga1, False)
    add_slots(g.ga1, g.ga2)
    reduce_two(g.ga2, g.ga3, *g.s_ga2, True)
    gather_wait(g.y_own, g.y_slots, y, 4, y_peer, *g.s_y)

    total = jnp.sum(g.y_slots[...], axis=0)
    g.wide_out[...] = total[8:16]
    g.bias_own[...] = total[8:16]
    remote(g.bias_own, g.bias_out.at[dp], *g.s_bias, partner).start()
    g.bias_out[dp] = g.bias_own[...]
    g.dm[...] = jnp.zeros_like(g.dm)
    for k in range(6):
        for i in range(4):
            g.dm[i:i + 1, k * 1024:(k + 1) * 1024] = g.y_slots[i, k:k + 1]
        g.ada_bias_out[:, k * 1024:(k + 1) * 1024] = total[k:k + 1]
    chunk = dp * 16 + ctx
    columns = g.dm[:, pl.ds(pl.multiple_of(((3 * chunk) // 2) * 128, 128), 256)]
    columns = jnp.where(chunk % 2 == 1, pltpu.roll(columns, 192, 1), columns)
    g.cond_part[...] = dot(columns, g.ada[...].astype(F32), NT, lax.Precision.HIGHEST)
    gather_start(g.cond_part, g.cond_slots, ctx, 16, ctx_peer, *g.s_c)
    g.cond_slots[ctx] = g.cond_part[...]
    g.ada_out[...] = dot(g.cond8[...], columns, TN, lax.Precision.HIGHEST)
    gather_wait(g.cond_part, g.cond_slots, ctx, 16, ctx_peer, *g.s_c)
    g.cond_sum[...] = jnp.sum(g.cond_slots[...], axis=0)
    cond_copy = remote(g.cond_sum, g.cond_other, *g.s_cx, partner)
    cond_copy.start()
    reduce_two(g.ga2, g.ga3, *g.s_ga2, False)
    add_slots(g.ga3, g.gas)
    remote(g.gas.at[1 - dp], g.ga_out.at[dp], *g.s_gax, partner).start()
    g.ga_out[dp] = g.gas[dp]
    cond_copy.wait()
    g.cond_out[...] = g.cond_sum[...] + g.cond_other[...]
    remote(g.bias_own, g.bias_out.at[1 - dp], *g.s_bias, partner).wait()
    remote(g.gbs.at[1 - dp], g.gb_out.at[1 - dp], *g.s_gbx, partner).wait()
    remote(g.gas.at[1 - dp], g.ga_out.at[1 - dp], *g.s_gax, partner).wait()
    spread(g.block_own, g.block_out, *g.s_block, False)
    spread(g.grad_own, g.grad_out, *g.s_grad, False)


def on_device(
    latents, cond, ada_weight, ada_bias, qkv_weight, qv_bias, out_weight, out_bias,
    first_weight, first_bias, second_weight, second_bias, cotangent,
):
    dp, ctx, t, x, y, z, core = place()
    cond_slice = lax.dynamic_slice_in_dim(cond.astype(F32), t * 256, 256, 1)
    cond_act = jax.nn.silu(cond_slice).astype(BF16).astype(F32)
    empty = jnp.zeros((1, 256), F32)
    even = jnp.concatenate([cond_act[0:1], empty, cond_act[1:2], empty])
    odd = jnp.concatenate([empty, cond_act[0:1], empty, cond_act[1:2]])
    cond_block = jnp.pad(jnp.where(dp == 0, even, odd), ((0, 4), (0, 0)))
    ada_pad = jnp.pad(ada_weight[0], ((0, 0), (0, 64)))
    qkv_half = qkv_weight[0].reshape(32, 3, 2, 128).transpose(2, 0, 1, 3).reshape(2, 32, 384)
    out_half = out_weight[0].T.reshape(32, 2, 128).transpose(1, 0, 2)
    first_half = first_weight[0].reshape(32, 2, 512).transpose(1, 0, 2)
    second_half = second_weight[0].T.reshape(32, 2, 512).transpose(1, 0, 2)
    args = [
        latents, cotangent,
        jnp.concatenate([qkv_half, out_half], axis=2),
        jnp.concatenate([first_half, second_half], axis=2),
        cond_block, ada_pad, ada_bias,
        lax.dynamic_slice_in_dim(qv_bias[0].astype(F32), dp * 128, 128, 1),
        lax.dynamic_slice_in_dim(first_bias.astype(F32), dp * 512, 512, 1),
        out_bias, second_bias,
    ]
    outs = pl.pallas_call(
        block_kernel,
        out_shape=[shape(*one) for one in OUTPUTS.values()],
        in_specs=[VMEM] * len(args),
        out_specs=[VMEM] * len(OUTPUTS),
        scratch_shapes=[pltpu.VMEM(*one) for one in BUFFERS.values()]
        + [DMA(one) for one in SEMS.values() for _ in range(2)],
        compiler_params=pltpu.CompilerParams(
            collective_id=1, has_side_effects=True, vmem_limit_bytes=60 << 20
        ),
        name="block",
    )(*args)
    o = Refs()
    for name, out in zip(OUTPUTS, outs):
        setattr(o, name, out)
    sigmoid = jax.nn.sigmoid(cond_slice)
    sums = o.cond_out
    cond_mine = jnp.where(dp == 0, sums[0:3:2], sums[1:4:2])
    cond_grad = cond_mine * sigmoid * (1.0 + cond_slice * (1.0 - sigmoid))
    pair = o.bias_out[:, 2]
    ga, gb = o.ga_out, o.gb_out
    qkv_grad = ga[:, :, :384].reshape(2, 32, 3, 128).transpose(1, 2, 0, 3).reshape(1, 32, 3, 256)
    out_grad = ga[:, :, 384:].transpose(0, 2, 1).reshape(1, 256, 32)
    first_grad = gb[:, :, :512].transpose(1, 0, 2).reshape(1, 32, 1024)
    second_grad = gb[:, :, 512:].transpose(0, 2, 1).reshape(1, 1024, 32)
    return (
        o.block_out.reshape(2, 64, 1024),
        o.grad_out.reshape(2, 64, 1024),
        cond_grad,
        o.ada_out[None, :, :192],
        o.ada_bias_out,
        qkv_grad,
        pair[:, 512:768].reshape(2, 2, 128).transpose(1, 0, 2).reshape(1, 2, 256),
        out_grad,
        o.wide_out[0:1],
        first_grad,
        pair[:, :512].reshape(1, 1024),
        second_grad,
        o.wide_out[1:2],
    )


def solution(mesh):
    return jax.shard_map(
        on_device,
        mesh=mesh,
        in_specs=(
            P("dp", "context", None),
            P("dp", None),
            P(None, "tensor", ("dp", "context")),
            P(),
            P(None, ("dp", "context"), None, "tensor"),
            P(None, None, "tensor"),
            P(None, "tensor", ("dp", "context")),
            P(),
            P(None, ("dp", "context"), "tensor"),
            P(None, "tensor"),
            P(None, "tensor", ("dp", "context")),
            P(),
            P("dp", "context", None),
        ),
        out_specs=(
            P("dp", "context", None),
            P("dp", "context", None),
            P("dp", "tensor"),
            P(None, "tensor", ("dp", "context")),
            P(),
            P(None, ("dp", "context"), None, "tensor"),
            P(None, None, "tensor"),
            P(None, "tensor", ("dp", "context")),
            P(),
            P(None, ("dp", "context"), "tensor"),
            P(None, "tensor"),
            P(None, "tensor", ("dp", "context")),
            P(),
        ),
        check_vma=False,
    )
```

time: 327 us -> 156 us (0.48)
  Pallas kernels: 249 us -> 133 us
  matrix products: 27.2 us -> 0 us
  other arithmetic: 19.4 us -> 5.14 us
  local copies, waits for them, and re-layouts: 26.7 us -> 15.8 us
    pallas_call x7 -> x1, Pallas kernels: 249 us -> 133 us  [on_device(): pl.pallas_call(block_kernel, out_shape=[shape(*one) for one in OUTPUTS.va...]
    dot_general x19 -> x0, matrix products: 26.3 us -> none  [the longest x12 20.1 us: dot(): lax.dot_general(left, right, ((contract[0], contract[1]), ((), ())), pref...]
    reduce_sum x6 -> x0, other arithmetic: 5.3 us -> none  [the longest x1 1.99 us: normalize(): center = values - jnp.mean(values, axis=-1, keepdims=True)]
    convert_element_type x9 -> x1, other arithmetic: 5.82 us -> 1.26 us  [on_device(): first_bias.astype(F32)]
    concatenate x7 -> x2, other arithmetic: 5.42 us -> 1.3 us  [the longest x1 0.66 us: on_device(): jnp.concatenate([first_half, second_half], axis=2)]
where the time goes in v2:
time: 156 us; the launch traced here: 155 us
  Pallas kernels  133 us (85%)
  local copies, waits for them, and re-layouts  15.8 us (10%)
  other arithmetic  5.14 us (3%)
    pallas_call x1, Pallas kernels, on_device(): pl.pallas_call(block_kernel, out_shape=[shape(*one) for one in OUTPUTS.va...  133 us
    unnamed x30, local copies, waits for them, and re-layouts  5.76 us

profile of v2, /device:TPU:0, one launch (start us, length us, event | category | flops | bytes accessed | tf_op | source)
XLA Modules:
  0.0 154.9 jit_solution(10052812618866984541)
XLA Ops:
  0.6 0.0 copy-start
  0.7 0.0 copy-start.6
  0.7 0.7 fusion.6
  1.4 0.6 pad.8.refs_4_
  2.0 1.3 dynamic-slice_convert_fusion.refs_8_
  3.3 0.0 copy-start.10
  3.3 0.7 copy-done.10
  4.0 0.6 convert_bitcast_fusion.refs_7_
  4.6 0.0 copy-done.6
  4.6 0.0 copy-start.7
  4.6 0.8 copy-done.7
  5.4 0.0 copy-start.5
  5.4 0.7 pad_maximum_fusion.refs_3_
  6.1 0.3 copy-done.5
  6.4 0.1 copy.45
  6.5 0.0 copy-start.8
  6.5 0.7 pad.9.refs_5_
  7.2 0.1 copy-done.8
  7.4 0.1 reshape.67
  7.4 0.0 copy-done
  7.4 0.6 pad_maximum_fusion.1.refs_2_
  8.1 133.1 %block.1 = (bf16[2,2,32,1024]{3,2,1,0:T(8,128)(2,1)}, f32[2,2,32,1024]{3,2,1,0:T(8,128)}, f32[8,256]{1,0:T(8,128)}, f32[256,256]{1,0:T(8,128)}, f32[1,6144]{1,0:...) custom-call(bf16[2,64,1024]{2,1,0:T(8,128)(2,1)} %refs_0_.1, ...), custom_call_target="tpu_custom_call" | custom-call | tf_op jit(solution)/shard_map/block/pallas_call | solution.py:596
  141.2 0.7 slice.46
  141.9 0.7 slice.47
  142.6 1.3 fusion.1
  143.9 1.0 slice_bitcast_fusion.1
  144.9 0.1 copy.49
  145.0 0.8 reshape.77
  145.8 0.1 copy.50
  145.9 0.0 copy-start.4
  145.9 0.8 reshape.79
  146.7 0.1 copy-done.4
  146.9 0.1 copy.46
  146.9 0.0 copy-start.3
  146.9 0.7 reshape.73
  147.7 0.6 reshape.76
  148.3 0.8 slice.50
  149.2 0.6 copy.55
  149.8 0.6 reshape.74
  150.4 1.4 fusion.7
  151.8 0.0 copy-done.3
  151.8 0.0 copy-start.2
  151.9 0.0 copy-start.1
  151.9 0.8 copy.51
  152.7 0.1 copy-done.2
  152.8 0.7 copy.68
  153.5 0.0 copy-done.1
  153.5 0.0 copy-start.9
  153.5 0.8 copy.69
  154.3 0.0 copy-done.9
  154.3 0.6 copy.70
  (17 shorter events, 0.2 us)
Async XLA Ops:
  0.6 6.8 %copy-start = (bf16[1,256,32]{1,2,0:T(8,128)(2,1)S(1)}, bf16[1,256,32]{1,2,0:T(8,128)(2,1)}, u32[]{:S(2)}) copy-start(bf16[1,256,32]{1,2,0:T(8,128)(2,1)} %param.19) | copy-start | bytes 49156
  0.7 3.9 %copy-start.6 = (bf16[1,32,1024]{2,1,0:T(8,128)(2,1)S(1)}, bf16[1,32,1024]{2,1,0:T(8,128)(2,1)}, u32[]{:S(2)}) copy-start(bf16[1,32,1024]{2,1,0:T(8,128)(2,1)} %param.21) | copy-start | bytes 196612
  3.3 0.7 copy-start.10
  4.6 0.8 copy-start.7
  5.4 0.9 copy-start.5
  6.5 0.8 copy-start.8
  145.9 0.9 copy-start.4
  146.9 4.9 %copy-start.3 = (f32[256,256]{1,0:T(8,128)S(1)}, f32[256,256]{1,0:T(8,128)}, u32[]{:S(2)}) copy-start(f32[256,256]{1,0:T(8,128)} %get-tuple-element.25) | copy-start | bytes 786436
  151.8 1.0 copy-start.2
  151.9 1.6 %copy-start.1 = (f32[2,2,32,1024]{3,2,1,0:T(8,128)S(1)}, f32[2,2,32,1024]{3,2,1,0:T(8,128)}, u32[]{:S(2)}) copy-start(f32[2,2,32,1024]{3,2,1,0:T(8,128)} %get-tuple-element.23) | copy-start | bytes 1572868
  153.5 0.8 copy-start.9

commit v3 on v2

v3 whole, which is shorter than its diff:
```python
import math

import jax
import jax.numpy as jnp
from jax import lax
from jax.experimental import pallas as pl
from jax.experimental.pallas import tpu as pltpu
from jax.sharding import PartitionSpec as P

EPSILON = 1e-06
F32 = jnp.float32
BF16 = jnp.bfloat16
MESH = pl.DeviceIdType.MESH
VMEM = pl.BlockSpec(memory_space=pltpu.VMEM)
DMA = pltpu.SemaphoreType.DMA


def place():
    dp = lax.axis_index("dp")
    ctx = lax.axis_index("context")
    t = lax.axis_index("tensor")
    return dp, ctx, t, (t // 2) * 2 + dp, ctx % 4, ctx // 4, t % 2


def device(x, y, z, core):
    return (x % 2, z * 4 + y, (x // 2) * 2 + core)


def remote(src, dst, send, recv, target):
    return pltpu.make_async_remote_copy(
        src_ref=src, dst_ref=dst, send_sem=send, recv_sem=recv,
        device_id=target, device_id_type=MESH,
    )


def greet(targets):
    barrier = pltpu.get_barrier_semaphore()
    count = 0
    for first, last, target in targets:
        def one(k, carry, target=target):
            pl.semaphore_signal(barrier, inc=1, device_id=target(k), device_id_type=MESH)
            return carry
        lax.fori_loop(first, last, one, 0)
        count += last - first
    pl.semaphore_wait(barrier, count)


def z_peer(k):
    dp, ctx, t, x, y, z, core = place()
    return (dp, ((z + k) % 4) * 4 + y, t)


def y_peer(k):
    dp, ctx, t, x, y, z, core = place()
    return (dp, z * 4 + (y + k) % 4, t)


def x_peer(k):
    dp, ctx, t, x, y, z, core = place()
    return device((x + k) % 4, y, z, core)


def sibling():
    dp, ctx, t, x, y, z, core = place()
    return device(x, y, z, 1 - core)


def ring_peer(k):
    dp, ctx, t, x, y, z, core = place()
    r = (x * 2 + core + k) % 8
    return device(r // 2, y, z, r % 2)


def gather_start(own, slots, mine, n, peer, send, recv):
    def one(k, carry):
        remote(own, slots.at[mine], send.at[k], recv.at[mine], peer(k)).start()
        return carry
    lax.fori_loop(1, n, one, 0)


def gather_wait(own, slots, mine, n, peer, send, recv):
    def one(k, carry):
        other = (mine + k) % n
        copy = remote(own, slots.at[other], send.at[k], recv.at[other], peer(k))
        copy.wait_recv()
        copy.wait_send()
        return carry
    lax.fori_loop(1, n, one, 0)


def scatter_start(parts, slots, mine, n, peer, send, recv):
    def one(k, carry):
        other = (mine + k) % n
        remote(parts.at[other], slots.at[mine], send.at[k], recv.at[mine], peer(k)).start()
        return carry
    lax.fori_loop(1, n, one, 0)


def scatter_wait(parts, slots, mine, n, peer, send, recv):
    def one(k, carry):
        other = (mine + k) % n
        copy = remote(parts.at[other], slots.at[other], send.at[k], recv.at[other], peer(k))
        copy.wait_recv()
        copy.wait_send()
        return carry
    lax.fori_loop(1, n, one, 0)


def shape(dims, dtype):
    return jax.ShapeDtypeStruct(dims, dtype)


def normalize(values):
    center = values - jnp.mean(values, axis=-1, keepdims=True)
    inverse = lax.rsqrt(jnp.mean(center * center, axis=-1, keepdims=True) + EPSILON)
    return center * inverse, inverse


def norm_back(grad_hat, normed, inverse):
    first = jnp.mean(grad_hat, axis=-1, keepdims=True)
    second = jnp.mean(grad_hat * normed, axis=-1, keepdims=True)
    return inverse * (grad_hat - first - normed * second)


def dot(left, right, contract, precision=None):
    return lax.dot_general(
        left, right, (contract, ((), ())), precision=precision, preferred_element_type=F32
    )


NN = ((1,), (0,))
NT = ((1,), (1,))
TN = ((0,), (0,))
SCALE = 1.0 / math.sqrt(64)
ROOT = math.sqrt(2.0 / math.pi)
STEPS = (1, 3, 2)


def from_back(k):
    y, z = lax.axis_index("context") % 4, lax.axis_index("context") // 4
    return (y + 4 - k) % 4, (z + 4 - k) % 4


def plane_one(full, h, send, recv, start):
    dp, ctx, t, x, y, z, core = place()
    mine = full.at[h, z, y]
    for k in STEPS:
        target = (dp, ((z + h * k) % 4) * 4 + (y + (1 - h) * k) % 4, t)
        if start:
            remote(mine, mine, send.at[h, k], recv.at[h, k], target).start()
        else:
            slot = full.at[h, (z + h * (4 - k)) % 4, (y + (1 - h) * (4 - k)) % 4]
            remote(mine, slot, send.at[h, k], recv.at[h, k], target).wait()


def plane_two(full, send, recv, start):
    dp, ctx, t, x, y, z, core = place()
    for k in STEPS:
        by, bz = from_back(k)
        row, column = full.at[0, z], full.at[1, :, y]
        if start:
            remote(row, row, send.at[0, k], recv.at[0, k], z_peer(k)).start()
            remote(column, column, send.at[1, k], recv.at[1, k], y_peer(k)).start()
        else:
            remote(row, full.at[0, bz], send.at[0, k], recv.at[0, k], z_peer(k)).wait()
            remote(column, full.at[1, :, by], send.at[1, k], recv.at[1, k], y_peer(k)).wait()


def reduce_one(parts, slots, send, recv, start):
    dp, ctx, t, x, y, z, core = place()
    for k in STEPS:
        by, bz = from_back(k)
        row, column = parts.at[0, (z + k) % 4], parts.at[1, :, (y + k) % 4]
        to_row = slots.at[0, z if start else bz]
        to_column = slots.at[1, y if start else by]
        for copy in (remote(row, to_row, send.at[0, k], recv.at[0, k], z_peer(k)),
                     remote(column, to_column, send.at[1, k], recv.at[1, k], y_peer(k))):
            copy.start() if start else copy.wait()
    if start:
        slots[0, z] = parts[0, z]
        slots[1, y] = parts[1, :, y]


def reduce_two(parts, slots, send, recv, start):
    dp, ctx, t, x, y, z, core = place()
    for k in STEPS:
        by, bz = from_back(k)
        to_y = slots.at[0, y if start else by]
        to_z = slots.at[1, z if start else bz]
        for copy in (remote(parts.at[0, (y + k) % 4], to_y, send.at[0, k], recv.at[0, k], y_peer(k)),
                     remote(parts.at[1, (z + k) % 4], to_z, send.at[1, k], recv.at[1, k], z_peer(k))):
            copy.start() if start else copy.wait()
    if start:
        slots[0, y] = parts[0, y]
        slots[1, z] = parts[1, z]


def add_slots(slots, out):
    for h in range(2):
        total = slots[h, 0].astype(F32)
        for k in range(1, 4):
            total = total + slots[h, k].astype(F32)
        out[h] = total.astype(out.dtype)


def tokens(src, dst, send, recv, start):
    dp, ctx, t, x, y, z, core = place()
    own = src.at[t // 2, pl.ds(pl.multiple_of(core * 32, 32), 32)]
    for other in range(4):
        same = jnp.logical_and(x == y, x == other)
        copy = remote(own, dst.at[y, core], send.at[other], recv.at[y], device(other, x, z, core))
        if start:
            @pl.when(jnp.logical_not(same))
            def _():
                copy.start()

            @pl.when(same)
            def _():
                pltpu.make_async_copy(own, dst.at[y, core], recv.at[y]).start()
        else:
            @pl.when(jnp.logical_not(same))
            def _():
                copy.wait_send()

            remote(own, dst.at[other, core], send.at[other], recv.at[other],
                   (1 - dp, ctx, t)).wait_recv()


def tokens_relay(dst, send, recv, start):
    dp, ctx, t, x, y, z, core = place()
    mine = dst.at[:, core]
    if start:
        remote(mine, mine, send, recv, sibling()).start()
    else:
        remote(mine, dst.at[:, 1 - core], send, recv, sibling()).wait()


def ring_gather(own, slots, send, recv, start):
    dp, ctx, t, x, y, z, core = place()
    if start:
        for k in (2, 1, 3):
            remote(own, slots.at[x, core], send.at[0, k], recv.at[0, k], x_peer(k)).start()
        remote(own, slots.at[x, core], send.at[1, 0], recv.at[1, 0], sibling()).start()
        slots[x, core] = own[...]
        return
    for k in STEPS:
        slot = slots.at[(x + 4 - k) % 4, core]
        remote(own, slot, send.at[0, k], recv.at[0, k], x_peer(k)).wait()
        remote(slot, slot, send.at[1, k], recv.at[1, k], sibling()).start()
    for k in (0,) + STEPS:
        slot = slots.at[(x + 4 - k) % 4, 1 - core]
        remote(slot, slot, send.at[1, k], recv.at[1, k], sibling()).wait()


def ring_scatter(parts, halves, mid, slots, send, recv, step):
    dp, ctx, t, x, y, z, core = place()
    order = (2, 1, 3, 0)
    if step == 0:
        for k in order:
            to = (x + k) % 4
            remote(parts.at[to, 1 - core], halves.at[to], send.at[0, k], recv.at[0, k],
                   sibling()).start()
    elif step == 1:
        for k in order:
            to = (x + k) % 4
            remote(parts.at[to, 1 - core], halves.at[to], send.at[0, k], recv.at[0, k],
                   sibling()).wait()
            both = parts[to, core].astype(F32) + halves[to].astype(F32)
            if k == 0:
                slots[x] = both.astype(BF16)
            else:
                mid[to] = both.astype(BF16)
                remote(mid.at[to], slots.at[x], send.at[1, k], recv.at[1, k], x_peer(k)).start()
    else:
        for k in STEPS:
            remote(mid.at[(x + k) % 4], slots.at[(x + 4 - k) % 4], send.at[1, k], recv.at[1, k],
                   x_peer(k)).wait()


def spread(src, dst, send, recv, start):
    dp, ctx, t, x, y, z, core = place()
    for k in range(4):
        x_hi, other = k // 2, k % 2
        x_to = 2 * x_hi + y % 2
        same = jnp.logical_and(jnp.logical_and(x_to == x, x == y), core == other)
        slot = dst.at[y // 2, core]
        recv_sem = recv.at[(y // 2) * 2 + core]
        copy = remote(src, slot, send.at[k], recv_sem, device(x_to, x, z, other))
        if start:
            @pl.when(jnp.logical_not(same))
            def _():
                copy.start()

            @pl.when(same)
            def _():
                pltpu.make_async_copy(src, slot, recv_sem).start()
        else:
            @pl.when(jnp.logical_not(same))
            def _():
                copy.wait_send()

            remote(src, dst.at[k // 2, k % 2], send.at[k], recv.at[k],
                   (1 - dp, ctx, t)).wait_recv()


def tokens_target(k):
    dp, ctx, t, x, y, z, core = place()
    return device(k, x, z, core)


def tokens_source(k):
    dp, ctx, t, x, y, z, core = place()
    return device(y, k, z, core)


def spread_target(k):
    dp, ctx, t, x, y, z, core = place()
    return device(2 * (k // 2) + y % 2, x, z, k % 2)


def spread_source(k):
    dp, ctx, t, x, y, z, core = place()
    return device(y, 2 * (k // 2) + dp, z, k % 2)


def ctx_peer(k):
    dp, ctx, t, x, y, z, core = place()
    return (dp, (ctx + k) % 16, t)


INPUTS = dict(lat=0, cond=1, ada=2, ada_bias=3, qkv=4, qv=5, wo=6, ob=7, w1=8, b1=9, w2=10, b2=11, cot=12)
OUTPUTS = dict(
    block_out=((2, 2, 32, 1024), BF16),
    grad_out=((2, 2, 32, 1024), BF16),
    cond_out=((2, 256), F32),
    ada_out=((192, 256), F32),
    ada_bias_out=((1, 6144), F32),
    ga_out=((2, 32, 512), F32),
    gb_out=((2, 32, 1024), F32),
    bias_out=((2, 1, 1024), F32),
    wide_out=((2, 1024), F32),
)
RING = ((4, 2, 32, 1024), BF16)
FOUR = ((4, 32, 1024), BF16)
BUFFERS = dict(
    xg=RING, cg=RING,
    packa=((2, 32, 512), BF16), packb=((2, 32, 1024), BF16),
    wa=((2, 4, 4, 32, 512), BF16), wb=((2, 4, 4, 32, 1024), BF16),
    cond_a=((8, 256), F32), cond_b=((8, 256), F32), cond8=((8, 256), F32),
    part=((4, 256), F32), parts=((8, 4, 256), F32), pair=((4, 2, 256), F32),
    modg=((16, 2, 256), F32), flat=((1, 6144), F32),
    normed=((256, 1024), F32), hidden=((256, 1024), BF16),
    k_own=((256, 128), BF16), kg=((4, 256, 128), BF16),
    v_own=((256, 128), BF16), vg=((4, 256, 128), BF16), prob=((2, 256, 1024), F32),
    branch_part=RING, branch_half=FOUR, branch_mid=FOUR, branch_slots=FOUR,
    h2_own=((32, 1024), BF16), h2=RING,
    d_feed=((256, 1024), BF16), d_act=((256, 512), F32),
    dh2_part=RING, dh2_half=FOUR, dh2_mid=FOUR, dh2_slots=FOUR,
    feed_part=RING, feed_half=FOUR, feed_mid=FOUR, feed_slots=FOUR,
    db_own=((32, 1024), BF16), db=RING,
    block_own=((32, 1024), BF16), d_middle=((32, 1024), F32),
    dk_part=((4, 256, 128), BF16), dk_slots=((4, 256, 128), BF16),
    dv_part=((4, 256, 128), BF16), dv_slots=((4, 256, 128), BF16),
    dh_part=RING, dh_half=FOUR, dh_mid=FOUR, dh_slots=FOUR,
    grad_own=((32, 1024), BF16),
    m_own=((4, 1024), F32), m_slots=((8, 4, 1024), F32),
    z_own=((8, 1024), F32), z_slots=((4, 8, 1024), F32),
    y_own=((8, 1024), F32), y_slots=((4, 8, 1024), F32),
    n_own=((2, 1024), F32), n_slots=((8, 2, 1024), F32),
    l_own=((4, 1024), F32), l_slots=((16, 4, 1024), F32),
    dm=((8, 6144), F32), bias_own=((1, 1024), F32),
    cond_part=((8, 256), F32), cond_slots=((16, 8, 256), F32), cond_sum=((8, 256), F32),
    cond_other=((8, 256), F32),
    ga=((2, 4, 4, 32, 512), BF16), ga1=((2, 4, 4, 32, 512), BF16),
    ga2=((2, 4, 32, 512), BF16), ga3=((2, 4, 32, 512), BF16), gas=((2, 32, 512), F32),
    gb=((2, 4, 4, 32, 1024), BF16), gb1=((2, 4, 4, 32, 1024), BF16),
    gb2=((2, 4, 32, 1024), BF16), gb3=((2, 4, 32, 1024), BF16), gbs=((2, 32, 1024), F32),
)
SEMS = dict(
    s_cond=(), s_xa=(), s_xb=(), s_xg=(4,), s_xr=(), s_cg=(4,), s_cr=(),
    s_wa1=(2, 4), s_wa2=(2, 4), s_wb1=(2, 4), s_wb2=(2, 4),
    s_mod=(8,), s_mod2=(16,), s_k=(4,), s_v=(4,),
    s_branch=(2, 4), s_h2=(2, 4), s_dh2=(2, 4), s_feed=(2, 4), s_db=(2, 4),
    s_block=(4,), s_dk=(4,), s_dv=(4,), s_dh=(2, 4), s_grad=(4,),
    s_m=(8,), s_z=(4,), s_y=(4,), s_n=(8,), s_l=(16,), s_bias=(), s_c=(16,), s_cx=(),
    s_ga1=(2, 4), s_ga2=(2, 4), s_gb1=(2, 4), s_gb2=(2, 4), s_gax=(), s_gbx=(),
)


class Refs:
    pass


def block_kernel(*refs):
    g = Refs()
    names = list(INPUTS) + list(OUTPUTS) + list(BUFFERS)
    for name, ref in zip(names, refs):
        setattr(g, name, ref)
    sems = refs[len(names):]
    for i, name in enumerate(SEMS):
        setattr(g, name, (sems[2 * i], sems[2 * i + 1]))
    dp, ctx, t, x, y, z, core = place()
    r = x * 2 + core
    partner = (1 - dp, ctx, t)

    greet([(1, 8, ring_peer), (1, 16, ctx_peer)] + [(0, 4, f) for f in (
        tokens_target, tokens_source, spread_target, spread_source)])

    cond_slice = g.cond[:, pl.ds(pl.multiple_of(t * 256, 256), 256)].astype(F32)
    sigmoid = 1.0 / (1.0 + jnp.exp(-cond_slice))
    cond_act = (cond_slice * sigmoid).astype(BF16).astype(F32)
    rows = lax.broadcasted_iota(jnp.int32, (8, 256), 0)
    g.cond_a[...] = jnp.where(rows == dp, cond_act[0:1], jnp.where(rows == dp + 2, cond_act[1:2], 0.0))
    cond_copy = remote(g.cond_a, g.cond_b, *g.s_cond, partner)
    cond_copy.start()
    tokens(g.lat, g.xg, *g.s_xg, True)
    for h in range(2):
        for k in range(3):
            g.packa[h, :, 128 * k:128 * k + 128] = g.qkv[k, :, 128 * h:128 * h + 128]
        g.packa[h, :, 384:] = g.wo[:, 128 * h:128 * h + 128]
    across_a = remote(g.packa.at[1 - dp], g.wa.at[dp, z, y], *g.s_xa, partner)
    across_a.start()
    g.wa[dp, z, y] = g.packa[dp]
    plane_one(g.wa, dp, *g.s_wa1, True)
    cond_copy.wait()
    g.cond8[...] = g.cond_a[...] + g.cond_b[...]
    g.part[:, :192] = dot(g.cond8[...].astype(BF16), g.ada[...], NT)[:4]
    gather_start(g.part, g.parts, r, 8, ring_peer, *g.s_mod)
    g.parts[r] = g.part[...]
    for h in range(2):
        g.packb[h, :, :512] = g.w1[0, :, 512 * h:512 * h + 512]
        g.packb[h, :, 512:] = g.w2[:, 512 * h:512 * h + 512]
    across_b = remote(g.packb.at[1 - dp], g.wb.at[dp, z, y], *g.s_xb, partner)
    across_b.start()
    g.wb[dp, z, y] = g.packb[dp]
    remote(g.packa.at[1 - dp], g.wa.at[1 - dp, z, y], *g.s_xa, partner).wait()
    plane_one(g.wa, 1 - dp, *g.s_wa1, True)
    gather_wait(g.part, g.parts, r, 8, ring_peer, *g.s_mod)
    for c in range(2):
        both = (g.parts[2 * c] + g.parts[2 * c + 1]) + (g.parts[2 * c + 4] + g.parts[2 * c + 5])
        for i in range(4):
            g.pair[i, c:c + 1, :192] = both[i:i + 1, :192]

    def mod_start(k, carry):
        remote(g.pair.at[(ctx + k) % 4], g.modg.at[ctx], g.s_mod2[0].at[k], g.s_mod2[1].at[ctx],
               ctx_peer(k)).start()
        return carry
    lax.fori_loop(1, 16, mod_start, 0)
    g.modg[ctx] = g.pair[y]
    tokens(g.lat, g.xg, *g.s_xg, False)
    tokens_relay(g.xg, *g.s_xr, True)
    plane_one(g.wa, dp, *g.s_wa1, False)
    plane_one(g.wa, 1 - dp, *g.s_wa1, False)
    plane_two(g.wa, *g.s_wa2, True)
    tokens_relay(g.xg, *g.s_xr, False)
    normed, _ = normalize(g.xg[...].astype(F32).reshape(256, 1024))
    g.normed[...] = normed
    plane_one(g.wb, dp, *g.s_wb1, True)
    remote(g.packb.at[1 - dp], g.wb.at[1 - dp, z, y], *g.s_xb, partner).wait()
    plane_one(g.wb, 1 - dp, *g.s_wb1, True)
    tokens(g.cot, g.cg, *g.s_cg, True)

    def mod_wait(k, carry):
        other = (ctx + k) % 16
        remote(g.pair.at[0], g.modg.at[other], g.s_mod2[0].at[k], g.s_mod2[1].at[other],
               ctx_peer(k)).wait()
        return carry
    lax.fori_loop(1, 16, mod_wait, 0)
    for p in range(16):
        c, first = p // 8, (2 * p) % 16
        both = jnp.concatenate(
            [g.modg[first, c:c + 1, :192], g.modg[first + 1, c:c + 1, :192]], axis=1)
        g.flat[:, 384 * p:384 * p + 384] = both + g.ada_bias[:, 384 * p:384 * p + 384].astype(F32)
    shift1, scale1, gate1, shift2, scale2, gate2 = [
        g.flat[:, k * 1024:(k + 1) * 1024] for k in range(6)]
    hidden = (g.normed[...] * (1.0 + scale1) + shift1).astype(BF16)
    g.hidden[...] = hidden
    plane_two(g.wa, *g.s_wa2, False)
    mixed = dot(hidden, g.wa[:, :, :, :, :384].reshape(1024, 384), NN)
    qv = g.qv[0, :, pl.ds(pl.multiple_of(dp * 128, 128), 128)].astype(F32)
    g.k_own[...] = mixed[:, 128:256].astype(BF16)
    gather_start(g.k_own, g.kg, z, 4, z_peer, *g.s_k)
    g.v_own[...] = (mixed[:, 256:] + qv[1:2]).astype(BF16)
    gather_start(g.v_own, g.vg, z, 4, z_peer, *g.s_v)
    query = (mixed[:, :128] + qv[0:1]).astype(BF16)
    g.kg[z] = g.k_own[...]
    g.vg[z] = g.v_own[...]
    plane_one(g.wb, dp, *g.s_wb1, False)
    plane_one(g.wb, 1 - dp, *g.s_wb1, False)
    plane_two(g.wb, *g.s_wb2, True)
    gather_wait(g.k_own, g.kg, z, 4, z_peer, *g.s_k)
    for h in range(2):
        key = g.kg[:, :, 64 * h:64 * h + 64].reshape(1024, 64)
        scores = dot(query[:, 64 * h:64 * h + 64], key, NT) * SCALE
        expo = jnp.exp(scores - jnp.max(scores, axis=-1, keepdims=True))
        g.prob[h] = expo / jnp.sum(expo, axis=-1, keepdims=True)
    gather_wait(g.v_own, g.vg, z, 4, z_peer, *g.s_v)
    heads = []
    for h in range(2):
        value = g.vg[:, :, 64 * h:64 * h + 64].reshape(1024, 64)
        heads.append(dot(g.prob[h].astype(BF16), value, NN))
    attended = jnp.concatenate(heads, axis=1).astype(BF16)
    w_out = g.wa[:, :, :, :, 384:].reshape(1024, 128)
    g.branch_part[...] = dot(attended, w_out, NT).astype(BF16).reshape(4, 2, 32, 1024)
    branch_ring = (g.branch_part, g.branch_half, g.branch_mid, g.branch_slots, *g.s_branch)
    ring_scatter(*branch_ring, 0)
    ring_scatter(*branch_ring, 1)
    tokens(g.cot, g.cg, *g.s_cg, False)
    tokens_relay(g.cg, *g.s_cr, True)
    tokens_relay(g.cg, *g.s_cr, False)
    d_feed = (g.cg[...].astype(F32).reshape(256, 1024) * gate2).astype(BF16)
    g.d_feed[...] = d_feed
    plane_two(g.wb, *g.s_wb2, False)
    w_second = g.wb[:, :, :, :, 512:].reshape(1024, 512)
    g.d_act[...] = dot(d_feed, w_second, NN)
    g.z_own[...] = jnp.zeros_like(g.z_own)
    g.z_own[5:6] = jnp.sum(d_feed.astype(F32), axis=0, keepdims=True)
    ring_scatter(*branch_ring, 2)

    x_own = g.xg[x, core].astype(F32)
    branch = jnp.sum(g.branch_slots[...].astype(F32), axis=0) + g.ob[...].astype(F32)
    middle = x_own + gate1 * branch
    normed_two, inverse_two = normalize(middle)
    g.h2_own[...] = (normed_two * (1.0 + scale2) + shift2).astype(BF16)
    ring_gather(g.h2_own, g.h2, *g.s_h2, True)
    ring_gather(g.h2_own, g.h2, *g.s_h2, False)

    hidden_two = g.h2[...].reshape(256, 1024)
    w_first = g.wb[:, :, :, :, :512].reshape(1024, 512)
    bias_first = g.b1[:, pl.ds(pl.multiple_of(dp * 512, 512), 512)].astype(F32)
    before = dot(hidden_two, w_first, NN) + bias_first
    square = before * before
    tanh = jnp.tanh(ROOT * before * (1.0 + 0.044715 * square))
    slope = 0.5 * (1.0 + tanh) + (0.5 * ROOT) * before * (1.0 - tanh * tanh) * (
        1.0 + (3.0 * 0.044715) * square)
    d_before = (g.d_act[...] * slope).astype(BF16)
    g.dh2_part[...] = dot(d_before, w_first, NT).astype(BF16).reshape(4, 2, 32, 1024)
    dh2_ring = (g.dh2_part, g.dh2_half, g.dh2_mid, g.dh2_slots, *g.s_dh2)
    ring_scatter(*dh2_ring, 0)
    activated = (0.5 * before * (1.0 + tanh)).astype(BF16)
    ring_scatter(*dh2_ring, 1)
    g.feed_part[...] = dot(activated, w_second, NT).astype(BF16).reshape(4, 2, 32, 1024)
    g.gb[:, :, :, :, :512] = dot(hidden_two, d_before, TN).astype(BF16).reshape(2, 4, 4, 32, 512)
    g.gb[:, :, :, :, 512:] = dot(d_feed, activated, TN).astype(BF16).reshape(2, 4, 4, 32, 512)
    reduce_one(g.gb, g.gb1, *g.s_gb1, True)
    g.z_own[6:7, :512] = jnp.sum(d_before.astype(F32), axis=0, keepdims=True)
    ring_scatter(*dh2_ring, 2)

    cot_own = g.cg[x, core].astype(F32)
    d_hidden = jnp.sum(g.dh2_slots[...].astype(F32), axis=0)
    d_middle = cot_own + norm_back(d_hidden * (1.0 + scale2), normed_two, inverse_two)
    g.d_middle[...] = d_middle
    g.db_own[...] = (d_middle * gate1).astype(BF16)
    ring_gather(g.db_own, g.db, *g.s_db, True)
    feed_ring = (g.feed_part, g.feed_half, g.feed_mid, g.feed_slots, *g.s_feed)
    ring_scatter(*feed_ring, 0)
    g.m_own[0:1] = jnp.sum(d_middle * branch, axis=0, keepdims=True)
    g.m_own[1:2] = jnp.sum(d_hidden, axis=0, keepdims=True)
    g.m_own[2:3] = jnp.sum(d_hidden * normed_two, axis=0, keepdims=True)
    ring_gather(g.db_own, g.db, *g.s_db, False)
    ring_scatter(*feed_ring, 1)

    d_branch = g.db[...].reshape(256, 1024)
    d_attended = dot(d_branch, w_out, NN).astype(BF16)
    d_one = [d_attended[:, 64 * h:64 * h + 64] for h in range(2)]
    d_value = [dot(g.prob[h].astype(BF16), d_one[h], TN) for h in range(2)]
    g.dv_part[...] = jnp.concatenate(d_value, axis=1).astype(BF16).reshape(4, 256, 128)
    scatter_start(g.dv_part, g.dv_slots, z, 4, z_peer, *g.s_dv)
    g.dv_slots[z] = g.dv_part[z]
    d_query, d_key = [], []
    for h in range(2):
        key = g.kg[:, :, 64 * h:64 * h + 64].reshape(1024, 64)
        value = g.vg[:, :, 64 * h:64 * h + 64].reshape(1024, 64)
        prob = g.prob[h]
        d_prob = dot(d_one[h], value, NT)
        d_scores = (prob * (d_prob - jnp.sum(prob * d_prob, axis=-1, keepdims=True))).astype(BF16)
        d_key.append(dot(d_scores, query[:, 64 * h:64 * h + 64], TN) * SCALE)
        d_query.append(dot(d_scores, key, NN) * SCALE)
    g.dk_part[...] = jnp.concatenate(d_key, axis=1).astype(BF16).reshape(4, 256, 128)
    scatter_start(g.dk_part, g.dk_slots, z, 4, z_peer, *g.s_dk)
    g.dk_slots[z] = g.dk_part[z]
    d_query = jnp.concatenate(d_query, axis=1).astype(BF16)
    ring_scatter(*feed_ring, 2)
    feed = jnp.sum(g.feed_slots[...].astype(F32), axis=0) + g.b2[...].astype(F32)
    g.block_own[...] = (middle + gate2 * feed).astype(BF16)
    spread(g.block_own, g.block_out, *g.s_block, True)
    g.m_own[3:4] = jnp.sum(cot_own * feed, axis=0, keepdims=True)
    gather_start(g.m_own, g.m_slots, r, 8, ring_peer, *g.s_m)
    g.m_slots[r] = g.m_own[...]
    g.ga[:, :, :, :, 384:] = dot(d_branch, attended, TN).astype(BF16).reshape(2, 4, 4, 32, 128)
    g.z_own[4:5] = jnp.sum(d_branch.astype(F32), axis=0, keepdims=True)
    g.z_own[6:7, 512:640] = jnp.sum(d_query.astype(F32), axis=0, keepdims=True)
    reduce_one(g.gb, g.gb1, *g.s_gb1, False)
    add_slots(g.gb1, g.gb2)
    scatter_wait(g.dv_part, g.dv_slots, z, 4, z_peer, *g.s_dv)
    scatter_wait(g.dk_part, g.dk_slots, z, 4, z_peer, *g.s_dk)
    reduce_two(g.gb2, g.gb3, *g.s_gb2, True)

    d_keys = jnp.sum(g.dk_slots[...].astype(F32), axis=0).astype(BF16)
    d_values = jnp.sum(g.dv_slots[...].astype(F32), axis=0).astype(BF16)
    d_qkv = jnp.concatenate([d_query, d_keys, d_values], axis=1)
    d_part = dot(d_qkv, g.wa[:, :, :, :, :384].reshape(1024, 384), NT)
    g.dh_part[...] = d_part.astype(BF16).reshape(4, 2, 32, 1024)
    dh_ring = (g.dh_part, g.dh_half, g.dh_mid, g.dh_slots, *g.s_dh)
    ring_scatter(*dh_ring, 0)
    g.n_own[0:1] = jnp.sum(d_part, axis=0, keepdims=True)
    g.n_own[1:2] = jnp.sum(d_part * g.normed[...], axis=0, keepdims=True)
    ring_scatter(*dh_ring, 1)
    gather_start(g.n_own, g.n_slots, r, 8, ring_peer, *g.s_n)
    g.n_slots[r] = g.n_own[...]
    g.ga[:, :, :, :, :384] = dot(g.hidden[...], d_qkv, TN).astype(BF16).reshape(2, 4, 4, 32, 384)
    reduce_one(g.ga, g.ga1, *g.s_ga1, True)
    gather_wait(g.m_own, g.m_slots, r, 8, ring_peer, *g.s_m)
    g.z_own[0:4] = jnp.sum(g.m_slots[...], axis=0)
    gather_start(g.z_own, g.z_slots, z, 4, z_peer, *g.s_z)
    g.z_slots[z] = g.z_own[...]
    gather_wait(g.n_own, g.n_slots, r, 8, ring_peer, *g.s_n)
    g.l_own[0:2] = jnp.sum(g.n_slots[...], axis=0)
    g.l_own[2:4] = jnp.zeros((2, 1024), F32)
    g.l_own[2:3, :128] = jnp.sum(d_values.astype(F32), axis=0, keepdims=True)
    gather_start(g.l_own, g.l_slots, ctx, 16, ctx_peer, *g.s_l)
    g.l_slots[ctx] = g.l_own[...]
    ring_scatter(*dh_ring, 2)

    x_normed, x_inverse = normalize(x_own)
    d_hidden = jnp.sum(g.dh_slots[...].astype(F32), axis=0)
    grad = g.d_middle[...] + norm_back(d_hidden * (1.0 + scale1), x_normed, x_inverse)
    g.grad_own[...] = grad.astype(BF16)
    spread(g.grad_own, g.grad_out, *g.s_grad, True)
    gather_wait(g.z_own, g.z_slots, z, 4, z_peer, *g.s_z)
    g.y_own[...] = jnp.sum(g.z_slots[...], axis=0)
    gather_start(g.y_own, g.y_slots, y, 4, y_peer, *g.s_y)
    g.y_slots[y] = g.y_own[...]
    reduce_two(g.gb2, g.gb3, *g.s_gb2, False)
    add_slots(g.gb3, g.gbs)
    remote(g.gbs.at[1 - dp], g.gb_out.at[dp], *g.s_gbx, partner).start()
    g.gb_out[dp] = g.gbs[dp]
    reduce_one(g.ga, g.ga1, *g.s_ga1, False)
    add_slots(g.ga1, g.ga2)
    reduce_two(g.ga2, g.ga3, *g.s_ga2, True)
    gather_wait(g.l_own, g.l_slots, ctx, 16, ctx_peer, *g.s_l)
    gather_wait(g.y_own, g.y_slots, y, 4, y_peer, *g.s_y)

    late = jnp.sum(g.l_slots[...].reshape(4, 4, 4, 1024), axis=0)
    early = jnp.sum(g.y_slots[...], axis=0)
    g.wide_out[...] = early[4:6]
    g.bias_own[:, :640] = early[6:7, :640]
    g.bias_own[:, 640:768] = jnp.sum(late[:, 2], axis=0, keepdims=True)[:, :128]
    g.bias_own[:, 768:] = jnp.zeros((1, 256), F32)
    remote(g.bias_own, g.bias_out.at[dp], *g.s_bias, partner).start()
    g.bias_out[dp] = g.bias_own[...]
    g.dm[...] = jnp.zeros_like(g.dm)
    for k in range(6):
        for i in range(4):
            row = late[i, k:k + 1] if k < 2 else g.y_slots[i, k - 2:k - 1]
            g.dm[i:i + 1, k * 1024:(k + 1) * 1024] = row
    g.ada_bias_out[...] = jnp.sum(g.dm[...], axis=0, keepdims=True)
    chunk = dp * 16 + ctx
    columns = g.dm[:, pl.ds(pl.multiple_of(((3 * chunk) // 2) * 128, 128), 256)]
    columns = jnp.where(chunk % 2 == 1, pltpu.roll(columns, 192, 1), columns)[:, :192]
    g.cond_part[...] = dot(columns, g.ada[...].astype(F32), NN, lax.Precision.HIGHEST)
    gather_start(g.cond_part, g.cond_slots, ctx, 16, ctx_peer, *g.s_c)
    g.cond_slots[ctx] = g.cond_part[...]
    g.ada_out[...] = dot(columns, g.cond8[...], TN, lax.Precision.HIGHEST)
    gather_wait(g.cond_part, g.cond_slots, ctx, 16, ctx_peer, *g.s_c)
    g.cond_sum[...] = jnp.sum(g.cond_slots[...], axis=0)
    cond_copy = remote(g.cond_sum, g.cond_other, *g.s_cx, partner)
    cond_copy.start()
    reduce_two(g.ga2, g.ga3, *g.s_ga2, False)
    add_slots(g.ga3, g.gas)
    remote(g.gas.at[1 - dp], g.ga_out.at[dp], *g.s_gax, partner).start()
    g.ga_out[dp] = g.gas[dp]
    cond_copy.wait()
    g.cond_part[...] = g.cond_sum[...] + g.cond_other[...]
    slope = sigmoid * (1.0 + cond_slice * (1.0 - sigmoid))
    for i in range(2):
        g.cond_out[i:i + 1] = g.cond_part[pl.ds(2 * i + dp, 1)] * slope[i:i + 1]
    remote(g.bias_own, g.bias_out.at[1 - dp], *g.s_bias, partner).wait()
    remote(g.gbs.at[1 - dp], g.gb_out.at[1 - dp], *g.s_gbx, partner).wait()
    remote(g.gas.at[1 - dp], g.ga_out.at[1 - dp], *g.s_gax, partner).wait()
    spread(g.block_own, g.block_out, *g.s_block, False)
    spread(g.grad_own, g.grad_out, *g.s_grad, False)


def unpack_kernel(block, grad, cond, ada, ada_bias, ga, gb, bias, wide,
                  block_out, grad_out, cond_out, ada_out, ada_bias_out, qkv_out, qv_out,
                  wo_out, ob_out, w1_out, b1_out, w2_out, b2_out):
    block_out[...] = block[...].reshape(2, 64, 1024)
    grad_out[...] = grad[...].astype(F32).reshape(2, 64, 1024)
    cond_out[...] = cond[...]
    ada_out[...] = ada[...]
    ada_bias_out[...] = ada_bias[...]
    for h in range(2):
        for k in range(3):
            qkv_out[k, :, 128 * h:128 * h + 128] = ga[h, :, 128 * k:128 * k + 128]
        for k in range(2):
            qv_out[0, k:k + 1, 128 * h:128 * h + 128] = bias[h, :, 512 + 128 * k:640 + 128 * k]
        wo_out[:, 128 * h:128 * h + 128] = ga[h, :, 384:]
        w1_out[0, :, 512 * h:512 * h + 512] = gb[h, :, :512]
        w2_out[:, 512 * h:512 * h + 512] = gb[h, :, 512:]
        b1_out[:, 512 * h:512 * h + 512] = bias[h, :, :512]
    ob_out[...] = wide[0:1]
    b2_out[...] = wide[1:2]


def on_device(
    latents, cond, ada_weight, ada_bias, qkv_weight, qv_bias, out_weight, out_bias,
    first_weight, first_bias, second_weight, second_bias, cotangent,
):
    args = [
        latents, cond, ada_weight[0].T, ada_bias, qkv_weight[0].transpose(1, 0, 2), qv_bias,
        out_weight[0].T, out_bias, first_weight, first_bias, second_weight[0].T, second_bias,
        cotangent,
    ]
    outs = pl.pallas_call(
        block_kernel,
        out_shape=[shape(*one) for one in OUTPUTS.values()],
        in_specs=[VMEM] * len(args),
        out_specs=[VMEM] * len(OUTPUTS),
        scratch_shapes=[pltpu.VMEM(*one) for one in BUFFERS.values()]
        + [DMA(one) for one in SEMS.values() for _ in range(2)],
        compiler_params=pltpu.CompilerParams(
            collective_id=1, has_side_effects=True, vmem_limit_bytes=56 << 20
        ),
        name="block",
    )(*args)
    final = [
        shape((2, 64, 1024), BF16), shape((2, 64, 1024), F32), shape((2, 256), F32),
        shape((192, 256), F32), shape((1, 6144), F32), shape((3, 32, 256), F32),
        shape((1, 2, 256), F32), shape((32, 256), F32), shape((1, 1024), F32),
        shape((1, 32, 1024), F32), shape((1, 1024), F32), shape((32, 1024), F32),
        shape((1, 1024), F32),
    ]
    results = pl.pallas_call(
        unpack_kernel, out_shape=final, in_specs=[VMEM] * len(outs), out_specs=[VMEM] * len(final),
        name="unpack",
    )(*outs)
    results = list(results)
    for k in (3, 7, 11):
        results[k] = results[k].T[None]
    results[5] = results[5].transpose(1, 0, 2)[None]
    return tuple(results)


def solution(mesh):
    return jax.shard_map(
        on_device,
        mesh=mesh,
        in_specs=(
            P("dp", "context", None),
            P("dp", None),
            P(None, "tensor", ("dp", "context")),
            P(),
            P(None, ("dp", "context"), None, "tensor"),
            P(None, None, "tensor"),
            P(None, "tensor", ("dp", "context")),
            P(),
            P(None, ("dp", "context"), "tensor"),
            P(None, "tensor"),
            P(None, "tensor", ("dp", "context")),
            P(),
            P("dp", "context", None),
        ),
        out_specs=(
            P("dp", "context", None),
            P("dp", "context", None),
            P("dp", "tensor"),
            P(None, "tensor", ("dp", "context")),
            P(),
            P(None, ("dp", "context"), None, "tensor"),
            P(None, None, "tensor"),
            P(None, "tensor", ("dp", "context")),
            P(),
            P(None, ("dp", "context"), "tensor"),
            P(None, "tensor"),
            P(None, "tensor", ("dp", "context")),
            P(),
        ),
        check_vma=False,
    )
```

time: 156 us -> 115 us (0.74)
  Pallas kernels: 133 us -> 114 us
  local copies, waits for them, and re-layouts: 15.8 us -> 0 us
  other arithmetic: 5.14 us -> 0 us
    pallas_call x1, Pallas kernels: 133 us -> 112 us  [on_device(): pl.pallas_call(block_kernel, out_shape=[shape(*one) for one in OUTPUTS.va...]
    unnamed x30 -> x0, local copies, waits for them, and re-layouts: 5.76 us -> none
    slice x7 -> x0, local copies, waits for them, and re-layouts: 3.72 us -> none  [the longest x1 1.44 us: on_device(): o.wide_out[1:2]]
    reshape x8 -> x0, local copies, waits for them, and re-layouts: 3.59 us -> none  [the longest x1 0.77 us: on_device(): first_grad = gb[:, :, :512].transpose(1, 0, 2).reshape(1, 32, 1024)]
    pallas_call x0 -> x1, Pallas kernels: none -> 2.43 us  [on_device(): pl.pallas_call(unpack_kernel, out_shape=final, in_specs=[VMEM] * len(outs...]
    convert_element_type x2 -> x0, other arithmetic: 1.98 us -> none  [the longest x1 1.26 us: on_device(): first_bias.astype(F32)]
where the time goes in v3:
time: 115 us
  Pallas kernels  114 us (99%)
    pallas_call x1, Pallas kernels, on_device(): pl.pallas_call(block_kernel, out_shape=[shape(*one) for one in OUTPUTS.va...  112 us
    pallas_call x1, Pallas kernels, on_device(): pl.pallas_call(unpack_kernel, out_shape=final, in_specs=[VMEM] * len(outs...  2.43 us

profile of v3, /device:TPU:0, one launch (start us, length us, event | category | flops | bytes accessed | tf_op | source)
XLA Modules:
  0.0 115.0 jit_solution(4678861620500117830)
XLA Ops:
  0.6 111.9 %block.1 = (bf16[2,2,32,1024]{3,2,1,0:T(8,128)(2,1)}, bf16[2,2,32,1024]{3,2,1,0:T(8,128)(2,1)}, f32[2,256]{1,0:T(2,128)}, f32[192,256]{1,0:T(8,128)}, f32[1,6144...) custom-call(bf16[2,64,1024]{2,1,0:T(8,128)(2,1)} %refs_0_.1, ...), custom_call_target="tpu_custom_call" | custom-call | tf_op jit(solution)/shard_map/block/pallas_call | solution.py:715
  112.5 2.4 %unpack.1 = (bf16[2,64,1024]{2,1,0:T(8,128)(2,1)}, f32[2,64,1024]{2,1,0:T(8,128)}, f32[2,256]{1,0:T(2,128)}, f32[192,256]{1,0:T(8,128)}, f32[1,6144]{1,0:T(1,128...) custom-call(bf16[2,2,32,1024]{3,2,1,0:T(8,128)(2,1)} %get-tuple-elem, ...), custom_call_target="tpu_custom_call" | custom-call | tf_op jit(solution)/shard_map/unpack/pallas_call | solution.py:734

commit v4 on v3

--- a/solution.py
+++ b/solution.py
@@ -15,15 +15,28 @@
 DMA = pltpu.SemaphoreType.DMA
 
 
+def mod(a, b):
+    return a % b if isinstance(a, int) else lax.rem(a, jnp.int32(b))
+
+
+def div(a, b):
+    return a // b if isinstance(a, int) else lax.div(a, jnp.int32(b))
+
+
 def place():
     dp = lax.axis_index("dp")
     ctx = lax.axis_index("context")
     t = lax.axis_index("tensor")
-    return dp, ctx, t, (t // 2) * 2 + dp, ctx % 4, ctx // 4, t % 2
+    return dp, ctx, t, div(t, 2) * 2 + dp, mod(ctx, 4), div(ctx, 4), mod(t, 2)
+
+
+def loop(first, last, one):
+    for k in range(first, last):
+        one(k, 0)
 
 
 def device(x, y, z, core):
-    return (x % 2, z * 4 + y, (x // 2) * 2 + core)
+    return (mod(x, 2), z * 4 + y, div(x, 2) * 2 + core)
 
 
 def remote(src, dst, send, recv, target):
@@ -40,24 +53,24 @@
         def one(k, carry, target=target):
             pl.semaphore_signal(barrier, inc=1, device_id=target(k), device_id_type=MESH)
             return carry
-        lax.fori_loop(first, last, one, 0)
+        loop(first, last, one)
         count += last - first
     pl.semaphore_wait(barrier, count)
 
 
 def z_peer(k):
     dp, ctx, t, x, y, z, core = place()
-    return (dp, ((z + k) % 4) * 4 + y, t)
+    return (dp, mod(z + k, 4) * 4 + y, t)
 
 
 def y_peer(k):
     dp, ctx, t, x, y, z, core = place()
-    return (dp, z * 4 + (y + k) % 4, t)
+    return (dp, z * 4 + mod(y + k, 4), t)
 
 
 def x_peer(k):
     dp, ctx, t, x, y, z, core = place()
-    return device((x + k) % 4, y, z, core)
+    return device(mod(x + k, 4), y, z, core)
 
 
 def sibling():
@@ -67,43 +80,43 @@
 
 def ring_peer(k):
     dp, ctx, t, x, y, z, core = place()
-    r = (x * 2 + core + k) % 8
-    return device(r // 2, y, z, r % 2)
+    r = mod(x * 2 + core + k, 8)
+    return device(div(r, 2), y, z, mod(r, 2))
 
 
 def gather_start(own, slots, mine, n, peer, send, recv):
     def one(k, carry):
         remote(own, slots.at[mine], send.at[k], recv.at[mine], peer(k)).start()
         return carry
-    lax.fori_loop(1, n, one, 0)
+    loop(1, n, one)
 
 
 def gather_wait(own, slots, mine, n, peer, send, recv):
     def one(k, carry):
-        other = (mine + k) % n
+        other = mod(mine + k, n)
         copy = remote(own, slots.at[other], send.at[k], recv.at[other], peer(k))
         copy.wait_recv()
         copy.wait_send()
         return carry
-    lax.fori_loop(1, n, one, 0)
+    loop(1, n, one)
 
 
 def scatter_start(parts, slots, mine, n, peer, send, recv):
     def one(k, carry):
-        other = (mine + k) % n
+        other = mod(mine + k, n)
         remote(parts.at[other], slots.at[mine], send.at[k], recv.at[mine], peer(k)).start()
         return carry
-    lax.fori_loop(1, n, one, 0)
+    loop(1, n, one)
 
 
 def scatter_wait(parts, slots, mine, n, peer, send, recv):
     def one(k, carry):
-        other = (mine + k) % n
+        other = mod(mine + k, n)
         copy = remote(parts.at[other], slots.at[other], send.at[k], recv.at[other], peer(k))
         copy.wait_recv()
         copy.wait_send()
         return carry
-    lax.fori_loop(1, n, one, 0)
+    loop(1, n, one)
 
 
 def shape(dims, dtype):
@@ -126,6 +139,16 @@
     return lax.dot_general(
         left, right, (contract, ((), ())), precision=precision, preferred_element_type=F32
     )
+
+
+def dot_split(left, right):
+    high = left.astype(BF16)
+    rest = left - high.astype(F32)
+    middle = rest.astype(BF16)
+    low = (rest - middle.astype(F32)).astype(BF16)
+    out = dot(jnp.concatenate([high, middle, low], axis=0), right, NN)
+    n = left.shape[0]
+    return out[:n] + (out[n:2 * n] + out[2 * n:])
 
 
 NN = ((1,), (0,))
@@ -137,20 +160,37 @@
 
 
 def from_back(k):
-    y, z = lax.axis_index("context") % 4, lax.axis_index("context") // 4
-    return (y + 4 - k) % 4, (z + 4 - k) % 4
-
-
-def plane_one(full, h, send, recv, start):
-    dp, ctx, t, x, y, z, core = place()
-    mine = full.at[h, z, y]
-    for k in STEPS:
-        target = (dp, ((z + h * k) % 4) * 4 + (y + (1 - h) * k) % 4, t)
-        if start:
-            remote(mine, mine, send.at[h, k], recv.at[h, k], target).start()
-        else:
-            slot = full.at[h, (z + h * (4 - k)) % 4, (y + (1 - h) * (4 - k)) % 4]
-            remote(mine, slot, send.at[h, k], recv.at[h, k], target).wait()
+    y, z = mod(lax.axis_index("context"), 4), div(lax.axis_index("context"), 4)
+    return mod(y + 4 - k, 4), mod(z + 4 - k, 4)
+
+
+def line_target(to, h, k):
+    dp, ctx, t, x, y, z, core = place()
+    return (to, mod(z + h * k, 4) * 4 + mod(y + (1 - h) * k, 4), t)
+
+
+def cross_y(k):
+    return line_target(1 - lax.axis_index("dp"), 0, k)
+
+
+def cross_z(k):
+    return line_target(1 - lax.axis_index("dp"), 1, k)
+
+
+def plane_one(full, pack, send, recv, start):
+    dp, ctx, t, x, y, z, core = place()
+    for side, order in ((0, STEPS), (1, (2, 1, 3, 0))):
+        to = dp if side == 0 else 1 - dp
+        for k in order:
+            target = line_target(to, dp, k)
+            if start:
+                remote(pack.at[to], full.at[dp, z, y], send.at[side, k], recv.at[side, k],
+                       target).start()
+            else:
+                slot = full.at[to, mod(z + to * (4 - k), 4), mod(y + (1 - to) * (4 - k), 4)]
+                remote(pack.at[to], slot, send.at[side, k], recv.at[side, k], target).wait()
+    if start:
+        full[dp, z, y] = pack[dp]
 
 
 def plane_two(full, send, recv, start):
@@ -170,7 +210,7 @@
     dp, ctx, t, x, y, z, core = place()
     for k in STEPS:
         by, bz = from_back(k)
-        row, column = parts.at[0, (z + k) % 4], parts.at[1, :, (y + k) % 4]
+        row, column = parts.at[0, mod(z + k, 4)], parts.at[1, :, mod(y + k, 4)]
         to_row = slots.at[0, z if start else bz]
         to_column = slots.at[1, y if start else by]
         for copy in (remote(row, to_row, send.at[0, k], recv.at[0, k], z_peer(k)),
@@ -183,16 +223,17 @@
 
 def reduce_two(parts, slots, send, recv, start):
     dp, ctx, t, x, y, z, core = place()
-    for k in STEPS:
-        by, bz = from_back(k)
-        to_y = slots.at[0, y if start else by]
-        to_z = slots.at[1, z if start else bz]
-        for copy in (remote(parts.at[0, (y + k) % 4], to_y, send.at[0, k], recv.at[0, k], y_peer(k)),
-                     remote(parts.at[1, (z + k) % 4], to_z, send.at[1, k], recv.at[1, k], z_peer(k))):
+    for side, order in ((0, STEPS), (1, (2, 1, 3, 0))):
+        to = dp if side == 0 else 1 - dp
+        at = y * (1 - to) + z * to
+        mine = y * (1 - dp) + z * dp
+        for k in order:
+            slot = slots.at[dp, at] if start else slots.at[to, mod(mine + 4 - k, 4)]
+            copy = remote(parts.at[to, mod(at + k, 4)], slot, send.at[side, k], recv.at[side, k],
+                          line_target(to, to, k))
             copy.start() if start else copy.wait()
-    if start:
-        slots[0, y] = parts[0, y]
-        slots[1, z] = parts[1, z]
+        if start and side == 0:
+            slots[dp, at] = parts[dp, at]
 
 
 def add_slots(slots, out):
@@ -205,7 +246,7 @@
 
 def tokens(src, dst, send, recv, start):
     dp, ctx, t, x, y, z, core = place()
-    own = src.at[t // 2, pl.ds(pl.multiple_of(core * 32, 32), 32)]
+    own = src.at[div(t, 2), pl.ds(pl.multiple_of(core * 32, 32), 32)]
     for other in range(4):
         same = jnp.logical_and(x == y, x == other)
         copy = remote(own, dst.at[y, core], send.at[other], recv.at[y], device(other, x, z, core))
@@ -226,7 +267,7 @@
                    (1 - dp, ctx, t)).wait_recv()
 
 
-def tokens_relay(dst, send, recv, start):
+def relay(dst, send, recv, start):
     dp, ctx, t, x, y, z, core = place()
     mine = dst.at[:, core]
     if start:
@@ -244,11 +285,11 @@
         slots[x, core] = own[...]
         return
     for k in STEPS:
-        slot = slots.at[(x + 4 - k) % 4, core]
+        slot = slots.at[mod(x + 4 - k, 4), core]
         remote(own, slot, send.at[0, k], recv.at[0, k], x_peer(k)).wait()
         remote(slot, slot, send.at[1, k], recv.at[1, k], sibling()).start()
     for k in (0,) + STEPS:
-        slot = slots.at[(x + 4 - k) % 4, 1 - core]
+        slot = slots.at[mod(x + 4 - k, 4), 1 - core]
         remote(slot, slot, send.at[1, k], recv.at[1, k], sibling()).wait()
 
 
@@ -257,12 +298,12 @@
     order = (2, 1, 3, 0)
     if step == 0:
         for k in order:
-            to = (x + k) % 4
+            to = mod(x + k, 4)
             remote(parts.at[to, 1 - core], halves.at[to], send.at[0, k], recv.at[0, k],
                    sibling()).start()
     elif step == 1:
         for k in order:
-            to = (x + k) % 4
+            to = mod(x + k, 4)
             remote(parts.at[to, 1 - core], halves.at[to], send.at[0, k], recv.at[0, k],
                    sibling()).wait()
             both = parts[to, core].astype(F32) + halves[to].astype(F32)
@@ -273,19 +314,17 @@
                 remote(mid.at[to], slots.at[x], send.at[1, k], recv.at[1, k], x_peer(k)).start()
     else:
         for k in STEPS:
-            remote(mid.at[(x + k) % 4], slots.at[(x + 4 - k) % 4], send.at[1, k], recv.at[1, k],
+            remote(mid.at[mod(x + k, 4)], slots.at[mod(x + 4 - k, 4)], send.at[1, k], recv.at[1, k],
                    x_peer(k)).wait()
 
 
 def spread(src, dst, send, recv, start):
     dp, ctx, t, x, y, z, core = place()
-    for k in range(4):
-        x_hi, other = k // 2, k % 2
-        x_to = 2 * x_hi + y % 2
-        same = jnp.logical_and(jnp.logical_and(x_to == x, x == y), core == other)
-        slot = dst.at[y // 2, core]
-        recv_sem = recv.at[(y // 2) * 2 + core]
-        copy = remote(src, slot, send.at[k], recv_sem, device(x_to, x, z, other))
+    for k in range(2):
+        x_to = 2 * k + mod(y, 2)
+        same = jnp.logical_and(x_to == x, x == y)
+        slot = dst.at[div(y, 2), core]
+        copy = remote(src, slot, send.at[k], recv.at[div(y, 2)], device(x_to, x, z, core))
         if start:
             @pl.when(jnp.logical_not(same))
             def _():
@@ -293,14 +332,13 @@
 
             @pl.when(same)
             def _():
-                pltpu.make_async_copy(src, slot, recv_sem).start()
+                pltpu.make_async_copy(src, slot, recv.at[div(y, 2)]).start()
         else:
             @pl.when(jnp.logical_not(same))
             def _():
                 copy.wait_send()
 
-            remote(src, dst.at[k // 2, k % 2], send.at[k], recv.at[k],
-                   (1 - dp, ctx, t)).wait_recv()
+            remote(src, dst.at[k, core], send.at[k], recv.at[k], (1 - dp, ctx, t)).wait_recv()
 
 
 def tokens_target(k):
@@ -313,19 +351,9 @@
     return device(y, k, z, core)
 
 
-def spread_target(k):
-    dp, ctx, t, x, y, z, core = place()
-    return device(2 * (k // 2) + y % 2, x, z, k % 2)
-
-
-def spread_source(k):
-    dp, ctx, t, x, y, z, core = place()
-    return device(y, 2 * (k // 2) + dp, z, k % 2)
-
-
 def ctx_peer(k):
     dp, ctx, t, x, y, z, core = place()
-    return (dp, (ctx + k) % 16, t)
+    return (dp, mod(ctx + k, 16), t)
 
 
 INPUTS = dict(lat=0, cond=1, ada=2, ada_bias=3, qkv=4, qv=5, wo=6, ob=7, w1=8, b1=9, w2=10, b2=11, cot=12)
@@ -335,8 +363,9 @@
     cond_out=((2, 256), F32),
     ada_out=((192, 256), F32),
     ada_bias_out=((1, 6144), F32),
-    ga_out=((2, 32, 512), F32),
+    ga_out=((2, 32, 256), F32),
     gb_out=((2, 32, 1024), F32),
+    gc_out=((2, 32, 256), F32),
     bias_out=((2, 1, 1024), F32),
     wide_out=((2, 1024), F32),
 )
@@ -369,21 +398,22 @@
     n_own=((2, 1024), F32), n_slots=((8, 2, 1024), F32),
     l_own=((4, 1024), F32), l_slots=((16, 4, 1024), F32),
     dm=((8, 6144), F32), bias_own=((1, 1024), F32),
-    cond_part=((8, 256), F32), cond_slots=((16, 8, 256), F32), cond_sum=((8, 256), F32),
-    cond_other=((8, 256), F32),
-    ga=((2, 4, 4, 32, 512), BF16), ga1=((2, 4, 4, 32, 512), BF16),
-    ga2=((2, 4, 32, 512), BF16), ga3=((2, 4, 32, 512), BF16), gas=((2, 32, 512), F32),
+    cond_part=((4, 256), F32), cond_slots=((16, 4, 256), F32), cond_sum=((4, 256), F32), ada_b=((192, 256), BF16),
+    ga=((2, 4, 4, 32, 256), BF16), ga1=((2, 4, 4, 32, 256), BF16),
+    ga2=((2, 4, 32, 256), BF16), ga3=((2, 4, 32, 256), BF16),
     gb=((2, 4, 4, 32, 1024), BF16), gb1=((2, 4, 4, 32, 1024), BF16),
-    gb2=((2, 4, 32, 1024), BF16), gb3=((2, 4, 32, 1024), BF16), gbs=((2, 32, 1024), F32),
+    gb2=((2, 4, 32, 1024), BF16), gb3=((2, 4, 32, 1024), BF16),
+    gc=((2, 4, 4, 32, 256), BF16), gc1=((2, 4, 4, 32, 256), BF16),
+    gc2=((2, 4, 32, 256), BF16), gc3=((2, 4, 32, 256), BF16),
 )
 SEMS = dict(
-    s_cond=(), s_xa=(), s_xb=(), s_xg=(4,), s_xr=(), s_cg=(4,), s_cr=(),
+    s_cond=(), s_xg=(4,), s_xr=(), s_cg=(4,), s_cr=(),
     s_wa1=(2, 4), s_wa2=(2, 4), s_wb1=(2, 4), s_wb2=(2, 4),
     s_mod=(8,), s_mod2=(16,), s_k=(4,), s_v=(4,),
     s_branch=(2, 4), s_h2=(2, 4), s_dh2=(2, 4), s_feed=(2, 4), s_db=(2, 4),
-    s_block=(4,), s_dk=(4,), s_dv=(4,), s_dh=(2, 4), s_grad=(4,),
-    s_m=(8,), s_z=(4,), s_y=(4,), s_n=(8,), s_l=(16,), s_bias=(), s_c=(16,), s_cx=(),
-    s_ga1=(2, 4), s_ga2=(2, 4), s_gb1=(2, 4), s_gb2=(2, 4), s_gax=(), s_gbx=(),
+    s_block=(2,), s_dk=(4,), s_dv=(4,), s_dh=(2, 4), s_grad=(2,), s_blockr=(), s_gradr=(), s_ada=(),
+    s_m=(8,), s_z=(4,), s_y=(4,), s_n=(8,), s_l=(16,), s_bias=(), s_c=(16,),
+    s_ga1=(2, 4), s_ga2=(2, 4), s_gb1=(2, 4), s_gb2=(2, 4), s_gc1=(2, 4), s_gc2=(2, 4),
 )
 
 
@@ -403,8 +433,8 @@
     r = x * 2 + core
     partner = (1 - dp, ctx, t)
 
-    greet([(1, 8, ring_peer), (1, 16, ctx_peer)] + [(0, 4, f) for f in (
-        tokens_target, tokens_source, spread_target, spread_source)])
+    greet([(1, 8, ring_peer), (1, 16, ctx_peer), (0, 4, tokens_target), (0, 4, tokens_source),
+           (1, 4, cross_y), (1, 4, cross_z)])
 
     cond_slice = g.cond[:, pl.ds(pl.multiple_of(t * 256, 256), 256)].astype(F32)
     sigmoid = 1.0 / (1.0 + jnp.exp(-cond_slice))
@@ -413,15 +443,12 @@
     g.cond_a[...] = jnp.where(rows == dp, cond_act[0:1], jnp.where(rows == dp + 2, cond_act[1:2], 0.0))
     cond_copy = remote(g.cond_a, g.cond_b, *g.s_cond, partner)
     cond_copy.start()
-    tokens(g.lat, g.xg, *g.s_xg, True)
     for h in range(2):
         for k in range(3):
             g.packa[h, :, 128 * k:128 * k + 128] = g.qkv[k, :, 128 * h:128 * h + 128]
         g.packa[h, :, 384:] = g.wo[:, 128 * h:128 * h + 128]
-    across_a = remote(g.packa.at[1 - dp], g.wa.at[dp, z, y], *g.s_xa, partner)
-    across_a.start()
-    g.wa[dp, z, y] = g.packa[dp]
-    plane_one(g.wa, dp, *g.s_wa1, True)
+    plane_one(g.wa, g.packa, *g.s_wa1, True)
+    tokens(g.lat, g.xg, *g.s_xg, True)
     cond_copy.wait()
     g.cond8[...] = g.cond_a[...] + g.cond_b[...]
     g.part[:, :192] = dot(g.cond8[...].astype(BF16), g.ada[...], NT)[:4]
@@ -430,11 +457,6 @@
     for h in range(2):
         g.packb[h, :, :512] = g.w1[0, :, 512 * h:512 * h + 512]
         g.packb[h, :, 512:] = g.w2[:, 512 * h:512 * h + 512]
-    across_b = remote(g.packb.at[1 - dp], g.wb.at[dp, z, y], *g.s_xb, partner)
-    across_b.start()
-    g.wb[dp, z, y] = g.packb[dp]
-    remote(g.packa.at[1 - dp], g.wa.at[1 - dp, z, y], *g.s_xa, partner).wait()
-    plane_one(g.wa, 1 - dp, *g.s_wa1, True)
     gather_wait(g.part, g.parts, r, 8, ring_peer, *g.s_mod)
     for c in range(2):
         both = (g.parts[2 * c] + g.parts[2 * c + 1]) + (g.parts[2 * c + 4] + g.parts[2 * c + 5])
@@ -442,32 +464,30 @@
             g.pair[i, c:c + 1, :192] = both[i:i + 1, :192]
 
     def mod_start(k, carry):
-        remote(g.pair.at[(ctx + k) % 4], g.modg.at[ctx], g.s_mod2[0].at[k], g.s_mod2[1].at[ctx],
+        remote(g.pair.at[mod(ctx + k, 4)], g.modg.at[ctx], g.s_mod2[0].at[k], g.s_mod2[1].at[ctx],
                ctx_peer(k)).start()
         return carry
-    lax.fori_loop(1, 16, mod_start, 0)
+    loop(1, 16, mod_start)
     g.modg[ctx] = g.pair[y]
     tokens(g.lat, g.xg, *g.s_xg, False)
-    tokens_relay(g.xg, *g.s_xr, True)
-    plane_one(g.wa, dp, *g.s_wa1, False)
-    plane_one(g.wa, 1 - dp, *g.s_wa1, False)
+    relay(g.xg, *g.s_xr, True)
+    plane_one(g.wa, g.packa, *g.s_wa1, False)
     plane_two(g.wa, *g.s_wa2, True)
-    tokens_relay(g.xg, *g.s_xr, False)
+    relay(g.xg, *g.s_xr, False)
     normed, _ = normalize(g.xg[...].astype(F32).reshape(256, 1024))
     g.normed[...] = normed
-    plane_one(g.wb, dp, *g.s_wb1, True)
-    remote(g.packb.at[1 - dp], g.wb.at[1 - dp, z, y], *g.s_xb, partner).wait()
-    plane_one(g.wb, 1 - dp, *g.s_wb1, True)
-    tokens(g.cot, g.cg, *g.s_cg, True)
+    plane_one(g.wb, g.packb, *g.s_wb1, True)
+    ada_copy = remote(g.ada, g.ada_b, *g.s_ada, partner)
+    ada_copy.start()
 
     def mod_wait(k, carry):
-        other = (ctx + k) % 16
+        other = mod(ctx + k, 16)
         remote(g.pair.at[0], g.modg.at[other], g.s_mod2[0].at[k], g.s_mod2[1].at[other],
                ctx_peer(k)).wait()
         return carry
-    lax.fori_loop(1, 16, mod_wait, 0)
+    loop(1, 16, mod_wait)
     for p in range(16):
-        c, first = p // 8, (2 * p) % 16
+        c, first = div(p, 8), mod(2 * p, 16)
         both = jnp.concatenate(
             [g.modg[first, c:c + 1, :192], g.modg[first + 1, c:c + 1, :192]], axis=1)
         g.flat[:, 384 * p:384 * p + 384] = both + g.ada_bias[:, 384 * p:384 * p + 384].astype(F32)
@@ -485,10 +505,10 @@
     query = (mixed[:, :128] + qv[0:1]).astype(BF16)
     g.kg[z] = g.k_own[...]
     g.vg[z] = g.v_own[...]
-    plane_one(g.wb, dp, *g.s_wb1, False)
-    plane_one(g.wb, 1 - dp, *g.s_wb1, False)
+    tokens(g.cot, g.cg, *g.s_cg, True)
+    gather_wait(g.k_own, g.kg, z, 4, z_peer, *g.s_k)
+    plane_one(g.wb, g.packb, *g.s_wb1, False)
     plane_two(g.wb, *g.s_wb2, True)
-    gather_wait(g.k_own, g.kg, z, 4, z_peer, *g.s_k)
     for h in range(2):
         key = g.kg[:, :, 64 * h:64 * h + 64].reshape(1024, 64)
         scores = dot(query[:, 64 * h:64 * h + 64], key, NT) * SCALE
@@ -506,13 +526,10 @@
     ring_scatter(*branch_ring, 0)
     ring_scatter(*branch_ring, 1)
     tokens(g.cot, g.cg, *g.s_cg, False)
-    tokens_relay(g.cg, *g.s_cr, True)
-    tokens_relay(g.cg, *g.s_cr, False)
+    relay(g.cg, *g.s_cr, True)
+    relay(g.cg, *g.s_cr, False)
     d_feed = (g.cg[...].astype(F32).reshape(256, 1024) * gate2).astype(BF16)
     g.d_feed[...] = d_feed
-    plane_two(g.wb, *g.s_wb2, False)
-    w_second = g.wb[:, :, :, :, 512:].reshape(1024, 512)
-    g.d_act[...] = dot(d_feed, w_second, NN)
     g.z_own[...] = jnp.zeros_like(g.z_own)
     g.z_own[5:6] = jnp.sum(d_feed.astype(F32), axis=0, keepdims=True)
     ring_scatter(*branch_ring, 2)
@@ -523,6 +540,9 @@
     normed_two, inverse_two = normalize(middle)
     g.h2_own[...] = (normed_two * (1.0 + scale2) + shift2).astype(BF16)
     ring_gather(g.h2_own, g.h2, *g.s_h2, True)
+    plane_two(g.wb, *g.s_wb2, False)
+    w_second = g.wb[:, :, :, :, 512:].reshape(1024, 512)
+    g.d_act[...] = dot(d_feed, w_second, NN)
     ring_gather(g.h2_own, g.h2, *g.s_h2, False)
 
     hidden_two = g.h2[...].reshape(256, 1024)
@@ -539,10 +559,13 @@
     ring_scatter(*dh2_ring, 0)
     activated = (0.5 * before * (1.0 + tanh)).astype(BF16)
     ring_scatter(*dh2_ring, 1)
-    g.feed_part[...] = dot(activated, w_second, NT).astype(BF16).reshape(4, 2, 32, 1024)
+    feed_part = dot(activated, w_second, NT)
+    g.feed_part[...] = feed_part.astype(BF16).reshape(4, 2, 32, 1024)
     g.gb[:, :, :, :, :512] = dot(hidden_two, d_before, TN).astype(BF16).reshape(2, 4, 4, 32, 512)
     g.gb[:, :, :, :, 512:] = dot(d_feed, activated, TN).astype(BF16).reshape(2, 4, 4, 32, 512)
     reduce_one(g.gb, g.gb1, *g.s_gb1, True)
+    g.m_own[3:4] = jnp.sum(
+        g.cg[...].astype(F32).reshape(256, 1024) * feed_part, axis=0, keepdims=True)
     g.z_own[6:7, :512] = jnp.sum(d_before.astype(F32), axis=0, keepdims=True)
     ring_scatter(*dh2_ring, 2)
 
@@ -557,6 +580,9 @@
     g.m_own[0:1] = jnp.sum(d_middle * branch, axis=0, keepdims=True)
     g.m_own[1:2] = jnp.sum(d_hidden, axis=0, keepdims=True)
     g.m_own[2:3] = jnp.sum(d_hidden * normed_two, axis=0, keepdims=True)
+    g.m_own[3:4] += jnp.sum(cot_own, axis=0, keepdims=True) * g.b2[...].astype(F32)
+    gather_start(g.m_own, g.m_slots, r, 8, ring_peer, *g.s_m)
+    g.m_slots[r] = g.m_own[...]
     ring_gather(g.db_own, g.db, *g.s_db, False)
     ring_scatter(*feed_ring, 1)
 
@@ -580,21 +606,24 @@
     scatter_start(g.dk_part, g.dk_slots, z, 4, z_peer, *g.s_dk)
     g.dk_slots[z] = g.dk_part[z]
     d_query = jnp.concatenate(d_query, axis=1).astype(BF16)
+    g.z_own[4:5] = jnp.sum(d_branch.astype(F32), axis=0, keepdims=True)
+    g.z_own[6:7, 512:640] = jnp.sum(d_query.astype(F32), axis=0, keepdims=True)
+    gather_wait(g.m_own, g.m_slots, r, 8, ring_peer, *g.s_m)
+    g.z_own[0:4] = jnp.sum(g.m_slots[...], axis=0)
+    gather_start(g.z_own, g.z_slots, z, 4, z_peer, *g.s_z)
+    g.z_slots[z] = g.z_own[...]
     ring_scatter(*feed_ring, 2)
     feed = jnp.sum(g.feed_slots[...].astype(F32), axis=0) + g.b2[...].astype(F32)
     g.block_own[...] = (middle + gate2 * feed).astype(BF16)
     spread(g.block_own, g.block_out, *g.s_block, True)
-    g.m_own[3:4] = jnp.sum(cot_own * feed, axis=0, keepdims=True)
-    gather_start(g.m_own, g.m_slots, r, 8, ring_peer, *g.s_m)
-    g.m_slots[r] = g.m_own[...]
-    g.ga[:, :, :, :, 384:] = dot(d_branch, attended, TN).astype(BF16).reshape(2, 4, 4, 32, 128)
-    g.z_own[4:5] = jnp.sum(d_branch.astype(F32), axis=0, keepdims=True)
-    g.z_own[6:7, 512:640] = jnp.sum(d_query.astype(F32), axis=0, keepdims=True)
+    g.gc[:, :, :, :, :128] = dot(g.hidden[...], d_query, TN).astype(BF16).reshape(2, 4, 4, 32, 128)
+    g.gc[:, :, :, :, 128:] = dot(d_branch, attended, TN).astype(BF16).reshape(2, 4, 4, 32, 128)
+    reduce_one(g.gc, g.gc1, *g.s_gc1, True)
     reduce_one(g.gb, g.gb1, *g.s_gb1, False)
     add_slots(g.gb1, g.gb2)
+    reduce_two(g.gb2, g.gb3, *g.s_gb2, True)
     scatter_wait(g.dv_part, g.dv_slots, z, 4, z_peer, *g.s_dv)
     scatter_wait(g.dk_part, g.dk_slots, z, 4, z_peer, *g.s_dk)
-    reduce_two(g.gb2, g.gb3, *g.s_gb2, True)
 
     d_keys = jnp.sum(g.dk_slots[...].astype(F32), axis=0).astype(BF16)
     d_values = jnp.sum(g.dv_slots[...].astype(F32), axis=0).astype(BF16)
@@ -603,17 +632,21 @@
     g.dh_part[...] = d_part.astype(BF16).reshape(4, 2, 32, 1024)
     dh_ring = (g.dh_part, g.dh_half, g.dh_mid, g.dh_slots, *g.s_dh)
     ring_scatter(*dh_ring, 0)
+    d_kv = jnp.concatenate([d_keys, d_values], axis=1)
+    g.ga[...] = dot(g.hidden[...], d_kv, TN).astype(BF16).reshape(2, 4, 4, 32, 256)
+    reduce_one(g.ga, g.ga1, *g.s_ga1, True)
     g.n_own[0:1] = jnp.sum(d_part, axis=0, keepdims=True)
     g.n_own[1:2] = jnp.sum(d_part * g.normed[...], axis=0, keepdims=True)
-    ring_scatter(*dh_ring, 1)
     gather_start(g.n_own, g.n_slots, r, 8, ring_peer, *g.s_n)
     g.n_slots[r] = g.n_own[...]
-    g.ga[:, :, :, :, :384] = dot(g.hidden[...], d_qkv, TN).astype(BF16).reshape(2, 4, 4, 32, 384)
-    reduce_one(g.ga, g.ga1, *g.s_ga1, True)
-    gather_wait(g.m_own, g.m_slots, r, 8, ring_peer, *g.s_m)
-    g.z_own[0:4] = jnp.sum(g.m_slots[...], axis=0)
-    gather_start(g.z_own, g.z_slots, z, 4, z_peer, *g.s_z)
-    g.z_slots[z] = g.z_own[...]
+    ring_scatter(*dh_ring, 1)
+    gather_wait(g.z_own, g.z_slots, z, 4, z_peer, *g.s_z)
+    g.y_own[...] = jnp.sum(g.z_slots[...], axis=0)
+    gather_start(g.y_own, g.y_slots, y, 4, y_peer, *g.s_y)
+    g.y_slots[y] = g.y_own[...]
+    reduce_one(g.gc, g.gc1, *g.s_gc1, False)
+    add_slots(g.gc1, g.gc2)
+    reduce_two(g.gc2, g.gc3, *g.s_gc2, True)
     gather_wait(g.n_own, g.n_slots, r, 8, ring_peer, *g.s_n)
     g.l_own[0:2] = jnp.sum(g.n_slots[...], axis=0)
     g.l_own[2:4] = jnp.zeros((2, 1024), F32)
@@ -627,21 +660,32 @@
     grad = g.d_middle[...] + norm_back(d_hidden * (1.0 + scale1), x_normed, x_inverse)
     g.grad_own[...] = grad.astype(BF16)
     spread(g.grad_own, g.grad_out, *g.s_grad, True)
-    gather_wait(g.z_own, g.z_slots, z, 4, z_peer, *g.s_z)
-    g.y_own[...] = jnp.sum(g.z_slots[...], axis=0)
-    gather_start(g.y_own, g.y_slots, y, 4, y_peer, *g.s_y)
-    g.y_slots[y] = g.y_own[...]
-    reduce_two(g.gb2, g.gb3, *g.s_gb2, False)
-    add_slots(g.gb3, g.gbs)
-    remote(g.gbs.at[1 - dp], g.gb_out.at[dp], *g.s_gbx, partner).start()
-    g.gb_out[dp] = g.gbs[dp]
     reduce_one(g.ga, g.ga1, *g.s_ga1, False)
     add_slots(g.ga1, g.ga2)
     reduce_two(g.ga2, g.ga3, *g.s_ga2, True)
+    g.dm[...] = jnp.zeros_like(g.dm)
+    gather_wait(g.y_own, g.y_slots, y, 4, y_peer, *g.s_y)
+    for k in range(2, 6):
+        for i in range(4):
+            g.dm[i:i + 1, k * 1024:(k + 1) * 1024] = g.y_slots[i, k - 2:k - 1]
     gather_wait(g.l_own, g.l_slots, ctx, 16, ctx_peer, *g.s_l)
-    gather_wait(g.y_own, g.y_slots, y, 4, y_peer, *g.s_y)
 
     late = jnp.sum(g.l_slots[...].reshape(4, 4, 4, 1024), axis=0)
+    for k in range(2):
+        for i in range(4):
+            g.dm[i:i + 1, k * 1024:(k + 1) * 1024] = late[i, k:k + 1]
+
+    def columns(chunk):
+        wide = g.dm[:, pl.ds(pl.multiple_of(div(3 * chunk, 2) * 128, 128), 256)]
+        return jnp.where(mod(chunk, 2) == 1, pltpu.roll(wide, 192, 1), wide)[:, :192]
+
+    own_columns = columns(dp * 16 + ctx)
+    ada_copy.wait()
+    highest = lax.Precision.HIGHEST
+    g.cond_part[...] = (
+        dot_split(own_columns, g.ada[...]) + dot_split(columns((1 - dp) * 16 + ctx), g.ada_b[...]))[:4]
+    gather_start(g.cond_part, g.cond_slots, ctx, 16, ctx_peer, *g.s_c)
+    g.cond_slots[ctx] = g.cond_part[...]
     early = jnp.sum(g.y_slots[...], axis=0)
     g.wide_out[...] = early[4:6]
     g.bias_own[:, :640] = early[6:7, :640]
@@ -649,40 +693,29 @@
     g.bias_own[:, 768:] = jnp.zeros((1, 256), F32)
     remote(g.bias_own, g.bias_out.at[dp], *g.s_bias, partner).start()
     g.bias_out[dp] = g.bias_own[...]
-    g.dm[...] = jnp.zeros_like(g.dm)
-    for k in range(6):
-        for i in range(4):
-            row = late[i, k:k + 1] if k < 2 else g.y_slots[i, k - 2:k - 1]
-            g.dm[i:i + 1, k * 1024:(k + 1) * 1024] = row
     g.ada_bias_out[...] = jnp.sum(g.dm[...], axis=0, keepdims=True)
-    chunk = dp * 16 + ctx
-    columns = g.dm[:, pl.ds(pl.multiple_of(((3 * chunk) // 2) * 128, 128), 256)]
-    columns = jnp.where(chunk % 2 == 1, pltpu.roll(columns, 192, 1), columns)[:, :192]
-    g.cond_part[...] = dot(columns, g.ada[...].astype(F32), NN, lax.Precision.HIGHEST)
-    gather_start(g.cond_part, g.cond_slots, ctx, 16, ctx_peer, *g.s_c)
-    g.cond_slots[ctx] = g.cond_part[...]
-    g.ada_out[...] = dot(columns, g.cond8[...], TN, lax.Precision.HIGHEST)
+    spread(g.block_own, g.block_out, *g.s_block, False)
+    relay(g.block_out, *g.s_blockr, True)
+    reduce_two(g.gb2, g.gb3, *g.s_gb2, False)
+    add_slots(g.gb3, g.gb_out)
+    reduce_two(g.gc2, g.gc3, *g.s_gc2, False)
+    add_slots(g.gc3, g.gc_out)
+    spread(g.grad_own, g.grad_out, *g.s_grad, False)
+    relay(g.grad_out, *g.s_gradr, True)
+    g.ada_out[...] = dot(own_columns, g.cond8[...], TN, highest)
+    reduce_two(g.ga2, g.ga3, *g.s_ga2, False)
+    add_slots(g.ga3, g.ga_out)
     gather_wait(g.cond_part, g.cond_slots, ctx, 16, ctx_peer, *g.s_c)
     g.cond_sum[...] = jnp.sum(g.cond_slots[...], axis=0)
-    cond_copy = remote(g.cond_sum, g.cond_other, *g.s_cx, partner)
-    cond_copy.start()
-    reduce_two(g.ga2, g.ga3, *g.s_ga2, False)
-    add_slots(g.ga3, g.gas)
-    remote(g.gas.at[1 - dp], g.ga_out.at[dp], *g.s_gax, partner).start()
-    g.ga_out[dp] = g.gas[dp]
-    cond_copy.wait()
-    g.cond_part[...] = g.cond_sum[...] + g.cond_other[...]
     slope = sigmoid * (1.0 + cond_slice * (1.0 - sigmoid))
     for i in range(2):
-        g.cond_out[i:i + 1] = g.cond_part[pl.ds(2 * i + dp, 1)] * slope[i:i + 1]
+        g.cond_out[i:i + 1] = g.cond_sum[pl.ds(2 * i + dp, 1)] * slope[i:i + 1]
     remote(g.bias_own, g.bias_out.at[1 - dp], *g.s_bias, partner).wait()
-    remote(g.gbs.at[1 - dp], g.gb_out.at[1 - dp], *g.s_gbx, partner).wait()
-    remote(g.gas.at[1 - dp], g.ga_out.at[1 - dp], *g.s_gax, partner).wait()
-    spread(g.block_own, g.block_out, *g.s_block, False)
-    spread(g.grad_own, g.grad_out, *g.s_grad, False)
-
-
-def unpack_kernel(block, grad, cond, ada, ada_bias, ga, gb, bias, wide,
+    relay(g.block_out, *g.s_blockr, False)
+    relay(g.grad_out, *g.s_gradr, False)
+
+
+def unpack_kernel(block, grad, cond, ada, ada_bias, ga, gb, gc, bias, wide,
                   block_out, grad_out, cond_out, ada_out, ada_bias_out, qkv_out, qv_out,
                   wo_out, ob_out, w1_out, b1_out, w2_out, b2_out):
     block_out[...] = block[...].reshape(2, 64, 1024)
@@ -692,10 +725,11 @@
     ada_bias_out[...] = ada_bias[...]
     for h in range(2):
         for k in range(3):
-            qkv_out[k, :, 128 * h:128 * h + 128] = ga[h, :, 128 * k:128 * k + 128]
+            part = gc[h, :, :128] if k == 0 else ga[h, :, 128 * k - 128:128 * k]
+            qkv_out[k, :, 128 * h:128 * h + 128] = part
         for k in range(2):
             qv_out[0, k:k + 1, 128 * h:128 * h + 128] = bias[h, :, 512 + 128 * k:640 + 128 * k]
-        wo_out[:, 128 * h:128 * h + 128] = ga[h, :, 384:]
+        wo_out[:, 128 * h:128 * h + 128] = gc[h, :, 128:]
         w1_out[0, :, 512 * h:512 * h + 512] = gb[h, :, :512]
         w2_out[:, 512 * h:512 * h + 512] = gb[h, :, 512:]
         b1_out[:, 512 * h:512 * h + 512] = bias[h, :, :512]

time: 115 us -> 112 us (0.974)
  Pallas kernels: 114 us -> 111 us
    pallas_call x1, Pallas kernels: 112 us -> 108 us  [on_device(): pl.pallas_call(block_kernel, out_shape=[shape(*one) for one in OUTPUTS.va...]
where the time goes in v4:
time: 112 us; the launch traced here: 111 us
  Pallas kernels  111 us (99%)
    pallas_call x1, Pallas kernels, on_device(): pl.pallas_call(block_kernel, out_shape=[shape(*one) for one in OUTPUTS.va...  108 us
    pallas_call x1, Pallas kernels, on_device(): pl.pallas_call(unpack_kernel, out_shape=final, in_specs=[VMEM] * len(outs...  2.43 us

profile of v4, /device:TPU:0, one launch (start us, length us, event | category | flops | bytes accessed | tf_op | source)
XLA Modules:
  0.0 111.5 jit_solution(3023346513798506218)
XLA Ops:
  0.6 108.4 %block.1 = (bf16[2,2,32,1024]{3,2,1,0:T(8,128)(2,1)}, bf16[2,2,32,1024]{3,2,1,0:T(8,128)(2,1)}, f32[2,256]{1,0:T(2,128)}, f32[192,256]{1,0:T(8,128)}, f32[1,6144...) custom-call(bf16[2,64,1024]{2,1,0:T(8,128)(2,1)} %refs_0_.1, ...), custom_call_target="tpu_custom_call" | custom-call | tf_op jit(solution)/shard_map/block/pallas_call | solution.py:749
  109.0 2.4 %unpack.1 = (bf16[2,64,1024]{2,1,0:T(8,128)(2,1)}, f32[2,64,1024]{2,1,0:T(8,128)}, f32[2,256]{1,0:T(2,128)}, f32[192,256]{1,0:T(8,128)}, f32[1,6144]{1,0:T(1,128...) custom-call(bf16[2,2,32,1024]{3,2,1,0:T(8,128)(2,1)} %get-tuple-elem, ...), custom_call_target="tpu_custom_call" | custom-call | tf_op jit(solution)/shard_map/unpack/pallas_call | solution.py:768

commit v5 on v4

--- a/solution.py
+++ b/solution.py
@@ -363,9 +363,9 @@
     cond_out=((2, 256), F32),
     ada_out=((192, 256), F32),
     ada_bias_out=((1, 6144), F32),
-    ga_out=((2, 32, 256), F32),
+    ga_out=((2, 32, 384), F32),
     gb_out=((2, 32, 1024), F32),
-    gc_out=((2, 32, 256), F32),
+    gc_out=((2, 32, 128), F32),
     bias_out=((2, 1, 1024), F32),
     wide_out=((2, 1024), F32),
 )
@@ -399,12 +399,12 @@
     l_own=((4, 1024), F32), l_slots=((16, 4, 1024), F32),
     dm=((8, 6144), F32), bias_own=((1, 1024), F32),
     cond_part=((4, 256), F32), cond_slots=((16, 4, 256), F32), cond_sum=((4, 256), F32), ada_b=((192, 256), BF16),
-    ga=((2, 4, 4, 32, 256), BF16), ga1=((2, 4, 4, 32, 256), BF16),
-    ga2=((2, 4, 32, 256), BF16), ga3=((2, 4, 32, 256), BF16),
+    ga=((2, 4, 4, 32, 384), BF16), ga1=((2, 4, 4, 32, 384), BF16),
+    ga2=((2, 4, 32, 384), BF16), ga3=((2, 4, 32, 384), BF16),
     gb=((2, 4, 4, 32, 1024), BF16), gb1=((2, 4, 4, 32, 1024), BF16),
     gb2=((2, 4, 32, 1024), BF16), gb3=((2, 4, 32, 1024), BF16),
-    gc=((2, 4, 4, 32, 256), BF16), gc1=((2, 4, 4, 32, 256), BF16),
-    gc2=((2, 4, 32, 256), BF16), gc3=((2, 4, 32, 256), BF16),
+    gc=((2, 4, 4, 32, 128), BF16), gc1=((2, 4, 4, 32, 128), BF16),
+    gc2=((2, 4, 32, 128), BF16), gc3=((2, 4, 32, 128), BF16),
 )
 SEMS = dict(
     s_cond=(), s_xg=(4,), s_xr=(), s_cg=(4,), s_cr=(),
@@ -587,6 +587,8 @@
     ring_scatter(*feed_ring, 1)
 
     d_branch = g.db[...].reshape(256, 1024)
+    g.gc[...] = dot(d_branch, attended, TN).astype(BF16).reshape(2, 4, 4, 32, 128)
+    reduce_one(g.gc, g.gc1, *g.s_gc1, True)
     d_attended = dot(d_branch, w_out, NN).astype(BF16)
     d_one = [d_attended[:, 64 * h:64 * h + 64] for h in range(2)]
     d_value = [dot(g.prob[h].astype(BF16), d_one[h], TN) for h in range(2)]
@@ -616,9 +618,6 @@
     feed = jnp.sum(g.feed_slots[...].astype(F32), axis=0) + g.b2[...].astype(F32)
     g.block_own[...] = (middle + gate2 * feed).astype(BF16)
     spread(g.block_own, g.block_out, *g.s_block, True)
-    g.gc[:, :, :, :, :128] = dot(g.hidden[...], d_query, TN).astype(BF16).reshape(2, 4, 4, 32, 128)
-    g.gc[:, :, :, :, 128:] = dot(d_branch, attended, TN).astype(BF16).reshape(2, 4, 4, 32, 128)
-    reduce_one(g.gc, g.gc1, *g.s_gc1, True)
     reduce_one(g.gb, g.gb1, *g.s_gb1, False)
     add_slots(g.gb1, g.gb2)
     reduce_two(g.gb2, g.gb3, *g.s_gb2, True)
@@ -632,8 +631,7 @@
     g.dh_part[...] = d_part.astype(BF16).reshape(4, 2, 32, 1024)
     dh_ring = (g.dh_part, g.dh_half, g.dh_mid, g.dh_slots, *g.s_dh)
     ring_scatter(*dh_ring, 0)
-    d_kv = jnp.concatenate([d_keys, d_values], axis=1)
-    g.ga[...] = dot(g.hidden[...], d_kv, TN).astype(BF16).reshape(2, 4, 4, 32, 256)
+    g.ga[...] = dot(g.hidden[...], d_qkv, TN).astype(BF16).reshape(2, 4, 4, 32, 384)
     reduce_one(g.ga, g.ga1, *g.s_ga1, True)
     g.n_own[0:1] = jnp.sum(d_part, axis=0, keepdims=True)
     g.n_own[1:2] = jnp.sum(d_part * g.normed[...], axis=0, keepdims=True)
@@ -725,11 +723,10 @@
     ada_bias_out[...] = ada_bias[...]
     for h in range(2):
         for k in range(3):
-            part = gc[h, :, :128] if k == 0 else ga[h, :, 128 * k - 128:128 * k]
-            qkv_out[k, :, 128 * h:128 * h + 128] = part
+            qkv_out[k, :, 128 * h:128 * h + 128] = ga[h, :, 128 * k:128 * k + 128]
         for k in range(2):
             qv_out[0, k:k + 1, 128 * h:128 * h + 128] = bias[h, :, 512 + 128 * k:640 + 128 * k]
-        wo_out[:, 128 * h:128 * h + 128] = gc[h, :, 128:]
+        wo_out[:, 128 * h:128 * h + 128] = gc[h]
         w1_out[0, :, 512 * h:512 * h + 512] = gb[h, :, :512]
         w2_out[:, 512 * h:512 * h + 512] = gb[h, :, 512:]
         b1_out[:, 512 * h:512 * h + 512] = bias[h, :, :512]

time: 112 us -> 110 us (0.982)
  Pallas kernels: 111 us -> 109 us
    pallas_call x1, Pallas kernels: 108 us -> 107 us  [on_device(): pl.pallas_call(block_kernel, out_shape=[shape(*one) for one in OUTPUTS.va...]
where the time goes in v5:
time: 110 us
  Pallas kernels  109 us (99%)
    pallas_call x1, Pallas kernels, on_device(): pl.pallas_call(block_kernel, out_shape=[shape(*one) for one in OUTPUTS.va...  107 us
    pallas_call x1, Pallas kernels, on_device(): pl.pallas_call(unpack_kernel, out_shape=final, in_specs=[VMEM] * len(outs...  2.42 us

profile of v5, /device:TPU:0, one launch (start us, length us, event | category | flops | bytes accessed | tf_op | source)
XLA Modules:
  0.0 109.6 jit_solution(16919408102262876605)
XLA Ops:
  0.6 106.5 %block.1 = (bf16[2,2,32,1024]{3,2,1,0:T(8,128)(2,1)}, bf16[2,2,32,1024]{3,2,1,0:T(8,128)(2,1)}, f32[2,256]{1,0:T(2,128)}, f32[192,256]{1,0:T(8,128)}, f32[1,6144...) custom-call(bf16[2,64,1024]{2,1,0:T(8,128)(2,1)} %refs_0_.1, ...), custom_call_target="tpu_custom_call" | custom-call | tf_op jit(solution)/shard_map/block/pallas_call | solution.py:746
  107.2 2.4 %unpack.1 = (bf16[2,64,1024]{2,1,0:T(8,128)(2,1)}, f32[2,64,1024]{2,1,0:T(8,128)}, f32[2,256]{1,0:T(2,128)}, f32[192,256]{1,0:T(8,128)}, f32[1,6144]{1,0:T(1,128...) custom-call(bf16[2,2,32,1024]{3,2,1,0:T(8,128)(2,1)} %get-tuple-elem, ...), custom_call_target="tpu_custom_call" | custom-call | tf_op jit(solution)/shard_map/unpack/pallas_call | solution.py:765

commit v6 on v5

--- a/solution.py
+++ b/solution.py
@@ -618,9 +618,6 @@
     feed = jnp.sum(g.feed_slots[...].astype(F32), axis=0) + g.b2[...].astype(F32)
     g.block_own[...] = (middle + gate2 * feed).astype(BF16)
     spread(g.block_own, g.block_out, *g.s_block, True)
-    reduce_one(g.gb, g.gb1, *g.s_gb1, False)
-    add_slots(g.gb1, g.gb2)
-    reduce_two(g.gb2, g.gb3, *g.s_gb2, True)
     scatter_wait(g.dv_part, g.dv_slots, z, 4, z_peer, *g.s_dv)
     scatter_wait(g.dk_part, g.dk_slots, z, 4, z_peer, *g.s_dk)
 
@@ -642,6 +639,9 @@
     g.y_own[...] = jnp.sum(g.z_slots[...], axis=0)
     gather_start(g.y_own, g.y_slots, y, 4, y_peer, *g.s_y)
     g.y_slots[y] = g.y_own[...]
+    reduce_one(g.gb, g.gb1, *g.s_gb1, False)
+    add_slots(g.gb1, g.gb2)
+    reduce_two(g.gb2, g.gb3, *g.s_gb2, True)
     reduce_one(g.gc, g.gc1, *g.s_gc1, False)
     add_slots(g.gc1, g.gc2)
     reduce_two(g.gc2, g.gc3, *g.s_gc2, True)

time: 110 us -> 114 us (1.036)
  Pallas kernels: 109 us -> 113 us
    pallas_call x1, Pallas kernels: 107 us -> 111 us  [on_device(): pl.pallas_call(block_kernel, out_shape=[shape(*one) for one in OUTPUTS.va...]
where the time goes in v6:
time: 114 us
  Pallas kernels  113 us (99%)
    pallas_call x1, Pallas kernels, on_device(): pl.pallas_call(block_kernel, out_shape=[shape(*one) for one in OUTPUTS.va...  111 us
    pallas_call x1, Pallas kernels, on_device(): pl.pallas_call(unpack_kernel, out_shape=final, in_specs=[VMEM] * len(outs...  2.42 us

profile of v6, /device:TPU:0, one launch (start us, length us, event | category | flops | bytes accessed | tf_op | source)
XLA Modules:
  0.0 113.7 jit_solution(4269738183586871460)
XLA Ops:
  0.6 110.7 %block.1 = (bf16[2,2,32,1024]{3,2,1,0:T(8,128)(2,1)}, bf16[2,2,32,1024]{3,2,1,0:T(8,128)(2,1)}, f32[2,256]{1,0:T(2,128)}, f32[192,256]{1,0:T(8,128)}, f32[1,6144...) custom-call(bf16[2,64,1024]{2,1,0:T(8,128)(2,1)} %refs_0_.1, ...), custom_call_target="tpu_custom_call" | custom-call | tf_op jit(solution)/shard_map/block/pallas_call | solution.py:746
  111.3 2.4 %unpack.1 = (bf16[2,64,1024]{2,1,0:T(8,128)(2,1)}, f32[2,64,1024]{2,1,0:T(8,128)}, f32[2,256]{1,0:T(2,128)}, f32[192,256]{1,0:T(8,128)}, f32[1,6144]{1,0:T(1,128...) custom-call(bf16[2,2,32,1024]{3,2,1,0:T(8,128)(2,1)} %get-tuple-elem, ...), custom_call_target="tpu_custom_call" | custom-call | tf_op jit(solution)/shard_map/unpack/pallas_call | solution.py:765
